TPU v7x, 32 devices: a whole 2x2x4 slice. The times are simulated.
32 devices in a mesh: groups: 2 (over y), wide: 4 (over z), narrow: 4 (over x, core).
Axes of the slice: x: 2, y: 2, z: 4, core: 2. Of those that a mesh axis runs over, the one named last changes fastest.
Arguments:
- tokens: bfloat16 [2, 128, 8192], P(None, ('groups', 'wide'), 'narrow'), parts along dimension 1, may hold values from -30 to 30
- assign: int32 [2, 128], P(None, 'groups'), parts along dimension 1, may hold values from 0 to 63, each once within a row
- state: bfloat16 [128, 2, 3, 8192], P(('groups', 'narrow'), None, None, 'wide'), parts along dimension 0, may hold values from -6 to 6
- norm_gain: float32 [8192], P('narrow'), may hold values from 0.1 to 1.9
- in_weight: bfloat16 [8192, 3, 8192], P('narrow', None, 'wide'), may hold values from -0.0625 to 0.0625
- conv_weight: float32 [3, 3, 8192], P(None, None, 'wide'), may hold values from -3 to 3
- out_weight: bfloat16 [8192, 8192], P('wide', 'narrow'), may hold values from -0.0625 to 0.0625
Outputs:
- mixer_out: bfloat16 [2, 128, 8192], P(None, ('groups', 'wide'), 'narrow'), parts along dimension 1
- new_state: bfloat16 [128, 2, 3, 8192], P(('groups', 'narrow'), None, None, 'wide'), parts along dimension 0
There are 2 independent parts, one for each index of `groups`. A program takes and returns all parts, laid end to end along the dimension named above; an argument that names none is the same for every part. Nothing has to cross between parts.
Inputs may be any that keep to these rules, and one draw needn't show every extreme that they name: `assign`: each step's row is a permutation of the 64 candidates of the group.
All inputs are finite; a program needn't handle non-finite values.
Results may differ from a plain program's by a relative error of at most 0.019.
Values may be sent and summed in bfloat16 or wider, within the bound.
No kernel may reach another device: no remote copies, remote signals or barrier semaphores. Data moves between devices by JAX's collectives and lax.ppermute only.
A program may use at most 128 MiB of HBM per device.

v0:
```python
import jax
import jax.numpy as jnp
from jax import lax
from jax.sharding import PartitionSpec as P

D = 8192


def shards(tokens, assign, state, norm_gain, in_weight, conv_weight, out_weight):
    narrow_count = lax.axis_size("narrow")
    chans = in_weight.shape[2]
    flat_in = in_weight.reshape(in_weight.shape[0], 3 * chans)
    results = []
    memory = state
    for moment in range(tokens.shape[0]):
        current = tokens[moment].astype(jnp.float32)
        squares = lax.psum(jnp.sum(current * current, axis=-1), "narrow")
        normed = (current * lax.rsqrt(squares[:, None] / D + 1e-05) * norm_gain).astype(
            jnp.bfloat16
        )
        gathered = lax.all_gather(normed, "wide", axis=0, tiled=True)
        total_rows = gathered.shape[0]
        share = total_rows // narrow_count
        summed = lax.psum_scatter(
            jnp.dot(gathered, flat_in, preferred_element_type=jnp.float32).astype(jnp.bfloat16),
            "narrow",
            scatter_dimension=0,
            tiled=True,
        )
        fresh = summed.reshape(share, 3, chans)
        wanted = lax.dynamic_slice_in_dim(
            assign[moment], lax.axis_index("narrow") * share, share, 0
        )
        piece = lax.all_gather(memory, "narrow", axis=0, tiled=True)
        inside = (wanted >= 0) & (wanted < piece.shape[0])
        taken = jnp.take(piece, jnp.clip(wanted, 0, piece.shape[0] - 1), axis=0)
        memory = jnp.where(inside[:, None, None, None], taken, jnp.zeros_like(memory))
        mixed = (
            conv_weight[0] * memory[:, 0] + conv_weight[1] * memory[:, 1] + conv_weight[2] * fresh
        )
        memory = jnp.stack([memory[:, 1], fresh], axis=1)
        gated = (mixed[:, 0] * mixed[:, 1] * mixed[:, 2]).astype(jnp.bfloat16)
        partial_out = jnp.dot(
            lax.all_gather(gated, "narrow", axis=0, tiled=True),
            out_weight,
            preferred_element_type=jnp.float32,
        )
        results.append(
            lax.psum_scatter(
                partial_out.astype(jnp.bfloat16), "wide", scatter_dimension=0, tiled=True
            )
        )
    return (jnp.stack(results), memory)


def solution(mesh):
    in_specs = (
        P(None, ("groups", "wide"), "narrow"),
        P(None, "groups"),
        P(("groups", "narrow"), None, None, "wide"),
        P("narrow"),
        P("narrow", None, "wide"),
        P(None, None, "wide"),
        P("wide", "narrow"),
    )
    out_specs = (P(None, ("groups", "wide"), "narrow"), P(("groups", "narrow"), None, None, "wide"))
    return jax.shard_map(shards, mesh=mesh, in_specs=in_specs, out_specs=out_specs, check_vma=False)
```

profile of v0, /device:TPU:0, one launch (start us, length us, event | category | flops | bytes accessed | tf_op | source)
XLA Modules:
  0.0 234.8 jit_solution(16398444274057969032)
XLA Ops:
  7.2 0.0 reduce-scatter.5.cloned.1.call-start
  7.2 1.0 fusion.8
  8.2 8.3 %all-reduce = (f32[16]{0:T(128)S(1)}, f32[16]{0:T(128)S(1)}) all-reduce(f32[16]{0:T(128)S(1)} %get-tuple-element.8, f32[16]{0:T(128)S(1)} %get-tuple-element.7), channel_id=1, replica_groups=mesh['groups'=2,'wide'=4,'narrow'=4] {'narrow'}, use_global_device_ids=true, to_apply=%region_5.7 | all-reduce | flops 32 | bytes 256 | tf_op jit(solution)/shard_map/psum | solution.py:17
  16.6 1.0 fusion.10
  17.6 14.1 %all_gather.19 = bf16[64,2048]{1,0:T(8,128)(2,1)S(1)} all-gather(bf16[16,2048]{1,0:T(8,128)(2,1)S(1)} %get-tuple-element.15), channel_id=1, replica_groups=mesh['groups'=2,'wide'=4,'narrow'=4] {'wide'}, dimensions={0}, use_global_device_ids=true | all-gather | bytes 327680 | tf_op jit(solution)/shard_map/all_gather | solution.py:21
  31.7 33.3 %copy.63 = bf16[2048,3,2048]{0,2,1:T(8,128)(2,1)} copy(bf16[2048,3,2048]{2,0,1:T(8,128)(2,1)} %param.13) | data formatting | bytes 50331648 | tf_op args[4]
  65.0 13.4 %convolution_convert_fusion.1 = bf16[64,6144]{1,0:T(8,128)(2,1)} fusion(bf16[64,2048]{1,0:T(8,128)(2,1)S(1)} %all_gather.19, bf16[2048,6144]{0,1:T(8,128)(2,1)} %bitcast.65), kind=kOutput, calls=%fused_computation.3 | convolution fusion | flops 1611005952 | bytes 26214400 | tf_op jit(solution)/shard_map/dot_general | solution.py:25
  78.4 0.0 reduce-scatter.5.cloned.1.call-update
  78.4 0.0 all-gather.5.cloned.1.call-start
  78.5 0.7 all-gather.5.cloned.1.call-update
  79.2 0.0 reduce-scatter.9.cloned.1.call-start
  79.2 14.2 %all_gather.22 = bf16[64,2048]{1,0:T(8,128)(2,1)S(1)} all-gather(bf16[16,2048]{1,0:T(8,128)(2,1)S(1)} %get-tuple-element.16), channel_id=1, replica_groups=mesh['groups'=2,'wide'=4,'narrow'=4] {'wide'}, dimensions={0}, use_global_device_ids=true | all-gather | bytes 327680 | tf_op jit(solution)/shard_map/all_gather | solution.py:21
  93.5 0.0 copy-start.2
  93.5 0.0 copy-start.1
  93.5 13.6 %convolution_convert_fusion = bf16[64,6144]{1,0:T(8,128)(2,1)} fusion(bf16[64,2048]{1,0:T(8,128)(2,1)S(1)} %all_gather.22, bf16[2048,6144]{0,1:T(8,128)(2,1)} %bitcast.66), kind=kOutput, calls=%fused_computation.2 | convolution fusion | flops 1611005952 | bytes 26214400 | tf_op jit(solution)/shard_map/dot_general | solution.py:25
  107.1 0.0 reduce-scatter.9.cloned.1.call-update
  107.1 0.0 all-gather.7.cloned.1.call-start
  107.1 0.0 copy-done.2
  107.2 0.1 and_bitcast_fusion.1
  107.2 0.1 compare_and_fusion.1
  107.3 0.0 reduce-scatter.5.cloned.1.call-done
  107.4 1.2 stack_reshape.6
  108.6 0.2 copy.65
  108.7 15.1 %all-gather.5.cloned.1.call-done = bf16[64,2,3,2048]{3,1,2,0:T(2,128)(2,1)} async-done(((bf16[16,2,3,2048]{3,1,2,0:T(2,128)(2,1)}), bf16[64,2,3,2048]{3,1,2,0:T(2,128)(2,1)}) %all-gather.5.cloned.1.call-update) | async-done | bytes 1572880 | tf_op jit(solution)/shard_map/all_gather | solution.py:34
  123.8 2.7 %gather_fusion = bf16[16,2,3,2048]{3,1,2,0:T(2,128)(2,1)S(1)} fusion(bf16[64,2,3,2048]{3,1,2,0:T(2,128)(2,1)} %all-gather.5.cloned.1.call-done, s32[1024]{0:T(1024)S(1)} %pad_clamp_fusion.1), kind=kCustom, calls=%fused_computation.clone | custom fusion | bytes 786496 | tf_op jit(solution)/shard_map/jit(_take)/gather | solution.py:36
  126.6 0.3 fusion.5
  126.9 1.2 copy.66
  128.1 0.0 all-gather.7.cloned.1.call-update
  128.1 0.0 reduce-scatter.11.cloned.1.call-start
  128.1 0.1 and_bitcast_fusion
  128.2 0.1 compare_and_fusion
  128.3 0.0 copy-done.1
  128.3 1.0 convert_element_type.107
  129.3 20.5 %reduce-scatter.9.cloned.1.call-done = bf16[16,6144]{1,0:T(8,128)(2,1)} async-done(((bf16[64,6144]{1,0:T(8,128)(2,1)}), bf16[16,6144]{1,0:T(8,128)(2,1)}) %reduce-scatter.9.cloned.1.call-update) | async-done | bytes 196624 | tf_op jit(solution)/shard_map/reduce_scatter | solution.py:24
  149.8 1.0 convert_element_type.111
  150.8 20.7 %all-gather.7.cloned.1.call-done = bf16[64,2,3,2048]{3,1,2,0:T(2,128)(2,1)} async-done(((bf16[16,2,3,2048]{3,1,2,0:T(2,128)(2,1)}), bf16[64,2,3,2048]{3,1,2,0:T(2,128)(2,1)}) %all-gather.7.cloned.1.call-update) | async-done | bytes 1572880 | tf_op jit(solution)/shard_map/all_gather | solution.py:34
  171.5 2.7 %gather_fusion.1 = bf16[16,2,3,2048]{3,1,2,0:T(2,128)(2,1)S(1)} fusion(bf16[64,2,3,2048]{3,1,2,0:T(2,128)(2,1)} %all-gather.7.cloned.1.call-done, s32[1024]{0:T(1024)S(1)} %pad_clamp_fusion), kind=kCustom, calls=%fused_computation.1.clone | custom fusion | bytes 786496 | tf_op jit(solution)/shard_map/jit(_take)/gather | solution.py:36
  174.2 0.3 fusion.4
  174.5 0.2 fusion.1
  174.8 6.0 %all-gather.1 = bf16[64,1,2048]{2,0,1:T(8,128)(2,1)S(1)} all-gather(bf16[16,1,2048]{2,0,1:T(8,128)(2,1)S(1)} %fusion.14), channel_id=3, replica_groups=mesh['groups'=2,'wide'=4,'narrow'=4] {'narrow'}, dimensions={0}, use_global_device_ids=true | all-gather | bytes 327680 | tf_op jit(solution)/shard_map/all_gather | solution.py:44
  180.8 5.7 %convolution_convert_fusion.2 = bf16[64,2048]{1,0:T(8,128)(2,1)} fusion(bf16[2048,2048]{1,0:T(8,128)(2,1)} %param.15, bf16[64,1,2048]{2,0,1:T(8,128)(2,1)S(1)} %all-gather.1), kind=kOutput, calls=%fused_computation.4 | convolution fusion | flops 537001984 | bytes 8912896 | tf_op jit(solution)/shard_map/dot_general | solution.py:43
  186.4 0.0 reduce-scatter.11.cloned.1.call-update
  186.4 0.0 reduce-scatter.7.cloned.1.call-start
  186.5 5.9 %all-gather = bf16[64,1,2048]{2,0,1:T(8,128)(2,1)S(1)} all-gather(bf16[16,1,2048]{2,0,1:T(8,128)(2,1)S(1)} %fusion.15), channel_id=2, replica_groups=mesh['groups'=2,'wide'=4,'narrow'=4] {'narrow'}, dimensions={0}, use_global_device_ids=true | all-gather | bytes 327680 | tf_op jit(solution)/shard_map/all_gather | solution.py:44
  192.4 0.0 copy-start
  192.4 5.7 %convolution_convert_fusion.3 = bf16[64,2048]{1,0:T(8,128)(2,1)} fusion(bf16[2048,2048]{1,0:T(8,128)(2,1)} %param.15, bf16[64,1,2048]{2,0,1:T(8,128)(2,1)S(1)} %all-gather), kind=kOutput, calls=%fused_computation.5 | convolution fusion | flops 537001984 | bytes 8912896 | tf_op jit(solution)/shard_map/dot_general | solution.py:43
  198.1 0.0 reduce-scatter.7.cloned.1.call-update
  198.1 0.0 copy-done
  198.1 0.3 stack_reshape.7
  198.4 0.2 copy.69
  198.6 1.2 copy.70
  199.8 6.5 %reduce-scatter.11.cloned.1.call-done = bf16[16,2048]{1,0:T(8,128)(2,1)} async-done(((bf16[64,2048]{1,0:T(8,128)(2,1)}), bf16[16,2048]{1,0:T(8,128)(2,1)}) %reduce-scatter.11.cloned.1.call-update) | async-done | bytes 65552 | tf_op jit(solution)/shard_map/reduce_scatter | solution.py:49
  206.3 20.2 %reduce-scatter.7.cloned.1.call-done = bf16[16,2048]{1,0:T(8,128)(2,1)} async-done(((bf16[64,2048]{1,0:T(8,128)(2,1)}), bf16[16,2048]{1,0:T(8,128)(2,1)}) %reduce-scatter.7.cloned.1.call-update) | async-done | bytes 65552 | tf_op jit(solution)/shard_map/reduce_scatter | solution.py:49
  226.5 1.5 pad_maximum_fusion.2
  (11 shorter events, 0.2 us)
Async XLA Ops:
  7.2 100.2 %reduce-scatter.5.cloned.1.call-start = ((), (), s32[]{:S(2)}) async-start(), calls=%async_computation.5 | async-start | bytes 983040 | tf_op jit(solution)/shard_map/reduce_scatter | solution.py:24
  78.4 45.4 %all-gather.5.cloned.1.call-start = ((), (), s32[]{:S(2)}) async-start(), calls=%async_computation.4 | async-start | bytes 1966080 | tf_op jit(solution)/shard_map/all_gather | solution.py:34
  79.2 70.6 %reduce-scatter.9.cloned.1.call-start = ((), (), s32[]{:S(2)}) async-start(), calls=%async_computation.8 | async-start | bytes 983040 | tf_op jit(solution)/shard_map/reduce_scatter | solution.py:24
  93.5 13.7 %copy-start.2 = (s32[2,64]{1,0:T(2,128)S(1)}, s32[2,64]{1,0:T(2,128)}, u32[]{:S(2)}) copy-start(s32[2,64]{1,0:T(2,128)} %param.10) | copy-start | bytes 1540
  93.5 34.8 %copy-start.1 = (f32[3,3,2048]{2,1,0:T(4,128)S(1)}, f32[3,3,2048]{2,1,0:T(4,128)}, u32[]{:S(2)}) copy-start(f32[3,3,2048]{2,1,0:T(4,128)} %param.14) | copy-start | bytes 221188
  107.1 64.4 %all-gather.7.cloned.1.call-start = ((), (), s32[]{:S(2)}) async-start(), calls=%async_computation.7 | async-start | bytes 1966080 | tf_op jit(solution)/shard_map/all_gather | solution.py:34
  128.1 78.2 %reduce-scatter.11.cloned.1.call-start = ((), (), s32[]{:S(2)}) async-start(), calls=%async_computation.9 | async-start | bytes 327680 | tf_op jit(solution)/shard_map/reduce_scatter | solution.py:49
  186.4 40.0 %reduce-scatter.7.cloned.1.call-start = ((), (), s32[]{:S(2)}) async-start(), calls=%async_computation.6 | async-start | bytes 327680 | tf_op jit(solution)/shard_map/reduce_scatter | solution.py:49
  192.4 5.7 %copy-start = (bf16[16,6144]{1,0:T(8,128)(2,1)S(1)}, bf16[16,6144]{1,0:T(8,128)(2,1)}, u32[]{:S(2)}) copy-start(bf16[16,6144]{1,0:T(8,128)(2,1)} %reduce-scatter.9.cloned.1.call-done) | copy-start | bytes 589828
Sparse Core Ops, SparseCore 0:
  78.6 23.8 reduce-scatter.4
  104.1 19.6 all-gather.4
  126.5 23.2 reduce-scatter.8
  151.8 19.6 all-gather.6
  186.6 19.6 reduce-scatter.10
  208.5 17.9 reduce-scatter.6
where the time goes:
time: 236 us; the launch traced here: 235 us
  waiting for transfers between devices  83.8 us (36%)
  blocking collectives  48.5 us (21%)
  local copies, waits for them, and re-layouts  43 us (18%)
  matrix products  38.4 us (16%)
  between operations  14.3 us (6%)
  other arithmetic  6.65 us (3%)
    all_gather x2, waiting for transfers between devices, shards(): piece = lax.all_gather(memory, 'narrow', axis=0, tiled=True)  35.8 us
    unnamed x8, local copies, waits for them, and re-layouts  34.5 us
    all_gather x2, blocking collectives, shards(): gathered = lax.all_gather(normed, 'wide', axis=0, tiled=True)  28.3 us
    dot_general x2, matrix products, shards(): jnp.dot(gathered, flat_in, preferred_element_type=jnp.float32)  27 us
    reduce_scatter x2, waiting for transfers between devices, shards(): lax.psum_scatter(partial_out.astype(jnp.bfloat16), 'wide', scatter_dimens...  26.7 us
    reduce_scatter x2, waiting for transfers between devices, shards(): lax.psum_scatter(jnp.dot(gathered, flat_in, preferred_element_type=jnp.fl...  20.5 us
    all_gather x2, blocking collectives, shards(): lax.all_gather(gated, 'narrow', axis=0, tiled=True)  11.8 us
    dot_general x2, matrix products, shards(): jnp.dot(lax.all_gather(gated, 'narrow', axis=0, tiled=True), out_weight,...  11.4 us
  transfers between devices with their start and end apart: 6, of which 5 were waited for; matrix products, arithmetic and copies ran while one was open for 12% of the time, Pallas kernels for 0%

commit v1 on v0

v1 whole, which is shorter than its diff:
```python
import jax
import jax.numpy as jnp
from jax import lax
from jax.sharding import PartitionSpec as P

D = 8192


def swap(value, axis, hop):
    count = lax.axis_size(axis)
    return lax.ppermute(value, axis, [(i, i ^ hop) for i in range(count)])


def shards(tokens, assign, state, norm_gain, in_weight, conv_weight, out_weight):
    narrow = lax.axis_size("narrow")
    wide = lax.axis_size("wide")
    steps, rows, feats = tokens.shape
    share = state.shape[0]
    total = narrow * share
    chans = in_weight.shape[2]
    mine = lax.axis_index("narrow")
    direct = wide <= 4
    place = lax.axis_index("wide") if direct else 0
    evens = [2 * k for k in range(narrow // 2)]
    rels = evens + [k + 1 for k in evens]
    half = (narrow // 2) * steps * share
    unit = steps * share

    past = state.transpose(0, 2, 1, 3)
    near = jnp.stack([past] + [swap(past, "narrow", k) for k in evens[1:]])
    far = swap(near, "narrow", 1)
    pool = jnp.concatenate([near, far]).reshape(total, -1)

    if direct:
        blocks = jnp.stack([tokens] + [swap(tokens, "wide", k) for k in range(1, wide)])
    else:
        blocks = lax.all_gather(tokens, "wide", axis=0)
    blocks = blocks.reshape(wide * steps * rows, feats)

    owners = jnp.array(rels, jnp.int32) ^ mine
    slots = (owners[:, None] * share + jnp.arange(share)[None, :])
    first = assign[1][slots]
    wanted = jnp.stack([first, slots], axis=1)
    stage = jnp.arange(steps, dtype=jnp.int32)[None, :, None]
    spot = (((wanted // rows) ^ place) * steps + stage) * rows + wanted % rows
    spot = spot.reshape(-1)
    picker = (spot[:, None] == jnp.arange(wide * steps * rows)[None, :]).astype(jnp.bfloat16)
    ordered = jnp.dot(picker, blocks, preferred_element_type=jnp.float32)
    squares = jnp.sum(ordered * ordered, axis=-1)
    scaled = (ordered * norm_gain).astype(jnp.bfloat16)

    def scatter(partial, kind):
        partial = partial[:half] + swap(partial[half:].astype(kind), "narrow", 1).astype(
            jnp.float32
        )
        result = partial[:unit]
        for index, k in enumerate(evens[1:], 1):
            piece = partial[index * unit : (index + 1) * unit].astype(kind)
            result = result + swap(piece, "narrow", k).astype(jnp.float32)
        return result

    meansq = scatter(squares, jnp.float32) / D
    scale = lax.rsqrt(meansq + 1e-05)[:, None]

    comp = assign[0][lax.dynamic_slice_in_dim(assign[1], mine * share, share, 0)]
    ranks = [rels.index(k) for k in range(narrow)]
    source = jnp.array(ranks, jnp.int32)[(comp // share) ^ mine] * share + comp % share
    chooser = (source[:, None] == jnp.arange(total)[None, :]).astype(jnp.bfloat16)
    kept = jnp.dot(chooser, pool, preferred_element_type=jnp.float32).reshape(share, 3, 2, chans)

    weights = in_weight.transpose(1, 0, 2)
    gates = []
    fresh = []
    for j in range(3):
        product = jnp.dot(scaled, weights[j], preferred_element_type=jnp.float32)
        new = (scatter(product, jnp.bfloat16) * scale).astype(jnp.bfloat16)
        new0, new1 = new[:share], new[share:]
        fresh.append(jnp.stack([new0, new1], axis=1))
        taps = conv_weight[:, j]
        new0, new1 = new0.astype(jnp.float32), new1.astype(jnp.float32)
        mixed0 = taps[0] * kept[:, j, 0] + taps[1] * kept[:, j, 1] + taps[2] * new0
        mixed1 = taps[0] * kept[:, j, 1] + taps[1] * new0 + taps[2] * new1
        gates.append(jnp.concatenate([mixed0, mixed1]))
    memory = jnp.stack(fresh, axis=1).transpose(0, 2, 1, 3)
    gated = (gates[0] * gates[1] * gates[2]).astype(jnp.bfloat16)

    near = jnp.stack([gated] + [swap(gated, "narrow", k) for k in evens[1:]])
    every = jnp.concatenate([near, swap(near, "narrow", 1)]).reshape(narrow * unit, chans)

    order = wanted.reshape(len(rels), steps, share)
    goal = (((order // rows) ^ place) * steps + stage) * rows + order % rows
    goal = goal.reshape(-1)
    sorter = (jnp.arange(wide * steps * rows)[:, None] == goal[None, :]).astype(jnp.bfloat16)
    lined = jnp.dot(sorter, every, preferred_element_type=jnp.float32).astype(jnp.bfloat16)
    partial_out = jnp.dot(lined, out_weight, preferred_element_type=jnp.float32)
    if direct:
        block = steps * rows
        out = partial_out[:block]
        for k in range(1, wide):
            piece = partial_out[k * block : (k + 1) * block].astype(jnp.bfloat16)
            out = out + swap(piece, "wide", k).astype(jnp.float32)
        out = out.astype(jnp.bfloat16)
    else:
        out = lax.psum_scatter(
            partial_out.astype(jnp.bfloat16), "wide", scatter_dimension=0, tiled=True
        )
    return (out.reshape(steps, rows, -1), memory)


def solution(mesh):
    in_specs = (
        P(None, ("groups", "wide"), "narrow"),
        P(None, "groups"),
        P(("groups", "narrow"), None, None, "wide"),
        P("narrow"),
        P("narrow", None, "wide"),
        P(None, None, "wide"),
        P("wide", "narrow"),
    )
    out_specs = (P(None, ("groups", "wide"), "narrow"), P(("groups", "narrow"), None, None, "wide"))
    return jax.shard_map(shards, mesh=mesh, in_specs=in_specs, out_specs=out_specs, check_vma=False)
```

time: 236 us -> 85.6 us (0.36)
  waiting for transfers between devices: 83.8 us -> 21.6 us
  blocking collectives: 48.5 us -> 0 us
  local copies, waits for them, and re-layouts: 43 us -> 9.99 us
  starting transfers between devices: 0.24 us -> 19.7 us
  matrix products: 38.4 us -> 21.5 us
  between operations: 14.3 us -> 0.95 us
  other arithmetic: 6.65 us -> 11.3 us
    reduce_scatter x4 -> x0, waiting for transfers between devices: 47.2 us -> none  [the longest x2 26.7 us: shards(): lax.psum_scatter(partial_out.astype(jnp.bfloat16), 'wide', scatter_dimens...]
    all_gather x4 -> x0, blocking collectives: 40.2 us -> none  [the longest x2 28.3 us: shards(): gathered = lax.all_gather(normed, 'wide', axis=0, tiled=True)]
    all_gather x2 -> x0, waiting for transfers between devices: 35.8 us -> none  [shards(): piece = lax.all_gather(memory, 'narrow', axis=0, tiled=True)]
    unnamed x8 -> x9, local copies, waits for them, and re-layouts: 34.5 us -> 1.17 us
    ppermute x0 -> x18, waiting for transfers between devices: none -> 21.6 us  [swap(): return lax.ppermute(value, axis, [(i, i ^ hop) for i in range(count)])]
    ppermute x0 -> x18, starting transfers between devices: none -> 19.7 us  [swap(): return lax.ppermute(value, axis, [(i, i ^ hop) for i in range(count)])]
    dot_general x4 -> x6, matrix products: 38.4 us -> 21.5 us  [the longest x3 14 us: shards(): product = jnp.dot(scaled, weights[j], preferred_element_type=jnp.float32)]
    psum x1 -> x0, blocking collectives: 8.34 us -> none  [shards(): squares = lax.psum(jnp.sum(current * current, axis=-1), 'narrow')]
  transfers between devices with their start and end apart: 6 -> 18, of which waited for: 5 -> 8; matrix products, arithmetic and copies ran while one was open for 12% -> 34% of each run, Pallas kernels for 0% -> 0%
where the time goes in v1:
time: 85.6 us; the launch traced here: 85 us
  waiting for transfers between devices  21.6 us (25%)
  matrix products  21.5 us (25%)
  starting transfers between devices  19.7 us (23%)
  other arithmetic  11.3 us (13%)
  local copies, waits for them, and re-layouts  9.99 us (12%)
  between operations  0.95 us (1%)
    ppermute x18, waiting for transfers between devices, swap(): return lax.ppermute(value, axis, [(i, i ^ hop) for i in range(count)])  21.6 us
    ppermute x18, starting transfers between devices, swap(): return lax.ppermute(value, axis, [(i, i ^ hop) for i in range(count)])  19.7 us
    dot_general x3, matrix products, shards(): product = jnp.dot(scaled, weights[j], preferred_element_type=jnp.float32)  14 us
    dot_general x1, matrix products, shards(): partial_out = jnp.dot(lined, out_weight, preferred_element_type=jnp.float32)  4.78 us
    another operation x3, other arithmetic, shards(): memory = jnp.stack(fresh, axis=1).transpose(0, 2, 1, 3)  2.44 us
    concatenate x1, other arithmetic, shards(): pool = jnp.concatenate([near, far]).reshape(total, -1)  2.3 us
  transfers between devices with their start and end apart: 18, of which 8 were waited for; matrix products, arithmetic and copies ran while one was open for 34% of the time, Pallas kernels for 0%

profile of v1, /device:TPU:0, one launch (start us, length us, event | category | flops | bytes accessed | tf_op | source)
XLA Modules:
  0.0 85.0 jit_solution(16385823965692124181)
XLA Ops:
  0.6 3.1 %collective-permute-start.2 = (bf16[2,16,2048]{2,1,0:T(8,128)(2,1)}, bf16[2,16,2048]{2,1,0:T(8,128)(2,1)S(1)}, u32[]{:S(2)}, u32[]{:S(2)}) collective-permute-start(bf16[2,16,2048]{2,1,0:T(8,128)(2,1)} %param.9), channel_id=1, source_target_pairs={{0,4},{4,0},{8,12},{12,8},{1,5},{5,1},{9,13},{13,9},{2,6},{6,2},{1... | collective-permute-start | bytes 393224 | tf_op jit(solution)/shard_map/ppermute | solution.py:11
  3.7 2.6 %collective-permute-start.3 = (bf16[2,16,2048]{2,1,0:T(8,128)(2,1)}, bf16[2,16,2048]{2,1,0:T(8,128)(2,1)S(1)}, u32[]{:S(2)}, u32[]{:S(2)}) collective-permute-start(bf16[2,16,2048]{2,1,0:T(8,128)(2,1)} %param.9), channel_id=1, source_target_pairs={{0,8},{4,12},{8,0},{12,4},{1,9},{5,13},{9,1},{13,5},{2,10},{6,14},... | collective-permute-start | bytes 393224 | tf_op jit(solution)/shard_map/ppermute | solution.py:11
  6.3 1.7 %collective-permute-start = (bf16[16,3,2,2048]{3,2,1,0:T(2,128)(2,1)}, bf16[16,3,2,2048]{3,2,1,0:T(2,128)(2,1)S(1)}, u32[]{:S(2)}, u32[]{:S(2)}) collective-permute-start(bf16[16,3,2,2048]{3,2,1,0:T(2,128)(2,1)} %bitcast.137), channel_id=1, source_target_pairs={{0,2},{1,3},{2,0},{3,1},{4,6},{5,7},{6,4},{7,5},{8,10},{9,11},{10,... | collective-permute-start | bytes 1179656 | tf_op jit(solution)/shard_map/ppermute | solution.py:11
  8.0 0.7 xor_multiply_fusion
  8.7 0.1 compare_select_fusion
  8.8 0.1 iota_add_fusion
  8.8 0.1 reshape.422
  8.9 0.8 slice_bitcast_fusion.19
  9.7 0.8 gather_fusion
  10.4 0.1 stack.79
  10.5 0.1 stack.81
  10.6 0.1 add.237
  10.7 0.1 fusion.44
  10.8 0.7 gather_fusion.1
  11.5 1.3 %gather_fusion.2 = s32[16]{0:T(128)S(1)} fusion(s32[4]{0:T(128)} %constant.82.clone, s32[1024]{0:T(1024)S(1)} %pad_clamp_fusion), kind=kCustom, calls=%fused_computation.2 | custom fusion | bytes 192 | tf_op jit(solution)/shard_map/gather | solution.py:67
  12.8 0.6 fusion.42
  13.4 1.6 %fusion.47 = (f32[1,1,2048]{2,1,0:T(1,128)S(1)}, f32[1,1,2048]{2,1,0:T(1,128)S(1)}, f32[1,1,2048]{2,1,0:T(1,128)}, f32[1,1,2048]{2,1,0:T(1,128)}, f32[1,1,2048]{...) fusion(f32[3,3,2048]{2,1,0:T(4,128)} %param.14), kind=kLoop, calls=%fused_computation.125 | loop fusion | bytes 147456 | tf_op jit(solution)/shard_map/slice | solution.py:81
  15.0 1.9 %collective-permute-done.3 = bf16[2,16,2048]{2,1,0:T(8,128)(2,1)S(1)} collective-permute-done((bf16[2,16,2048]{2,1,0:T(8,128)(2,1)}, bf16[2,16,2048]{2,1,0:T(8,128)(2,1)S(1)}, u32[]{:S(2)}, u32[]{:S(2)}) %collective-permute-start.3) | collective-permute-done | bytes 131104 | tf_op jit(solution)/shard_map/ppermute | solution.py:11
  16.9 1.0 %pad_maximum_fusion.2 = bf16[4,2,16,2048]{3,2,1,0:T(8,128)(2,1)S(1)} fusion(bf16[1,2,16,2048]{3,2,1,0:T(8,128)(2,1)S(1)} %bitcast.155, bf16[1,2,16,2048]{3,2,1,0:T(8,128)(2,1)S(1)} %bitcast.154, bf16[1,2,16,2048]{3,2,1,0:T(8,128)(2,1)S(1)} %bitcast.153, bf16[1,2,16,2048]{3,2,1,0:T(8,128)(2,1)} %bitcast.152), kind=kLoop, calls=%fused_computation.23 | loop fusion | flops 786432 | bytes 1048576 | tf_op jit(solution)/shard_map/stack | solution.py:35
  17.8 1.1 %multiply_reduce_fusion = (f32[128]{0:T(128)S(1)}, bf16[128,2048]{1,0:T(8,128)(2,1)S(1)}) fusion(f32[2048]{0:T(1024)} %param.12, bf16[128,2048]{1,0:T(8,128)(2,1)S(1)} %bitcast.148, s32[128]{0:T(128)S(1)} %fusion.41), kind=kOutput, calls=%fused_computation.14 | convolution fusion | flops 68173696 | bytes 1057792 | tf_op jit(solution)/shard_map/dot_general | solution.py:48
  19.0 4.7 %fusion.1 = f32[128,2048]{1,0:T(8,128)S(1)} fusion(bf16[128,2048]{1,0:T(8,128)(2,1)S(1)} %get-tuple-element.7, bf16[3,2048,2048]{2,1,0:T(8,128)(2,1)} %bitcast.165), kind=kOutput, calls=%fused_computation.6 | convolution fusion | flops 1073741824 | bytes 9961472 | tf_op jit(solution)/shard_map/dot_general | solution.py:75
  23.6 4.7 %fusion = f32[128,2048]{1,0:T(8,128)S(1)} fusion(bf16[128,2048]{1,0:T(8,128)(2,1)S(1)} %get-tuple-element.7, bf16[3,2048,2048]{2,1,0:T(8,128)(2,1)} %bitcast.166), kind=kOutput, calls=%fused_computation.4 | convolution fusion | flops 1073741824 | bytes 9961472 | tf_op jit(solution)/shard_map/dot_general | solution.py:75
  28.3 0.1 slice.194
  28.4 4.7 %fusion.2 = f32[128,2048]{1,0:T(8,128)S(1)} fusion(bf16[128,2048]{1,0:T(8,128)(2,1)S(1)} %get-tuple-element.7, bf16[3,2048,2048]{2,1,0:T(8,128)(2,1)} %bitcast.167), kind=kOutput, calls=%fused_computation.8 | convolution fusion | flops 1073741824 | bytes 9961472 | tf_op jit(solution)/shard_map/dot_general | solution.py:75
  33.2 0.5 collective-permute-start.9
  33.7 0.1 collective-permute-start.11
  33.9 0.1 slice.196
  34.0 1.5 %collective-permute-start.8 = (f32[32]{0:T(128)S(1)}, f32[32]{0:T(128)S(1)}, u32[]{:S(2)}, u32[]{:S(2)}) collective-permute-start(f32[32]{0:T(128)S(1)} %slice.196), channel_id=1, source_target_pairs={{0,2},{1,3},{2,0},{3,1},{4,6},{5,7},{6,4},{7,5},{8,10},{9,11},{10,... | collective-permute-start | bytes 392 | tf_op jit(solution)/shard_map/ppermute | solution.py:11
  35.5 0.2 collective-permute-start.5
  35.7 1.8 %collective-permute-done.8 = f32[32]{0:T(128)S(1)} collective-permute-done((f32[32]{0:T(128)S(1)}, f32[32]{0:T(128)S(1)}, u32[]{:S(2)}, u32[]{:S(2)}) %collective-permute-start.8) | collective-permute-done | bytes 160 | tf_op jit(solution)/shard_map/ppermute | solution.py:11
  37.5 0.1 slice_add_fusion.1
  37.6 1.6 %collective-permute-start.10 = (bf16[32,2048]{1,0:T(8,128)(2,1)S(1)}, bf16[32,2048]{1,0:T(8,128)(2,1)S(1)}, u32[]{:S(2)}, u32[]{:S(2)}) collective-permute-start(bf16[32,2048]{1,0:T(8,128)(2,1)S(1)} %slice.360), channel_id=1, source_target_pairs={{0,2},{1,3},{2,0},{3,1},{4,6},{5,7},{6,4},{7,5},{8,10},{9,11},{10,... | collective-permute-start | bytes 393224 | tf_op jit(solution)/shard_map/ppermute | solution.py:11
  39.2 0.1 slice_add_fusion
  39.3 0.6 collective-permute-start.12
  39.9 0.1 slice_add_fusion.2
  40.0 1.5 %collective-permute-start.6 = (bf16[32,2048]{1,0:T(8,128)(2,1)S(1)}, bf16[32,2048]{1,0:T(8,128)(2,1)S(1)}, u32[]{:S(2)}, u32[]{:S(2)}) collective-permute-start(bf16[32,2048]{1,0:T(8,128)(2,1)S(1)} %slice.361), channel_id=1, source_target_pairs={{0,2},{1,3},{2,0},{3,1},{4,6},{5,7},{6,4},{7,5},{8,10},{9,11},{10,... | collective-permute-start | bytes 393224 | tf_op jit(solution)/shard_map/ppermute | solution.py:11
  41.5 1.1 %pad_maximum_fusion.1 = bf16[2,16,3,2,2048]{4,3,2,1,0:T(2,128)(2,1)S(1)} fusion(bf16[1,16,3,2,2048]{4,3,2,1,0:T(2,128)(2,1)S(1)} %bitcast.140, bf16[1,16,3,2,2048]{4,3,2,1,0:T(2,128)(2,1)S(1)} %bitcast.138), kind=kLoop, calls=%fused_computation.16 | loop fusion | flops 393216 | bytes 1572864 | tf_op jit(solution)/shard_map/stack | solution.py:30
  42.6 0.1 collective-permute-start.1
  42.7 1.4 %collective-permute-done.10 = bf16[32,2048]{1,0:T(8,128)(2,1)S(1)} collective-permute-done((bf16[32,2048]{1,0:T(8,128)(2,1)S(1)}, bf16[32,2048]{1,0:T(8,128)(2,1)S(1)}, u32[]{:S(2)}, u32[]{:S(2)}) %collective-permute-start.10) | collective-permute-done | bytes 131104 | tf_op jit(solution)/shard_map/ppermute | solution.py:11
  44.1 2.5 %collective-permute-done.12 = bf16[32,2048]{1,0:T(8,128)(2,1)S(1)} collective-permute-done((bf16[32,2048]{1,0:T(8,128)(2,1)S(1)}, bf16[32,2048]{1,0:T(8,128)(2,1)S(1)}, u32[]{:S(2)}, u32[]{:S(2)}) %collective-permute-start.12) | collective-permute-done | bytes 131104 | tf_op jit(solution)/shard_map/ppermute | solution.py:11
  46.6 1.4 %collective-permute-done.6 = bf16[32,2048]{1,0:T(8,128)(2,1)S(1)} collective-permute-done((bf16[32,2048]{1,0:T(8,128)(2,1)S(1)}, bf16[32,2048]{1,0:T(8,128)(2,1)S(1)}, u32[]{:S(2)}, u32[]{:S(2)}) %collective-permute-start.6) | collective-permute-done | bytes 131104 | tf_op jit(solution)/shard_map/ppermute | solution.py:11
  48.0 0.1 fusion.10
  48.2 0.7 maximum_bitcast_fusion.1
  48.8 0.7 slice_bitcast_fusion.15
  49.5 2.3 %pad_maximum_fusion = bf16[4,16,3,2,2048]{4,3,2,1,0:T(2,128)(2,1)S(1)} fusion(bf16[2,16,3,2,2048]{4,3,2,1,0:T(2,128)(2,1)S(1)} %collective-permute-done.1, bf16[1,16,3,2,2048]{4,3,2,1,0:T(2,128)(2,1)S(1)} %bitcast.141, bf16[1,16,3,2,2048]{4,3,2,1,0:T(2,128)(2,1)S(1)} %bitcast.139), kind=kLoop, calls=%fused_computation.10 | loop fusion | flops 1572864 | bytes 3145728 | tf_op jit(solution)/shard_map/concatenate | solution.py:32
  51.8 1.2 %reshape.416 = bf16[64,12288]{1,0:T(8,128)(2,1)S(1)} reshape(bf16[4,16,3,2,2048]{4,3,2,1,0:T(2,128)(2,1)S(1)} %pad_maximum_fusion) | data formatting | bytes 3145728 | tf_op jit(solution)/shard_map/reshape | solution.py:32
  53.0 1.2 %dot_general.26 = bf16[3,2,2048,64]{2,1,0,3:T(2,128)(2,1)S(1)} reshape(bf16[12288,64]{0,1:T(8,128)(2,1)S(1)} %bitcast.135) | data formatting | bytes 3145728 | tf_op jit(solution)/shard_map/dot_general | solution.py:69
  54.2 1.6 %fusion.3 = f32[16,3,2,2048]{3,0,2,1:T(8,128)S(1)} fusion(bf16[3,2,2048,64]{2,1,0,3:T(2,128)(2,1)S(1)} %dot_general.26, s32[16]{0:T(128)} %fusion.42), kind=kOutput, calls=%fused_computation.11 | convolution fusion | flops 25166848 | bytes 2359360 | tf_op jit(solution)/shard_map/dot_general | solution.py:69
  55.8 0.8 fusion.19
  56.6 0.9 %fusion.25 = (f32[16,2048]{1,0:T(8,128)S(1)}, f32[16,2048]{1,0:T(8,128)S(1)}, f32[16,2048]{1,0:T(8,128)S(1)}, f32[16,2048]{1,0:T(8,128)S(1)}) fusion(f32[16,3,2,2048]{3,0,2,1:T(8,128)S(1)} %fusion.3, f32[2048]{0:T(1024)} %bitcast.160, f32[2048]{0:T(1024)} %bitcast.161, f32[2048]{0:T(1024)S(1)} %bitcast.156, bf16[32,2048]{1,0:T(8,128)(2,1)S(1)} %get-tuple-element.37, ...), kind=kLoop, calls=%fused_computation.61 | loop fusion | flops 786432 | bytes 1359872 | tf_op jit(solution)/shard_map/add | solution.py:81
  57.5 1.6 %collective-permute-start.13 = (bf16[32,2048]{1,0:T(8,128)(2,1)S(1)}, bf16[32,2048]{1,0:T(8,128)(2,1)S(1)}, u32[]{:S(2)}, u32[]{:S(2)}) collective-permute-start(bf16[32,2048]{1,0:T(8,128)(2,1)S(1)} %fusion.18), channel_id=1, source_target_pairs={{0,2},{1,3},{2,0},{3,1},{4,6},{5,7},{6,4},{7,5},{8,10},{9,11},{10,... | collective-permute-start | bytes 393224 | tf_op jit(solution)/shard_map/ppermute | solution.py:11
  59.2 3.4 %collective-permute-done.13 = bf16[32,2048]{1,0:T(8,128)(2,1)S(1)} collective-permute-done((bf16[32,2048]{1,0:T(8,128)(2,1)S(1)}, bf16[32,2048]{1,0:T(8,128)(2,1)S(1)}, u32[]{:S(2)}, u32[]{:S(2)}) %collective-permute-start.13) | collective-permute-done | bytes 131104 | tf_op jit(solution)/shard_map/ppermute | solution.py:11
  62.6 0.1 collective-permute-start.14
  62.7 0.9 %maximum_bitcast_fusion.2 = bf16[16,1,2,2048]{3,0,2,1:T(8,128)(2,1)S(1)} fusion(bf16[16,1,2048]{2,0,1:T(8,128)(2,1)} %get-tuple-element.42, bf16[16,1,2048]{2,0,1:T(8,128)(2,1)} %get-tuple-element.43), kind=kLoop, calls=%fused_computation.77 | loop fusion | flops 65536 | bytes 262144 | tf_op jit(solution)/shard_map/stack | solution.py:84
  63.6 0.9 %maximum_bitcast_fusion.3 = bf16[16,1,2,2048]{3,0,2,1:T(8,128)(2,1)S(1)} fusion(bf16[16,1,2048]{2,0,1:T(8,128)(2,1)} %get-tuple-element.24, bf16[16,1,2048]{2,0,1:T(8,128)(2,1)} %get-tuple-element.23), kind=kLoop, calls=%fused_computation.78 | loop fusion | flops 65536 | bytes 262144 | tf_op jit(solution)/shard_map/stack | solution.py:84
  64.5 0.1 pad_maximum_fusion.3
  64.5 4.8 %fusion.48 = (bf16[128,2048]{1,0:T(8,128)(2,1)S(1)}, f32[128,2048]{1,0:T(8,128)S(1)}) fusion(bf16[2048,2048]{1,0:T(8,128)(2,1)} %param.15, bf16[128,2048]{1,0:T(8,128)(2,1)S(1)} %bitcast.136, s32[128]{0:T(128)S(1)} %copy-done.3), kind=kOutput, calls=%fused_computation.126 | convolution fusion | flops 1141391360 | bytes 10486272 | tf_op jit(solution)/shard_map/dot_general | solution.py:95
  69.4 2.0 %collective-permute-start.15 = (bf16[32,2048]{1,0:T(8,128)(2,1)S(1)}, bf16[32,2048]{1,0:T(8,128)(2,1)S(1)}, u32[]{:S(2)}, u32[]{:S(2)}) collective-permute-start(bf16[32,2048]{1,0:T(8,128)(2,1)S(1)} %get-tuple-element.16), channel_id=1, source_target_pairs={{0,4},{4,0},{8,12},{12,8},{1,5},{5,1},{9,13},{13,9},{2,6},{6,2},{1... | collective-permute-start | bytes 393224 | tf_op jit(solution)/shard_map/ppermute | solution.py:11
  71.4 1.1 %collective-permute-start.16 = (bf16[32,2048]{1,0:T(8,128)(2,1)S(1)}, bf16[32,2048]{1,0:T(8,128)(2,1)S(1)}, u32[]{:S(2)}, u32[]{:S(2)}) collective-permute-start(bf16[32,2048]{1,0:T(8,128)(2,1)S(1)} %get-tuple-element.18), channel_id=1, source_target_pairs={{0,8},{4,12},{8,0},{12,4},{1,9},{5,13},{9,1},{13,5},{2,10},{6,14},... | collective-permute-start | bytes 393224 | tf_op jit(solution)/shard_map/ppermute | solution.py:11
  72.5 1.4 %collective-permute-start.17 = (bf16[32,2048]{1,0:T(8,128)(2,1)S(1)}, bf16[32,2048]{1,0:T(8,128)(2,1)S(1)}, u32[]{:S(2)}, u32[]{:S(2)}) collective-permute-start(bf16[32,2048]{1,0:T(8,128)(2,1)S(1)} %get-tuple-element.17), channel_id=1, source_target_pairs={{0,12},{4,8},{8,4},{12,0},{1,13},{5,9},{9,5},{13,1},{2,14},{6,10},... | collective-permute-start | bytes 393224 | tf_op jit(solution)/shard_map/ppermute | solution.py:11
  73.9 1.2 %copy.15 = bf16[16,2,3,2048]{3,1,2,0:T(2,128)(2,1)} copy(bf16[16,2,3,2048]{3,0,1,2:T(8,128)(2,1)S(1)} %maximum_bitcast_fusion) | data formatting | bytes 786432
  75.1 2.7 %collective-permute-done.15 = bf16[32,2048]{1,0:T(8,128)(2,1)S(1)} collective-permute-done((bf16[32,2048]{1,0:T(8,128)(2,1)S(1)}, bf16[32,2048]{1,0:T(8,128)(2,1)S(1)}, u32[]{:S(2)}, u32[]{:S(2)}) %collective-permute-start.15) | collective-permute-done | bytes 131104 | tf_op jit(solution)/shard_map/ppermute | solution.py:11
  77.8 6.5 %collective-permute-done.16 = bf16[32,2048]{1,0:T(8,128)(2,1)S(1)} collective-permute-done((bf16[32,2048]{1,0:T(8,128)(2,1)S(1)}, bf16[32,2048]{1,0:T(8,128)(2,1)S(1)}, u32[]{:S(2)}, u32[]{:S(2)}) %collective-permute-start.16) | collective-permute-done | bytes 131104 | tf_op jit(solution)/shard_map/ppermute | solution.py:11
  84.3 0.7 fusion.8
  (42 shorter events, 0.5 us)
Async XLA Ops:
  0.6 14.4 %collective-permute-start.2 = (bf16[2,16,2048]{2,1,0:T(8,128)(2,1)}, bf16[2,16,2048]{2,1,0:T(8,128)(2,1)S(1)}, u32[]{:S(2)}, u32[]{:S(2)}) collective-permute-start(bf16[2,16,2048]{2,1,0:T(8,128)(2,1)} %param.9), channel_id=1, source_target_pairs={{0,4},{4,0},{8,12},{12,8},{1,5},{5,1},{9,13},{13,9},{2,6},{6,2},{1... | collective-permute-start | bytes 393224 | tf_op jit(solution)/shard_map/ppermute | solution.py:11
  3.7 13.2 %collective-permute-start.3 = (bf16[2,16,2048]{2,1,0:T(8,128)(2,1)}, bf16[2,16,2048]{2,1,0:T(8,128)(2,1)S(1)}, u32[]{:S(2)}, u32[]{:S(2)}) collective-permute-start(bf16[2,16,2048]{2,1,0:T(8,128)(2,1)} %param.9), channel_id=1, source_target_pairs={{0,8},{4,12},{8,0},{12,4},{1,9},{5,13},{9,1},{13,5},{2,10},{6,14},... | collective-permute-start | bytes 393224 | tf_op jit(solution)/shard_map/ppermute | solution.py:11
  6.3 10.6 %collective-permute-start.4 = (bf16[2,16,2048]{2,1,0:T(8,128)(2,1)}, bf16[2,16,2048]{2,1,0:T(8,128)(2,1)S(1)}, u32[]{:S(2)}, u32[]{:S(2)}) collective-permute-start(bf16[2,16,2048]{2,1,0:T(8,128)(2,1)} %param.9), channel_id=1, source_target_pairs={{0,12},{4,8},{8,4},{12,0},{1,13},{5,9},{9,5},{13,1},{2,14},{6,10},... | collective-permute-start | bytes 393224 | tf_op jit(solution)/shard_map/ppermute | solution.py:11
  6.3 35.2 %collective-permute-start = (bf16[16,3,2,2048]{3,2,1,0:T(2,128)(2,1)}, bf16[16,3,2,2048]{3,2,1,0:T(2,128)(2,1)S(1)}, u32[]{:S(2)}, u32[]{:S(2)}) collective-permute-start(bf16[16,3,2,2048]{3,2,1,0:T(2,128)(2,1)} %bitcast.137), channel_id=1, source_target_pairs={{0,2},{1,3},{2,0},{3,1},{4,6},{5,7},{6,4},{7,5},{8,10},{9,11},{10,... | collective-permute-start | bytes 1179656 | tf_op jit(solution)/shard_map/ppermute | solution.py:11
  15.0 13.3 %copy-start.2 = (s32[128]{0:T(128)}, s32[128]{0:T(128)S(1)}, u32[]{:S(2)}) copy-start(s32[128]{0:T(128)S(1)} %fusion.41) | copy-start | bytes 1540
  28.4 13.1 %copy-start = (bf16[16,2,3,2048]{3,1,2,0:T(2,128)(2,1)S(1)}, bf16[16,2,3,2048]{3,1,2,0:T(2,128)(2,1)}, u32[]{:S(2)}) copy-start(bf16[16,2,3,2048]{3,1,2,0:T(2,128)(2,1)} %param.11) | copy-start | bytes 1179652
  28.4 5.5 %collective-permute-start.7 = (f32[64]{0:T(128)S(1)}, f32[64]{0:T(128)S(1)}, u32[]{:S(2)}, u32[]{:S(2)}) collective-permute-start(f32[64]{0:T(128)S(1)} %slice.194), channel_id=1, source_target_pairs={{0,1},{1,0},{2,3},{3,2},{4,5},{5,4},{6,7},{7,6},{8,9},{9,8},{10,11... | collective-permute-start | bytes 776 | tf_op jit(solution)/shard_map/ppermute | solution.py:11
  33.2 4.3 %collective-permute-start.9 = (bf16[64,2048]{1,0:T(8,128)(2,1)S(1)}, bf16[64,2048]{1,0:T(8,128)(2,1)S(1)}, u32[]{:S(2)}, u32[]{:S(2)}) collective-permute-start(bf16[64,2048]{1,0:T(8,128)(2,1)S(1)} %slice.357), channel_id=1, source_target_pairs={{0,1},{1,0},{2,3},{3,2},{4,5},{5,4},{6,7},{7,6},{8,9},{9,8},{10,11... | collective-permute-start | bytes 786440 | tf_op jit(solution)/shard_map/ppermute | solution.py:11
  33.7 5.4 %collective-permute-start.11 = (bf16[64,2048]{1,0:T(8,128)(2,1)S(1)}, bf16[64,2048]{1,0:T(8,128)(2,1)S(1)}, u32[]{:S(2)}, u32[]{:S(2)}) collective-permute-start(bf16[64,2048]{1,0:T(8,128)(2,1)S(1)} %slice.356), channel_id=1, source_target_pairs={{0,1},{1,0},{2,3},{3,2},{4,5},{5,4},{6,7},{7,6},{8,9},{9,8},{10,11... | collective-permute-start | bytes 786440 | tf_op jit(solution)/shard_map/ppermute | solution.py:11
  34.0 3.5 %collective-permute-start.8 = (f32[32]{0:T(128)S(1)}, f32[32]{0:T(128)S(1)}, u32[]{:S(2)}, u32[]{:S(2)}) collective-permute-start(f32[32]{0:T(128)S(1)} %slice.196), channel_id=1, source_target_pairs={{0,2},{1,3},{2,0},{3,1},{4,6},{5,7},{6,4},{7,5},{8,10},{9,11},{10,... | collective-permute-start | bytes 392 | tf_op jit(solution)/shard_map/ppermute | solution.py:11
  35.5 4.4 %collective-permute-start.5 = (bf16[64,2048]{1,0:T(8,128)(2,1)S(1)}, bf16[64,2048]{1,0:T(8,128)(2,1)S(1)}, u32[]{:S(2)}, u32[]{:S(2)}) collective-permute-start(bf16[64,2048]{1,0:T(8,128)(2,1)S(1)} %slice.358), channel_id=1, source_target_pairs={{0,1},{1,0},{2,3},{3,2},{4,5},{5,4},{6,7},{7,6},{8,9},{9,8},{10,11... | collective-permute-start | bytes 786440 | tf_op jit(solution)/shard_map/ppermute | solution.py:11
  37.6 6.5 %collective-permute-start.10 = (bf16[32,2048]{1,0:T(8,128)(2,1)S(1)}, bf16[32,2048]{1,0:T(8,128)(2,1)S(1)}, u32[]{:S(2)}, u32[]{:S(2)}) collective-permute-start(bf16[32,2048]{1,0:T(8,128)(2,1)S(1)} %slice.360), channel_id=1, source_target_pairs={{0,2},{1,3},{2,0},{3,1},{4,6},{5,7},{6,4},{7,5},{8,10},{9,11},{10,... | collective-permute-start | bytes 393224 | tf_op jit(solution)/shard_map/ppermute | solution.py:11
  39.3 7.3 %collective-permute-start.12 = (bf16[32,2048]{1,0:T(8,128)(2,1)S(1)}, bf16[32,2048]{1,0:T(8,128)(2,1)S(1)}, u32[]{:S(2)}, u32[]{:S(2)}) collective-permute-start(bf16[32,2048]{1,0:T(8,128)(2,1)S(1)} %slice.359), channel_id=1, source_target_pairs={{0,2},{1,3},{2,0},{3,1},{4,6},{5,7},{6,4},{7,5},{8,10},{9,11},{10,... | collective-permute-start | bytes 393224 | tf_op jit(solution)/shard_map/ppermute | solution.py:11
  40.0 8.0 %collective-permute-start.6 = (bf16[32,2048]{1,0:T(8,128)(2,1)S(1)}, bf16[32,2048]{1,0:T(8,128)(2,1)S(1)}, u32[]{:S(2)}, u32[]{:S(2)}) collective-permute-start(bf16[32,2048]{1,0:T(8,128)(2,1)S(1)} %slice.361), channel_id=1, source_target_pairs={{0,2},{1,3},{2,0},{3,1},{4,6},{5,7},{6,4},{7,5},{8,10},{9,11},{10,... | collective-permute-start | bytes 393224 | tf_op jit(solution)/shard_map/ppermute | solution.py:11
  42.6 6.9 %collective-permute-start.1 = (bf16[2,16,3,2,2048]{4,3,2,1,0:T(2,128)(2,1)S(1)}, bf16[2,16,3,2,2048]{4,3,2,1,0:T(2,128)(2,1)S(1)}, u32[]{:S(2)}, u32[]{:S(2)}) collective-permute-start(bf16[2,16,3,2,2048]{4,3,2,1,0:T(2,128)(2,1)S(1)} %pad_maximum_fusion.1), channel_id=1, source_target_pairs={{0,1},{1,0},{2,3},{3,2},{4,5},{5,4},{6,7},{7,6},{8,9},{9,8},{10,11... | collective-permute-start | bytes 2359304 | tf_op jit(solution)/shard_map/ppermute | solution.py:11
  54.2 10.3 %copy-start.3 = (s32[128]{0:T(128)S(1)}, s32[128]{0:T(128)}, u32[]{:S(2)}) copy-start(s32[128]{0:T(128)} %copy-done.2) | copy-start | bytes 1540
  56.6 17.3 %copy-start.1 = (bf16[16,1,2,2048]{3,0,2,1:T(8,128)(2,1)S(1)}, bf16[16,1,2,2048]{3,0,2,1:T(8,128)(2,1)}, u32[]{:S(2)}) copy-start(bf16[16,1,2,2048]{3,0,2,1:T(8,128)(2,1)} %maximum_bitcast_fusion.1) | copy-start | bytes 393220
  57.5 5.0 %collective-permute-start.13 = (bf16[32,2048]{1,0:T(8,128)(2,1)S(1)}, bf16[32,2048]{1,0:T(8,128)(2,1)S(1)}, u32[]{:S(2)}, u32[]{:S(2)}) collective-permute-start(bf16[32,2048]{1,0:T(8,128)(2,1)S(1)} %fusion.18), channel_id=1, source_target_pairs={{0,2},{1,3},{2,0},{3,1},{4,6},{5,7},{6,4},{7,5},{8,10},{9,11},{10,... | collective-permute-start | bytes 393224 | tf_op jit(solution)/shard_map/ppermute | solution.py:11
  62.6 1.9 %collective-permute-start.14 = (bf16[2,32,2048]{2,1,0:T(8,128)(2,1)S(1)}, bf16[2,32,2048]{2,1,0:T(8,128)(2,1)S(1)}, u32[]{:S(2)}, u32[]{:S(2)}) collective-permute-start(bf16[2,32,2048]{2,1,0:T(8,128)(2,1)S(1)} %pad_maximum_fusion.4), channel_id=1, source_target_pairs={{0,1},{1,0},{2,3},{3,2},{4,5},{5,4},{6,7},{7,6},{8,9},{9,8},{10,11... | collective-permute-start | bytes 786440 | tf_op jit(solution)/shard_map/ppermute | solution.py:11
  69.4 8.4 %collective-permute-start.15 = (bf16[32,2048]{1,0:T(8,128)(2,1)S(1)}, bf16[32,2048]{1,0:T(8,128)(2,1)S(1)}, u32[]{:S(2)}, u32[]{:S(2)}) collective-permute-start(bf16[32,2048]{1,0:T(8,128)(2,1)S(1)} %get-tuple-element.16), channel_id=1, source_target_pairs={{0,4},{4,0},{8,12},{12,8},{1,5},{5,1},{9,13},{13,9},{2,6},{6,2},{1... | collective-permute-start | bytes 393224 | tf_op jit(solution)/shard_map/ppermute | solution.py:11
  71.4 12.9 %collective-permute-start.16 = (bf16[32,2048]{1,0:T(8,128)(2,1)S(1)}, bf16[32,2048]{1,0:T(8,128)(2,1)S(1)}, u32[]{:S(2)}, u32[]{:S(2)}) collective-permute-start(bf16[32,2048]{1,0:T(8,128)(2,1)S(1)} %get-tuple-element.18), channel_id=1, source_target_pairs={{0,8},{4,12},{8,0},{12,4},{1,9},{5,13},{9,1},{13,5},{2,10},{6,14},... | collective-permute-start | bytes 393224 | tf_op jit(solution)/shard_map/ppermute | solution.py:11
  72.5 11.8 %collective-permute-start.17 = (bf16[32,2048]{1,0:T(8,128)(2,1)S(1)}, bf16[32,2048]{1,0:T(8,128)(2,1)S(1)}, u32[]{:S(2)}, u32[]{:S(2)}) collective-permute-start(bf16[32,2048]{1,0:T(8,128)(2,1)S(1)} %get-tuple-element.17), channel_id=1, source_target_pairs={{0,12},{4,8},{8,4},{12,0},{1,13},{5,9},{9,5},{13,1},{2,14},{6,10},... | collective-permute-start | bytes 393224 | tf_op jit(solution)/shard_map/ppermute | solution.py:11

commit v2 on v0

v2 whole, which is shorter than its diff:
```python
import functools

import jax
import jax.numpy as jnp
from jax import lax
from jax.experimental import pallas as pl
from jax.experimental.pallas import tpu as pltpu
from jax.sharding import PartitionSpec as P

D = 8192
F32 = jnp.float32
BF16 = jnp.bfloat16
LANES = 128


def swap(value, axis, hop):
    count = lax.axis_size(axis)
    return lax.ppermute(value, axis, [(i, i ^ hop) for i in range(count)])


def call(body, outs, args, flops=0, scalars=0):
    whole = pl.BlockSpec(memory_space=pltpu.VMEM)
    small = pl.BlockSpec(memory_space=pltpu.SMEM)
    size = sum(a.size * a.dtype.itemsize for a in (*args, *outs))
    return pl.pallas_call(
        body,
        out_shape=outs,
        in_specs=[small] * scalars + [whole] * (len(args) - scalars),
        out_specs=[whole] * len(outs),
        compiler_params=pltpu.CompilerParams(vmem_limit_bytes=12 << 20),
        cost_estimate=pl.CostEstimate(flops=flops, bytes_accessed=size, transcendentals=0),
    )(*args)


def struct(*shape, dtype=BF16):
    return jax.ShapeDtypeStruct(shape, dtype)


def tiles(width):
    step = min(width, 512)
    return [slice(at, at + step) for at in range(0, width, step)]


def iota(shape, dim):
    return lax.broadcasted_iota(jnp.int32, shape, dim)


def look(keys, table):
    hit = keys == iota((keys.shape[0], table.shape[1]), 1)
    return jnp.sum(jnp.where(hit, table.astype(F32), 0.0), axis=1, keepdims=True).astype(jnp.int32)


def index_body(n, share, steps, rows, ids, assign, picker, chooser):
    mine, place = ids[0], ids[1]
    total = n * share
    unit = steps * share
    row = iota((n * unit, 1), 0)
    rank = lax.div(row, unit)
    rel = jnp.where(rank < n // 2, 2 * rank, 2 * (rank - n // 2) + 1)
    stage = lax.rem(lax.div(row, share), steps)
    slot = (rel ^ mine) * share + lax.rem(row, share)
    wanted = jnp.where(stage == 0, look(slot, assign[1:2, :]), slot)
    spot = ((lax.div(wanted, rows) ^ place) * steps + stage) * rows + lax.rem(wanted, rows)
    hit = spot == iota((n * unit, n * unit), 1)
    picker[...] = jnp.where(hit, 1.0, 0.0).astype(BF16)
    own = iota((share, 1), 0) + mine * share
    cand = look(look(own, assign[1:2, :]), assign[0:1, :])
    rel = lax.div(cand, share) ^ mine
    rank = lax.div(rel, 2) + lax.rem(rel, 2) * (n // 2)
    hit = rank * share + lax.rem(cand, share) == iota((share, total), 1)
    chooser[...] = jnp.where(hit, 1.0, 0.0).astype(BF16)


def split3(value):
    high = value.astype(BF16).astype(F32)
    mid = (value - high).astype(BF16).astype(F32)
    low = value - high - mid
    lane = iota((value.shape[0], LANES), 1)
    return jnp.where(
        lane == 0, high, jnp.where(lane == 1, mid, jnp.where(lane == 2, low, 0.0))
    ).astype(BF16)


def join3(value):
    return jnp.sum(value.astype(F32), axis=1, keepdims=True)


def project_tile(x, weight, keep, send, half):
    for cols in tiles(weight.shape[1]):
        product = jnp.dot(x, weight[:, cols], preferred_element_type=F32)
        keep[:, cols] = product[:half]
        send[:, cols] = product[half:].astype(BF16)


def load_body(weight, *refs):
    outs, sems = refs[:-1], refs[-1]
    copies = [
        pltpu.make_async_copy(weight.at[j], out, sems.at[j]) for j, out in enumerate(outs)
    ]
    for copy in copies:
        copy.start()
    for copy in copies:
        copy.wait()


def load(weight):
    one = struct(*weight.shape[1:])
    size = 2 * weight.size * weight.dtype.itemsize
    return pl.pallas_call(
        load_body,
        out_shape=[one] * 3,
        in_specs=[pl.BlockSpec(memory_space=pltpu.HBM)],
        out_specs=[pl.BlockSpec(memory_space=pltpu.VMEM)] * 3,
        scratch_shapes=[pltpu.SemaphoreType.DMA((3,))],
        compiler_params=pltpu.CompilerParams(vmem_limit_bytes=12 << 20),
        cost_estimate=pl.CostEstimate(flops=0, bytes_accessed=size, transcendentals=0),
    )(weight)


def first_body(half, count, picker, gain, weight, *refs):
    blocks, (scaled, keep, send, squares) = refs[:count], refs[count:]
    x = jnp.concatenate([block[...] for block in blocks]) if count > 1 else blocks[0][...]
    total = jnp.zeros((x.shape[0], 1), F32)
    for cols in tiles(x.shape[1]):
        ordered = jnp.dot(picker[...], x[:, cols], preferred_element_type=F32)
        total = total + jnp.sum(ordered * ordered, axis=1, keepdims=True)
        scaled[:, cols] = (ordered * gain[:, cols]).astype(BF16)
    width = weight.shape[1]
    project_tile(scaled[...], weight, keep, send, half)
    squares[...] = jnp.broadcast_to(total[:half], squares.shape)
    send[:, width:] = split3(total[half:])


def next_body(half, scaled, weight, keep, send):
    project_tile(scaled[...], weight, keep, send, half)


def add_body(unit, with_squares, *refs):
    if with_squares:
        keep, got, squares, own, send, own_squares = refs
    else:
        keep, got, own, send = refs
    width = keep.shape[1]
    for cols in tiles(width):
        own[:, cols] = keep[:unit, cols] + got[:unit, cols].astype(F32)
        send[:, cols] = (keep[unit:, cols] + got[unit:, cols].astype(F32)).astype(BF16)
    if with_squares:
        total = squares[:, :1] + join3(got[:, width:])
        own_squares[...] = jnp.broadcast_to(total[:unit], own_squares.shape)
        send[:, width:] = split3(total[unit:])


def past_body(chooser, conv, near, far, older, newer):
    share = older.shape[1]
    blocks = near.shape[0]
    for j in range(3):
        for cols in tiles(older.shape[2]):
            sums = []
            for k in range(2):
                pool = jnp.concatenate(
                    [near[b, j, k, :, cols] for b in range(blocks)]
                    + [far[b, j, k, :, cols] for b in range(blocks)]
                )
                sums.append(jnp.dot(chooser[...], pool, preferred_element_type=F32))
            first = conv[0, j : j + 1, cols]
            older[j, :, cols] = first * sums[0] + conv[1, j : j + 1, cols] * sums[1]
            newer[j, :, cols] = first * sums[1]


def mix_body(share, peers, conv, older, newer, squares, *refs):
    owns, gots = refs[:3], refs[3 : 3 + 3 * peers]
    gated, fresh = refs[3 + 3 * peers :]
    width = gated.shape[1]
    total = squares[:, :1]
    for p in range(peers):
        total = total + join3(gots[p][:, width:])
    scale = lax.rsqrt(total / D + 1e-05)
    for cols in tiles(width):
        gate = None
        for j in range(3):
            new = owns[j][:, cols]
            for p in range(peers):
                new = new + gots[j * peers + p][:, cols].astype(F32)
            new = (new * scale).astype(BF16)
            new0, new1 = new[:share], new[share:]
            fresh[j, 0, :, cols] = new0
            fresh[j, 1, :, cols] = new1
            new0, new1 = new0.astype(F32), new1.astype(F32)
            last = conv[2, j : j + 1, cols]
            mixed0 = older[j, :, cols] + last * new0
            mixed1 = newer[j, :, cols] + conv[1, j : j + 1, cols] * new0 + last * new1
            mixed = jnp.concatenate([mixed0, mixed1])
            gate = mixed if gate is None else gate * mixed
        gated[:, cols] = gate.astype(BF16)


def out_body(block, picker, near, far, weight, own, *rest):
    rows = near.shape[0] * near.shape[1]
    every = jnp.concatenate(
        [near[b] for b in range(near.shape[0])] + [far[b] for b in range(far.shape[0])]
    )
    lined = lax.dot_general(
        picker[...], every, (((0,), (0,)), ((), ())), preferred_element_type=F32
    ).astype(BF16)
    for cols in tiles(weight.shape[1]):
        product = jnp.dot(lined, weight[:, cols], preferred_element_type=F32)
        own[:, cols] = product[:block].astype(own.dtype)
        for k, ref in enumerate(rest, 1):
            ref[:, cols] = product[k * block : (k + 1) * block].astype(BF16)


def shards(tokens, assign, state, norm_gain, in_weight, conv_weight, out_weight):
    n = lax.axis_size("narrow")
    wide = lax.axis_size("wide")
    steps, rows, feats = tokens.shape
    share = state.shape[0]
    chans = in_weight.shape[2]
    outs = out_weight.shape[1]
    direct = wide <= 4
    mine = lax.axis_index("narrow")
    place = lax.axis_index("wide") if direct else 0
    evens = [2 * k for k in range(n // 2)]
    unit = steps * share
    half = (n // 2) * unit
    peers = n // 2 - 1
    block = steps * rows

    mine_tokens = tokens.reshape(block, feats)
    if direct:
        blocks = [mine_tokens] + [swap(mine_tokens, "wide", k) for k in range(1, wide)]
    else:
        blocks = [lax.all_gather(mine_tokens, "wide", axis=0, tiled=True)]

    past = state.transpose(2, 1, 0, 3)
    near = jnp.stack([past] + [swap(past, "narrow", k) for k in evens[1:]])
    far = swap(near, "narrow", 1)

    ids = jnp.stack([mine, place]).astype(jnp.int32)
    picker, chooser = call(
        functools.partial(index_body, n, share, steps, rows),
        [struct(n * unit, n * unit), struct(share, n * share)],
        [ids, assign],
        scalars=1,
    )
    weights = load(in_weight.transpose(1, 0, 2))
    cost = 2 * n * unit * feats * chans
    keeps, sends = [None] * 3, [None] * 3
    scaled, keeps[0], sends[0], squares = call(
        functools.partial(first_body, half, len(blocks)),
        [
            struct(n * unit, feats),
            struct(half, chans, dtype=F32),
            struct(half, chans + LANES),
            struct(half, LANES, dtype=F32),
        ],
        [picker, norm_gain.reshape(1, feats), weights[0], *blocks],
        flops=cost,
    )
    for j in (1, 2):
        keeps[j], sends[j] = call(
            functools.partial(next_body, half),
            [struct(half, chans, dtype=F32), struct(half, chans)],
            [scaled, weights[j]],
            flops=cost,
        )
    owns, gots = [None] * 3, []
    for j in range(3):
        got = swap(sends[j], "narrow", 1)
        extra = LANES if j == 0 else 0
        shapes = [struct(unit, chans, dtype=F32), struct(half - unit, chans + extra)]
        args = [keeps[j], got]
        if j == 0:
            shapes.append(struct(unit, LANES, dtype=F32))
            args.append(squares)
        result = call(functools.partial(add_body, unit, j == 0), shapes, args)
        owns[j] = result[0]
        if j == 0:
            squares = result[2]
        for p, k in enumerate(evens[1:]):
            gots.append(swap(result[1][p * unit : (p + 1) * unit], "narrow", k))
    older, newer = call(
        past_body,
        [struct(3, share, chans, dtype=F32)] * 2,
        [chooser, conv_weight, near, far],
        flops=2 * share * n * share * 6 * chans,
    )
    gated, fresh = call(
        functools.partial(mix_body, share, peers),
        [struct(unit, chans), struct(3, 2, share, chans)],
        [conv_weight, older, newer, squares, *owns, *gots],
    )
    memory = fresh.transpose(2, 1, 0, 3)

    near = jnp.stack([gated] + [swap(gated, "narrow", k) for k in evens[1:]])
    far = swap(near, "narrow", 1)
    cost = 2 * n * unit * chans * outs
    if direct:
        own, *rest = call(
            functools.partial(out_body, block),
            [struct(block, outs, dtype=F32)] + [struct(block, outs)] * (wide - 1),
            [picker, near, far, out_weight],
            flops=cost,
        )
        for k in range(1, wide):
            own = own + swap(rest[k - 1], "wide", k).astype(F32)
        out = own.astype(BF16)
    else:
        (partial,) = call(
            functools.partial(out_body, n * unit),
            [struct(n * unit, outs)],
            [picker, near, far, out_weight],
            flops=cost,
        )
        out = lax.psum_scatter(partial, "wide", scatter_dimension=0, tiled=True)
    return (out.reshape(steps, rows, outs), memory)


def solution(mesh):
    in_specs = (
        P(None, ("groups", "wide"), "narrow"),
        P(None, "groups"),
        P(("groups", "narrow"), None, None, "wide"),
        P("narrow"),
        P("narrow", None, "wide"),
        P(None, None, "wide"),
        P("wide", "narrow"),
    )
    out_specs = (P(None, ("groups", "wide"), "narrow"), P(("groups", "narrow"), None, None, "wide"))
    return jax.shard_map(shards, mesh=mesh, in_specs=in_specs, out_specs=out_specs, check_vma=False)
```

time: 236 us -> 60.4 us (0.26)
  waiting for transfers between devices: 83.8 us -> 24.8 us
  blocking collectives: 48.5 us -> 0 us
  local copies, waits for them, and re-layouts: 43 us -> 2.29 us
  matrix products: 38.4 us -> 0 us
  starting transfers between devices: 0.24 us -> 16.1 us
  Pallas kernels: 0 us -> 15.4 us
  between operations: 14.3 us -> 0.79 us
  other arithmetic: 6.65 us -> 0.91 us
    reduce_scatter x4 -> x0, waiting for transfers between devices: 47.2 us -> none  [the longest x2 26.7 us: shards(): lax.psum_scatter(partial_out.astype(jnp.bfloat16), 'wide', scatter_dimens...]
    all_gather x4 -> x0, blocking collectives: 40.2 us -> none  [the longest x2 28.3 us: shards(): gathered = lax.all_gather(normed, 'wide', axis=0, tiled=True)]
    dot_general x4 -> x0, matrix products: 38.4 us -> none  [the longest x2 27 us: shards(): jnp.dot(gathered, flat_in, preferred_element_type=jnp.float32)]
    all_gather x2 -> x0, waiting for transfers between devices: 35.8 us -> none  [shards(): piece = lax.all_gather(memory, 'narrow', axis=0, tiled=True)]
    unnamed x8 -> x14, local copies, waits for them, and re-layouts: 34.5 us -> 2.29 us
    ppermute x0 -> x16, waiting for transfers between devices: none -> 24.8 us  [swap(): return lax.ppermute(value, axis, [(i, i ^ hop) for i in range(count)])]
    ppermute x0 -> x16, starting transfers between devices: none -> 16.1 us  [swap(): return lax.ppermute(value, axis, [(i, i ^ hop) for i in range(count)])]
    pallas_call x0 -> x11, Pallas kernels: none -> 15.4 us  [the longest x1 8.22 us: load(): pl.pallas_call(load_body, out_shape=[one] * 3, in_specs=[pl.BlockSpec(mem...]
  transfers between devices with their start and end apart: 6 -> 16, of which waited for: 5 -> 7; matrix products, arithmetic and copies ran while one was open for 12% -> 2% of each run, Pallas kernels for 0% -> 23%
where the time goes in v2:
time: 60.4 us; the launch traced here: 60.2 us
  waiting for transfers between devices  24.8 us (41%)
  starting transfers between devices  16.1 us (27%)
  Pallas kernels  15.4 us (25%)
  local copies, waits for them, and re-layouts  2.29 us (4%)
  other arithmetic  0.91 us (2%)
  between operations  0.79 us (1%)
    ppermute x16, waiting for transfers between devices, swap(): return lax.ppermute(value, axis, [(i, i ^ hop) for i in range(count)])  24.8 us
    ppermute x16, starting transfers between devices, swap(): return lax.ppermute(value, axis, [(i, i ^ hop) for i in range(count)])  16.1 us
    pallas_call x1, Pallas kernels, load(): pl.pallas_call(load_body, out_shape=[one] * 3, in_specs=[pl.BlockSpec(mem...  8.22 us
    pallas_call x10, Pallas kernels, call(): pl.pallas_call(body, out_shape=outs, in_specs=[small] * scalars + [whole]...  7.17 us
    unnamed x14, local copies, waits for them, and re-layouts  2.29 us
  transfers between devices with their start and end apart: 16, of which 7 were waited for; matrix products, arithmetic and copies ran while one was open for 2% of the time, Pallas kernels for 23%

profile of v2, /device:TPU:0, one launch (start us, length us, event | category | flops | bytes accessed | tf_op | source)
XLA Modules:
  0.0 60.2 jit_solution(16919778086466792225)
XLA Ops:
  0.6 1.1 %copy.13 = bf16[16,2,3,2048]{3,0,1,2:T(8,128)(2,1)S(1)} copy(bf16[16,2,3,2048]{3,1,2,0:T(2,128)(2,1)} %param.9) | data formatting | bytes 786432 | tf_op args[2]
  1.7 3.0 %collective-permute-start = (bf16[3,2,16,2048]{3,2,1,0:T(8,128)(2,1)S(1)}, bf16[3,2,16,2048]{3,2,1,0:T(8,128)(2,1)S(1)}, u32[]{:S(2)}, u32[]{:S(2)}) collective-permute-start(bf16[3,2,16,2048]{3,2,1,0:T(8,128)(2,1)S(1)} %bitcast.26), channel_id=1, source_target_pairs={{0,2},{1,3},{2,0},{3,1},{4,6},{5,7},{6,4},{7,5},{8,10},{9,11},{10,... | collective-permute-start | bytes 1179656 | tf_op jit(solution)/shard_map/ppermute | solution.py:18
  4.8 1.6 %collective-permute-start.2 = (bf16[32,2048]{1,0:T(8,128)(2,1)}, bf16[32,2048]{1,0:T(8,128)(2,1)S(1)}, u32[]{:S(2)}, u32[]{:S(2)}) collective-permute-start(bf16[32,2048]{1,0:T(8,128)(2,1)} %bitcast.19), channel_id=1, source_target_pairs={{0,4},{4,0},{8,12},{12,8},{1,5},{5,1},{9,13},{13,9},{2,6},{6,2},{1... | collective-permute-start | bytes 393224 | tf_op jit(solution)/shard_map/ppermute | solution.py:18
  6.3 2.6 %collective-permute-start.3 = (bf16[32,2048]{1,0:T(8,128)(2,1)}, bf16[32,2048]{1,0:T(8,128)(2,1)S(1)}, u32[]{:S(2)}, u32[]{:S(2)}) collective-permute-start(bf16[32,2048]{1,0:T(8,128)(2,1)} %bitcast.20), channel_id=1, source_target_pairs={{0,8},{4,12},{8,0},{12,4},{1,9},{5,13},{9,1},{13,5},{2,10},{6,14},... | collective-permute-start | bytes 393224 | tf_op jit(solution)/shard_map/ppermute | solution.py:18
  8.9 0.2 collective-permute-start.4
  9.1 0.0 copy-start.3
  9.1 0.0 copy-start.1
  9.1 0.0 copy-start.2
  9.1 8.2 %shard_map.88 = (bf16[2048,2048]{1,0:T(8,128)(2,1)S(1)}, bf16[2048,2048]{1,0:T(8,128)(2,1)S(1)}, bf16[2048,2048]{1,0:T(8,128)(2,1)S(1)}) custom-call(bf16[3,2048,2048]{2,1,0:T(8,128)(2,1)} %bitcast.25), custom_call_target="tpu_custom_call" | custom-call | bytes 50331648 | tf_op jit(solution)/shard_map/pallas_call | solution.py:109
  17.4 0.0 collective-permute-done
  17.4 0.1 pad_maximum_fusion.near
  17.5 0.1 collective-permute-start.1
  17.5 0.1 pad_add_fusion.ids
  17.6 0.0 copy-done.3
  17.6 0.7 %shard_map.86 = (bf16[128,128]{1,0:T(8,128)(2,1)S(1)}, bf16[16,64]{1,0:T(8,128)(2,1)S(1)}) custom-call(s32[2]{0:T(128)S(1)} %pad_add_fusion.ids, s32[2,64]{1,0:T(2,128)S(1)} %copy-done.3), custom_call_target="tpu_custom_call" | custom-call | bytes 35336 | tf_op jit(solution)/shard_map/pallas_call | solution.py:25
  18.4 0.0 collective-permute-done.2.refs_1_
  18.4 0.8 %collective-permute-done.3.refs_2_ = bf16[32,2048]{1,0:T(8,128)(2,1)S(1)} collective-permute-done((bf16[32,2048]{1,0:T(8,128)(2,1)}, bf16[32,2048]{1,0:T(8,128)(2,1)S(1)}, u32[]{:S(2)}, u32[]{:S(2)}) %collective-permute-start.3) | collective-permute-done | bytes 131104 | tf_op jit(solution)/shard_map/ppermute | solution.py:18
  19.2 0.0 collective-permute-done.4.refs_3_
  19.2 0.0 copy-done.1
  19.2 0.0 copy-done.2
  19.2 1.4 %shard_map.89 = (bf16[128,2048]{1,0:T(8,128)(2,1)S(1)}, f32[64,2048]{1,0:T(8,128)S(1)}, bf16[64,2176]{1,0:T(8,128)(2,1)S(1)}, f32[64,128]{1,0:T(8,128)S(1)}) custom-call(bf16[128,128]{1,0:T(8,128)(2,1)S(1)} %get-tuple-element.30.picker, f32[1,2048]{1,0:T(1,128)S(1)} %bitcast.24, bf16[2048,2048]{1,0:T(8,128)(2,1)S(1)} %get-tuple-element.34.weight, ...), custom_call_target="tpu_custom_call" | custom-call | flops 1073741824 | bytes 10313728 | tf_op jit(solution)/shard_map/pallas_call | solution.py:25
  20.7 0.1 collective-permute-start.5
  20.7 0.0 copy-start
  20.8 1.3 %shard_map.93 = (f32[64,2048]{1,0:T(8,128)S(1)}, bf16[64,2048]{1,0:T(8,128)(2,1)S(1)}) custom-call(bf16[128,2048]{1,0:T(8,128)(2,1)S(1)} %get-tuple-element.40.scaled, bf16[2048,2048]{1,0:T(8,128)(2,1)S(1)} %get-tuple-element.45.weight), custom_call_target="tpu_custom_call" | custom-call | flops 1073741824 | bytes 9699328 | tf_op jit(solution)/shard_map/pallas_call | solution.py:25
  22.1 0.0 slice-start
  22.1 0.6 collective-permute-start.7
  22.6 0.0 slice-start.1
  22.6 1.3 %shard_map.91 = (f32[64,2048]{1,0:T(8,128)S(1)}, bf16[64,2048]{1,0:T(8,128)(2,1)S(1)}) custom-call(bf16[128,2048]{1,0:T(8,128)(2,1)S(1)} %get-tuple-element.40.scaled, bf16[2048,2048]{1,0:T(8,128)(2,1)S(1)} %get-tuple-element.41.weight), custom_call_target="tpu_custom_call" | custom-call | flops 1073741824 | bytes 9699328 | tf_op jit(solution)/shard_map/pallas_call | solution.py:25
  23.9 0.1 collective-permute-start.6
  24.0 0.0 collective-permute-done.5.refs_1_
  24.0 0.2 shard_map.90
  24.2 0.6 collective-permute-start.8
  24.8 0.0 collective-permute-done.7.refs_1_
  24.8 0.1 shard_map.94
  24.9 1.6 %collective-permute-start.10 = (bf16[32,2048]{1,0:T(8,128)(2,1)S(1)}, bf16[32,2048]{1,0:T(8,128)(2,1)S(1)}, u32[]{:S(2)}, u32[]{:S(2)}) collective-permute-start(bf16[32,2048]{1,0:T(8,128)(2,1)S(1)} %get-tuple-element.51), channel_id=1, source_target_pairs={{0,2},{1,3},{2,0},{3,1},{4,6},{5,7},{6,4},{7,5},{8,10},{9,11},{10,... | collective-permute-start | bytes 393224 | tf_op jit(solution)/shard_map/ppermute | solution.py:18
  26.4 0.0 collective-permute-done.6.refs_1_
  26.4 0.1 shard_map.92
  26.5 0.6 collective-permute-start.9
  27.1 0.0 collective-permute-done.1.far
  27.1 0.0 copy-done
  27.1 0.3 shard_map.87
  27.4 6.1 %collective-permute-done.10.refs_5_ = bf16[32,2048]{1,0:T(8,128)(2,1)S(1)} collective-permute-done((bf16[32,2048]{1,0:T(8,128)(2,1)S(1)}, bf16[32,2048]{1,0:T(8,128)(2,1)S(1)}, u32[]{:S(2)}, u32[]{:S(2)}) %collective-permute-start.10) | collective-permute-done | bytes 131104 | tf_op jit(solution)/shard_map/ppermute | solution.py:18
  33.5 2.4 %collective-permute-done.9.refs_4_ = bf16[32,2048]{1,0:T(8,128)(2,1)S(1)} collective-permute-done((bf16[32,2048]{1,0:T(8,128)(2,1)S(1)}, bf16[32,2048]{1,0:T(8,128)(2,1)S(1)}, u32[]{:S(2)}, u32[]{:S(2)}) %collective-permute-start.9) | collective-permute-done | bytes 131104 | tf_op jit(solution)/shard_map/ppermute | solution.py:18
  35.9 0.0 collective-permute-done.8.refs_3_
  36.0 0.4 shard_map.95
  36.3 0.6 collective-permute-start.11
  36.9 4.6 %collective-permute-done.11 = bf16[32,2048]{1,0:T(8,128)(2,1)S(1)} collective-permute-done((bf16[32,2048]{1,0:T(8,128)(2,1)S(1)}, bf16[32,2048]{1,0:T(8,128)(2,1)S(1)}, u32[]{:S(2)}, u32[]{:S(2)}) %collective-permute-start.11) | collective-permute-done | bytes 131104 | tf_op jit(solution)/shard_map/ppermute | solution.py:18
  41.6 0.1 collective-permute-start.12
  41.6 1.5 %collective-permute-done.12.far = bf16[2,32,2048]{2,1,0:T(8,128)(2,1)S(1)} collective-permute-done((bf16[2,32,2048]{2,1,0:T(8,128)(2,1)S(1)}, bf16[2,32,2048]{2,1,0:T(8,128)(2,1)S(1)}, u32[]{:S(2)}, u32[]{:S(2)}) %collective-permute-start.12) | collective-permute-done | bytes 262176 | tf_op jit(solution)/shard_map/ppermute | solution.py:18
  43.2 0.0 slice-done
  43.2 0.0 slice-done.1
  43.2 1.4 %shard_map.96 = (f32[32,2048]{1,0:T(8,128)S(1)}, bf16[32,2048]{1,0:T(8,128)(2,1)S(1)}, bf16[32,2048]{1,0:T(8,128)(2,1)S(1)}, bf16[32,2048]{1,0:T(8,128)(2,1)S(1)}) custom-call(bf16[128,128]{1,0:T(8,128)(2,1)S(1)} %get-tuple-element.30.picker, bf16[2,32,2048]{2,1,0:T(8,128)(2,1)S(1)} %pad_maximum_fusion.1.near, ...), custom_call_target="tpu_custom_call" | custom-call | flops 1073741824 | bytes 9601024 | tf_op jit(solution)/shard_map/pallas_call | solution.py:25
  44.6 2.0 %collective-permute-start.13 = (bf16[32,2048]{1,0:T(8,128)(2,1)S(1)}, bf16[32,2048]{1,0:T(8,128)(2,1)S(1)}, u32[]{:S(2)}, u32[]{:S(2)}) collective-permute-start(bf16[32,2048]{1,0:T(8,128)(2,1)S(1)} %get-tuple-element.54), channel_id=1, source_target_pairs={{0,4},{4,0},{8,12},{12,8},{1,5},{5,1},{9,13},{13,9},{2,6},{6,2},{1... | collective-permute-start | bytes 393224 | tf_op jit(solution)/shard_map/ppermute | solution.py:18
  46.6 1.3 %collective-permute-start.14 = (bf16[32,2048]{1,0:T(8,128)(2,1)S(1)}, bf16[32,2048]{1,0:T(8,128)(2,1)S(1)}, u32[]{:S(2)}, u32[]{:S(2)}) collective-permute-start(bf16[32,2048]{1,0:T(8,128)(2,1)S(1)} %get-tuple-element.55), channel_id=1, source_target_pairs={{0,8},{4,12},{8,0},{12,4},{1,9},{5,13},{9,1},{13,5},{2,10},{6,14},... | collective-permute-start | bytes 393224 | tf_op jit(solution)/shard_map/ppermute | solution.py:18
  47.9 1.2 %collective-permute-start.15 = (bf16[32,2048]{1,0:T(8,128)(2,1)S(1)}, bf16[32,2048]{1,0:T(8,128)(2,1)S(1)}, u32[]{:S(2)}, u32[]{:S(2)}) collective-permute-start(bf16[32,2048]{1,0:T(8,128)(2,1)S(1)} %get-tuple-element.56), channel_id=1, source_target_pairs={{0,12},{4,8},{8,4},{12,0},{1,13},{5,9},{9,5},{13,1},{2,14},{6,10},... | collective-permute-start | bytes 393224 | tf_op jit(solution)/shard_map/ppermute | solution.py:18
  49.1 1.1 %copy.10 = bf16[16,2,3,2048]{3,1,2,0:T(2,128)(2,1)} copy(bf16[16,2,3,2048]{3,0,1,2:T(8,128)(2,1)S(1)} %bitcast.18) | data formatting | bytes 786432
  50.2 2.1 %collective-permute-done.13 = bf16[32,2048]{1,0:T(8,128)(2,1)S(1)} collective-permute-done((bf16[32,2048]{1,0:T(8,128)(2,1)S(1)}, bf16[32,2048]{1,0:T(8,128)(2,1)S(1)}, u32[]{:S(2)}, u32[]{:S(2)}) %collective-permute-start.13) | collective-permute-done | bytes 131104 | tf_op jit(solution)/shard_map/ppermute | solution.py:18
  52.3 7.2 %collective-permute-done.14 = bf16[32,2048]{1,0:T(8,128)(2,1)S(1)} collective-permute-done((bf16[32,2048]{1,0:T(8,128)(2,1)S(1)}, bf16[32,2048]{1,0:T(8,128)(2,1)S(1)}, u32[]{:S(2)}, u32[]{:S(2)}) %collective-permute-start.14) | collective-permute-done | bytes 131104 | tf_op jit(solution)/shard_map/ppermute | solution.py:18
  59.5 0.0 collective-permute-done.15
  59.5 0.7 %add_convert_fusion = bf16[32,2048]{1,0:T(8,128)(2,1)} fusion(bf16[32,2048]{1,0:T(8,128)(2,1)S(1)} %collective-permute-done.15, bf16[32,2048]{1,0:T(8,128)(2,1)S(1)} %collective-permute-done.14, f32[32,2048]{1,0:T(8,128)S(1)} %get-tuple-element.53, bf16[32,2048]{1,0:T(8,128)(2,1)S(1)} %collective-permute-done.13), kind=kLoop, calls=%fused_computation.4 | loop fusion | flops 458752 | bytes 786432 | tf_op jit(solution)/shard_map/convert_element_type | solution.py:306
  (2 shorter events, 0.0 us)
Async XLA Ops:
  1.7 15.6 %collective-permute-start = (bf16[3,2,16,2048]{3,2,1,0:T(8,128)(2,1)S(1)}, bf16[3,2,16,2048]{3,2,1,0:T(8,128)(2,1)S(1)}, u32[]{:S(2)}, u32[]{:S(2)}) collective-permute-start(bf16[3,2,16,2048]{3,2,1,0:T(8,128)(2,1)S(1)} %bitcast.26), channel_id=1, source_target_pairs={{0,2},{1,3},{2,0},{3,1},{4,6},{5,7},{6,4},{7,5},{8,10},{9,11},{10,... | collective-permute-start | bytes 1179656 | tf_op jit(solution)/shard_map/ppermute | solution.py:18
  4.8 13.6 %collective-permute-start.2 = (bf16[32,2048]{1,0:T(8,128)(2,1)}, bf16[32,2048]{1,0:T(8,128)(2,1)S(1)}, u32[]{:S(2)}, u32[]{:S(2)}) collective-permute-start(bf16[32,2048]{1,0:T(8,128)(2,1)} %bitcast.19), channel_id=1, source_target_pairs={{0,4},{4,0},{8,12},{12,8},{1,5},{5,1},{9,13},{13,9},{2,6},{6,2},{1... | collective-permute-start | bytes 393224 | tf_op jit(solution)/shard_map/ppermute | solution.py:18
  6.3 12.9 %collective-permute-start.3 = (bf16[32,2048]{1,0:T(8,128)(2,1)}, bf16[32,2048]{1,0:T(8,128)(2,1)S(1)}, u32[]{:S(2)}, u32[]{:S(2)}) collective-permute-start(bf16[32,2048]{1,0:T(8,128)(2,1)} %bitcast.20), channel_id=1, source_target_pairs={{0,8},{4,12},{8,0},{12,4},{1,9},{5,13},{9,1},{13,5},{2,10},{6,14},... | collective-permute-start | bytes 393224 | tf_op jit(solution)/shard_map/ppermute | solution.py:18
  8.9 10.3 %collective-permute-start.4 = (bf16[32,2048]{1,0:T(8,128)(2,1)}, bf16[32,2048]{1,0:T(8,128)(2,1)S(1)}, u32[]{:S(2)}, u32[]{:S(2)}) collective-permute-start(bf16[32,2048]{1,0:T(8,128)(2,1)} %bitcast.21), channel_id=1, source_target_pairs={{0,12},{4,8},{8,4},{12,0},{1,13},{5,9},{9,5},{13,1},{2,14},{6,10},... | collective-permute-start | bytes 393224 | tf_op jit(solution)/shard_map/ppermute | solution.py:18
  9.1 8.5 %copy-start.3 = (s32[2,64]{1,0:T(2,128)S(1)}, s32[2,64]{1,0:T(2,128)}, u32[]{:S(2)}) copy-start(s32[2,64]{1,0:T(2,128)} %assign.1) | copy-start | bytes 1540
  9.1 10.1 %copy-start.1 = (bf16[2,16,2048]{2,1,0:T(8,128)(2,1)S(1)}, bf16[2,16,2048]{2,1,0:T(8,128)(2,1)}, u32[]{:S(2)}) copy-start(bf16[2,16,2048]{2,1,0:T(8,128)(2,1)} %param.7) | copy-start | bytes 393220
  9.1 10.1 %copy-start.2 = (f32[2048]{0:T(1024)S(1)}, f32[2048]{0:T(1024)}, u32[]{:S(2)}) copy-start(f32[2048]{0:T(1024)} %param.10) | copy-start | bytes 24580
  17.5 9.6 %collective-permute-start.1 = (bf16[2,3,2,16,2048]{4,3,2,1,0:T(8,128)(2,1)S(1)}, bf16[2,3,2,16,2048]{4,3,2,1,0:T(8,128)(2,1)S(1)}, u32[]{:S(2)}, u32[]{:S(2)}) collective-permute-start(bf16[2,3,2,16,2048]{4,3,2,1,0:T(8,128)(2,1)S(1)} %pad_maximum_fusion.near), channel_id=1, source_target_pairs={{0,1},{1,0},{2,3},{3,2},{4,5},{5,4},{6,7},{7,6},{8,9},{9,8},{10,11... | collective-permute-start | bytes 2359304 | tf_op jit(solution)/shard_map/ppermute | solution.py:18
  20.7 3.3 %collective-permute-start.5 = (bf16[64,2176]{1,0:T(8,128)(2,1)S(1)}, bf16[64,2176]{1,0:T(8,128)(2,1)S(1)}, u32[]{:S(2)}, u32[]{:S(2)}) collective-permute-start(bf16[64,2176]{1,0:T(8,128)(2,1)S(1)} %get-tuple-element.36), channel_id=1, source_target_pairs={{0,1},{1,0},{2,3},{3,2},{4,5},{5,4},{6,7},{7,6},{8,9},{9,8},{10,11... | collective-permute-start | bytes 835592 | tf_op jit(solution)/shard_map/ppermute | solution.py:18
  20.7 6.3 %copy-start = (f32[3,3,2048]{2,1,0:T(4,128)S(1)}, f32[3,3,2048]{2,1,0:T(4,128)}, u32[]{:S(2)}) copy-start(f32[3,3,2048]{2,1,0:T(4,128)} %conv.3) | copy-start | bytes 221188
  22.1 21.1 %slice-start = ((s8[8388608]{0:T(1024)(128)(4,1)}), s8[4194304]{0:T(1024)(128)(4,1)S(1)}, s32[]{:S(2)}) async-start(s8[8388608]{0:T(1024)(128)(4,1)} %bitcast.16), calls=%async_computation | async-start | bytes 8388608
  22.1 2.7 %collective-permute-start.7 = (bf16[64,2048]{1,0:T(8,128)(2,1)S(1)}, bf16[64,2048]{1,0:T(8,128)(2,1)S(1)}, u32[]{:S(2)}, u32[]{:S(2)}) collective-permute-start(bf16[64,2048]{1,0:T(8,128)(2,1)S(1)} %get-tuple-element.47), channel_id=1, source_target_pairs={{0,1},{1,0},{2,3},{3,2},{4,5},{5,4},{6,7},{7,6},{8,9},{9,8},{10,11... | collective-permute-start | bytes 786440 | tf_op jit(solution)/shard_map/ppermute | solution.py:18
  22.6 20.5 %slice-start.1 = ((s8[8388608]{0:T(1024)(128)(4,1)}), s8[4194304]{0:T(1024)(128)(4,1)S(1)}, s32[]{:S(2)}) async-start(s8[8388608]{0:T(1024)(128)(4,1)} %bitcast.16), calls=%async_computation.1 | async-start | bytes 8388608
  23.9 2.5 %collective-permute-start.6 = (bf16[64,2048]{1,0:T(8,128)(2,1)S(1)}, bf16[64,2048]{1,0:T(8,128)(2,1)S(1)}, u32[]{:S(2)}, u32[]{:S(2)}) collective-permute-start(bf16[64,2048]{1,0:T(8,128)(2,1)S(1)} %get-tuple-element.43), channel_id=1, source_target_pairs={{0,1},{1,0},{2,3},{3,2},{4,5},{5,4},{6,7},{7,6},{8,9},{9,8},{10,11... | collective-permute-start | bytes 786440 | tf_op jit(solution)/shard_map/ppermute | solution.py:18
  24.2 11.8 %collective-permute-start.8 = (bf16[32,2176]{1,0:T(8,128)(2,1)S(1)}, bf16[32,2176]{1,0:T(8,128)(2,1)S(1)}, u32[]{:S(2)}, u32[]{:S(2)}) collective-permute-start(bf16[32,2176]{1,0:T(8,128)(2,1)S(1)} %get-tuple-element.49), channel_id=1, source_target_pairs={{0,2},{1,3},{2,0},{3,1},{4,6},{5,7},{6,4},{7,5},{8,10},{9,11},{10,... | collective-permute-start | bytes 417800 | tf_op jit(solution)/shard_map/ppermute | solution.py:18
  24.9 8.7 %collective-permute-start.10 = (bf16[32,2048]{1,0:T(8,128)(2,1)S(1)}, bf16[32,2048]{1,0:T(8,128)(2,1)S(1)}, u32[]{:S(2)}, u32[]{:S(2)}) collective-permute-start(bf16[32,2048]{1,0:T(8,128)(2,1)S(1)} %get-tuple-element.51), channel_id=1, source_target_pairs={{0,2},{1,3},{2,0},{3,1},{4,6},{5,7},{6,4},{7,5},{8,10},{9,11},{10,... | collective-permute-start | bytes 393224 | tf_op jit(solution)/shard_map/ppermute | solution.py:18
  26.5 9.5 %collective-permute-start.9 = (bf16[32,2048]{1,0:T(8,128)(2,1)S(1)}, bf16[32,2048]{1,0:T(8,128)(2,1)S(1)}, u32[]{:S(2)}, u32[]{:S(2)}) collective-permute-start(bf16[32,2048]{1,0:T(8,128)(2,1)S(1)} %get-tuple-element.50), channel_id=1, source_target_pairs={{0,2},{1,3},{2,0},{3,1},{4,6},{5,7},{6,4},{7,5},{8,10},{9,11},{10,... | collective-permute-start | bytes 393224 | tf_op jit(solution)/shard_map/ppermute | solution.py:18
  36.3 5.2 %collective-permute-start.11 = (bf16[32,2048]{1,0:T(8,128)(2,1)S(1)}, bf16[32,2048]{1,0:T(8,128)(2,1)S(1)}, u32[]{:S(2)}, u32[]{:S(2)}) collective-permute-start(bf16[32,2048]{1,0:T(8,128)(2,1)S(1)} %get-tuple-element.52), channel_id=1, source_target_pairs={{0,2},{1,3},{2,0},{3,1},{4,6},{5,7},{6,4},{7,5},{8,10},{9,11},{10,... | collective-permute-start | bytes 393224 | tf_op jit(solution)/shard_map/ppermute | solution.py:18
  41.6 1.6 %collective-permute-start.12 = (bf16[2,32,2048]{2,1,0:T(8,128)(2,1)S(1)}, bf16[2,32,2048]{2,1,0:T(8,128)(2,1)S(1)}, u32[]{:S(2)}, u32[]{:S(2)}) collective-permute-start(bf16[2,32,2048]{2,1,0:T(8,128)(2,1)S(1)} %pad_maximum_fusion.1.near), channel_id=1, source_target_pairs={{0,1},{1,0},{2,3},{3,2},{4,5},{5,4},{6,7},{7,6},{8,9},{9,8},{10,11... | collective-permute-start | bytes 786440 | tf_op jit(solution)/shard_map/ppermute | solution.py:18
  44.6 7.7 %collective-permute-start.13 = (bf16[32,2048]{1,0:T(8,128)(2,1)S(1)}, bf16[32,2048]{1,0:T(8,128)(2,1)S(1)}, u32[]{:S(2)}, u32[]{:S(2)}) collective-permute-start(bf16[32,2048]{1,0:T(8,128)(2,1)S(1)} %get-tuple-element.54), channel_id=1, source_target_pairs={{0,4},{4,0},{8,12},{12,8},{1,5},{5,1},{9,13},{13,9},{2,6},{6,2},{1... | collective-permute-start | bytes 393224 | tf_op jit(solution)/shard_map/ppermute | solution.py:18
  46.6 12.9 %collective-permute-start.14 = (bf16[32,2048]{1,0:T(8,128)(2,1)S(1)}, bf16[32,2048]{1,0:T(8,128)(2,1)S(1)}, u32[]{:S(2)}, u32[]{:S(2)}) collective-permute-start(bf16[32,2048]{1,0:T(8,128)(2,1)S(1)} %get-tuple-element.55), channel_id=1, source_target_pairs={{0,8},{4,12},{8,0},{12,4},{1,9},{5,13},{9,1},{13,5},{2,10},{6,14},... | collective-permute-start | bytes 393224 | tf_op jit(solution)/shard_map/ppermute | solution.py:18
  47.9 11.6 %collective-permute-start.15 = (bf16[32,2048]{1,0:T(8,128)(2,1)S(1)}, bf16[32,2048]{1,0:T(8,128)(2,1)S(1)}, u32[]{:S(2)}, u32[]{:S(2)}) collective-permute-start(bf16[32,2048]{1,0:T(8,128)(2,1)S(1)} %get-tuple-element.56), channel_id=1, source_target_pairs={{0,12},{4,8},{8,4},{12,0},{1,13},{5,9},{9,5},{13,1},{2,14},{6,10},... | collective-permute-start | bytes 393224 | tf_op jit(solution)/shard_map/ppermute | solution.py:18

commit v3 on v0

v3 whole, which is shorter than its diff:
```python
import functools

import jax
import jax.numpy as jnp
from jax import lax
from jax.experimental import pallas as pl
from jax.experimental.pallas import tpu as pltpu
from jax.sharding import PartitionSpec as P

D = 8192
F32 = jnp.float32
BF16 = jnp.bfloat16
LANES = 128
GROUPS = ((0,), (1,), (2,))


def swap(value, axis, hop):
    count = lax.axis_size(axis)
    return lax.ppermute(value, axis, [(i, i ^ hop) for i in range(count)])


def call(body, outs, args, flops=0, scalars=0):
    whole = pl.BlockSpec(memory_space=pltpu.VMEM)
    small = pl.BlockSpec(memory_space=pltpu.SMEM)
    size = sum(a.size * a.dtype.itemsize for a in (*args, *outs))
    return pl.pallas_call(
        body,
        out_shape=outs,
        in_specs=[small] * scalars + [whole] * (len(args) - scalars),
        out_specs=[whole] * len(outs),
        compiler_params=pltpu.CompilerParams(vmem_limit_bytes=12 << 20),
        cost_estimate=pl.CostEstimate(flops=flops, bytes_accessed=size, transcendentals=0),
    )(*args)


def struct(*shape, dtype=BF16):
    return jax.ShapeDtypeStruct(shape, dtype)


def tiles(width):
    step = next(size for size in (512, 256, 128, width) if width % size == 0)
    return [slice(at, at + step) for at in range(0, width, step)]


def iota(shape, dim):
    return lax.broadcasted_iota(jnp.int32, shape, dim)


def look(keys, table):
    hit = keys == iota((keys.shape[0], table.shape[1]), 1)
    return jnp.sum(jnp.where(hit, table.astype(F32), 0.0), axis=1, keepdims=True).astype(jnp.int32)


def index_body(n, share, rows, mine, place, assign, first, second):
    total = n * share
    row = iota((total, 1), 0)
    rank = lax.div(row, share)
    rel = jnp.where(rank < n // 2, 2 * rank, 2 * (rank - n // 2) + 1)
    slot = (rel ^ mine) * share + lax.rem(row, share)
    for picker, wanted in ((first, look(slot, assign[1:2, :])), (second, slot)):
        spot = (lax.div(wanted, rows) ^ place) * rows + lax.rem(wanted, rows)
        hit = spot == iota((total, total), 1)
        picker[...] = jnp.where(hit, 1.0, 0.0).astype(BF16)


def load_body(n, share, rows, direct, assign, weight, first, second, *refs):
    outs, (table, sems) = refs[:-2], refs[-2:]
    fetch = pltpu.make_async_copy(assign, table, sems.at[len(outs)])
    fetch.start()
    copies = [
        pltpu.make_async_copy(weight.at[j], out, sems.at[j]) for j, out in enumerate(outs)
    ]
    for copy in copies:
        copy.start()
    mine = lax.axis_index("narrow")
    place = lax.axis_index("wide") if direct else 0
    fetch.wait()
    index_body(n, share, rows, mine, place, table, first, second)
    for copy in copies:
        copy.wait()


def load(n, share, rows, direct, assign, weight):
    one = struct(*weight.shape[1:])
    size = 2 * weight.size * weight.dtype.itemsize
    vmem = pl.BlockSpec(memory_space=pltpu.VMEM)
    hbm = pl.BlockSpec(memory_space=pltpu.HBM)
    return pl.pallas_call(
        functools.partial(load_body, n, share, rows, direct),
        out_shape=[struct(n * share, n * share)] * 2 + [one] * 3,
        in_specs=[hbm, hbm],
        out_specs=[vmem] * 5,
        scratch_shapes=[pltpu.VMEM(assign.shape, jnp.int32), pltpu.SemaphoreType.DMA((4,))],
        compiler_params=pltpu.CompilerParams(vmem_limit_bytes=12 << 20),
        cost_estimate=pl.CostEstimate(flops=0, bytes_accessed=size, transcendentals=0),
    )(assign, weight)


def split3(value):
    high = value.astype(BF16).astype(F32)
    mid = (value - high).astype(BF16).astype(F32)
    low = value - high - mid
    lane = iota((value.shape[0], LANES), 1)
    return jnp.where(
        lane == 0, high, jnp.where(lane == 1, mid, jnp.where(lane == 2, low, 0.0))
    ).astype(BF16)


def join3(value):
    return jnp.sum(value.astype(F32), axis=1, keepdims=True)


def project_tiles(scaled, weights, keep, send):
    half = keep.shape[0]
    for j, weight in enumerate(weights):
        width = weight.shape[1]
        for cols in tiles(width):
            product = jnp.dot(scaled[...], weight[:, cols], preferred_element_type=F32)
            at = slice(j * width + cols.start, j * width + cols.stop)
            keep[:, at] = product[:half]
            send[:, at] = product[half:].astype(BF16)


def first_body(share, rows, steps, order, first, second, gain, *refs):
    count = 1 + len(order)
    blocks, weights = refs[:count], refs[count:-4]
    blocks = [blocks[0]] + [blocks[1 + order.index(k)] for k in range(1, count)]
    scaled, keep, send, squares = refs[-4:]
    length, feats = blocks[0].shape
    total = first.shape[0]
    half, width = keep.shape
    for stage, picker in enumerate((first, second)):
        x = jnp.concatenate(
            [
                block[at : at + rows, :]
                for block in blocks
                for at in range(stage * rows, length, steps * rows)
            ]
        )
        sums = jnp.zeros((total, 1), F32)
        spots = [
            (slice(at, at + share), slice(at * steps + stage * share, at * steps + (stage + 1) * share))
            for at in range(0, total, share)
        ]
        for cols in tiles(feats):
            ordered = jnp.dot(picker[...], x[:, cols], preferred_element_type=F32)
            sums = sums + jnp.sum(ordered * ordered, axis=1, keepdims=True)
            value = (ordered * gain[:, cols]).astype(BF16)
            for source, target in spots:
                scaled[target, cols] = value[source]
        for source, target in spots:
            if target.start < half:
                squares[target, :] = jnp.broadcast_to(sums[source], (share, LANES))
            else:
                send[target.start - half : target.stop - half, width:] = split3(sums[source])
    project_tiles(scaled, weights, keep, send)


def next_body(scaled, *refs):
    *weights, keep, send = refs
    project_tiles(scaled, weights, keep, send)


def add_body(unit, with_squares, keep, got, *refs):
    width = keep.shape[1]
    if with_squares:
        squares, own, own_squares, *sends = refs
        total = squares[:, :1] + join3(got[:, width:])
        own_squares[...] = jnp.broadcast_to(total[:unit], own_squares.shape)
    else:
        own, *sends = refs
    for cols in tiles(width):
        own[:, cols] = keep[:unit, cols] + got[:unit, cols].astype(F32)
        for p, send in enumerate(sends, 1):
            part = slice(p * unit, (p + 1) * unit)
            send[:, cols] = (keep[part, cols] + got[part, cols].astype(F32)).astype(BF16)
    if with_squares:
        for p, send in enumerate(sends, 1):
            send[:, width:] = split3(total[p * unit : (p + 1) * unit])


def past_body(n, share, assign, conv, *refs):
    pools, (older, newer) = refs[:n], refs[n:]
    mine = lax.axis_index("narrow")

    def one(row, carry):
        cand = assign[0, assign[1, mine * share + row]]
        rel = lax.div(cand, share) ^ mine
        spot = lax.rem(cand, share)
        for j in range(3):
            both = pools[0][spot, j].astype(F32)
            for k in range(1, n):
                both = jnp.where(rel == k, pools[k][spot, j].astype(F32), both)
            first = conv[0, j : j + 1, :]
            older[j, pl.ds(row, 1), :] = first * both[0:1] + conv[1, j : j + 1, :] * both[1:2]
            newer[j, pl.ds(row, 1), :] = first * both[1:2]
        return carry

    lax.fori_loop(0, share, one, 0)


def mix_body(share, peers, groups, conv, older, newer, squares, *refs):
    gated, fresh = refs[-2:]
    owns = refs[: len(groups)]
    gots = [refs[at : at + peers] for at in range(len(groups), len(refs) - 2, peers)]
    width = gated.shape[1]
    total = squares[:, :1]
    for got in gots[0]:
        total = total + join3(got[:, owns[0].shape[1] :])
    scale = lax.rsqrt(total / D + 1e-05)
    for cols in tiles(width):
        gate = None
        for g, group in enumerate(groups):
            for at, j in enumerate(group):
                spot = slice(at * width + cols.start, at * width + cols.stop)
                new = owns[g][:, spot]
                for got in gots[g]:
                    new = new + got[:, spot].astype(F32)
                new = (new * scale).astype(BF16)
                new0, new1 = new[:share], new[share:]
                fresh[j, 0, :, cols] = new0
                fresh[j, 1, :, cols] = new1
                new0, new1 = new0.astype(F32), new1.astype(F32)
                last = conv[2, j : j + 1, cols]
                mixed0 = older[j, :, cols] + last * new0
                mixed1 = newer[j, :, cols] + conv[1, j : j + 1, cols] * new0 + last * new1
                mixed = jnp.concatenate([mixed0, mixed1])
                gate = mixed if gate is None else gate * mixed
        gated[:, cols] = gate.astype(BF16)


def out_body(n, share, rows, first, second, weight, *refs):
    pieces, own, rest = refs[:n], refs[n], refs[n + 1 :]
    lined = []
    for stage, picker in enumerate((first, second)):
        part = slice(stage * share, (stage + 1) * share)
        every = jnp.concatenate([piece[part, :] for piece in pieces])
        lined.append(
            lax.dot_general(
                picker[...], every, (((0,), (0,)), ((), ())), preferred_element_type=F32
            ).astype(BF16)
        )
    blocks = range(0, first.shape[0], rows)
    lined = jnp.concatenate([part[at : at + rows] for at in blocks for part in lined])
    block = own.shape[0]
    for cols in tiles(weight.shape[1]):
        product = jnp.dot(lined, weight[:, cols], preferred_element_type=F32)
        own[:, cols] = product[:block].astype(own.dtype)
        for k, ref in enumerate(rest, 1):
            ref[:, cols] = product[k * block : (k + 1) * block].astype(BF16)


def shards(tokens, assign, state, norm_gain, in_weight, conv_weight, out_weight):
    n = lax.axis_size("narrow")
    wide = lax.axis_size("wide")
    steps, rows, feats = tokens.shape
    share = state.shape[0]
    chans = in_weight.shape[2]
    outs = out_weight.shape[1]
    direct = wide <= 4
    order = [k for k in (2, 3, 1) if k < wide]
    evens = [2 * k for k in range(n // 2)]
    total = n * share
    half = total // 2

    mine_tokens = tokens.reshape(steps * rows, feats)
    if direct:
        blocks = [mine_tokens] + [swap(mine_tokens, "wide", k) for k in order]
    else:
        blocks = [lax.all_gather(mine_tokens, "wide", axis=0, tiled=True)]

    past = state.transpose(0, 2, 1, 3)
    pools = [past] * n
    for k in evens:
        pools[k] = swap(past, "narrow", k) if k else past
        pools[k + 1] = swap(pools[k], "narrow", 1)

    *pickers, w0, w1, w2 = load(n, share, rows, direct, assign, in_weight.transpose(1, 0, 2))
    weights = [w0, w1, w2]
    older, newer = call(
        functools.partial(past_body, n, share),
        [struct(3, share, chans, dtype=F32)] * 2,
        [assign, conv_weight, *pools],
        scalars=1,
    )

    unit = steps * share
    cost = 2 * steps * total * feats * chans
    owns, gots = [], []
    for group in GROUPS:
        first = not owns
        width = chans * len(group)
        wider = width + LANES * first
        shapes = [struct(steps * half, width, dtype=F32), struct(steps * half, wider)]
        if first:
            scaled, keep, send, squares = call(
                functools.partial(first_body, share, rows, steps, order if direct else []),
                [struct(steps * total, feats), *shapes, struct(steps * half, LANES, dtype=F32)],
                [*pickers, norm_gain.reshape(1, feats), *blocks, *(weights[j] for j in group)],
                flops=cost * len(group),
            )
        else:
            keep, send = call(
                next_body,
                shapes,
                [scaled, *(weights[j] for j in group)],
                flops=cost * len(group),
            )
        extra = [squares] if first else []
        kept = [struct(unit, width, dtype=F32)] + [struct(unit, LANES, dtype=F32)] * len(extra)
        result = call(
            functools.partial(add_body, unit, first),
            kept + [struct(unit, wider)] * (n // 2 - 1),
            [keep, swap(send, "narrow", 1), *extra],
        )
        owns.append(result[0])
        if first:
            squares = result[1]
        gots += [swap(p, "narrow", k) for p, k in zip(result[len(kept) :], evens[1:])]
    gated, fresh = call(
        functools.partial(mix_body, share, n // 2 - 1, GROUPS),
        [struct(unit, chans), struct(3, 2, share, chans)],
        [conv_weight, older, newer, squares, *owns, *gots],
    )
    near = [swap(gated, "narrow", k) if k else gated for k in evens]
    far = [swap(piece, "narrow", 1) for piece in near]
    block = steps * rows
    shapes = [struct(steps * total, outs)]
    if direct:
        shapes = [struct(block, outs, dtype=F32)] + [struct(block, outs)] * (wide - 1)
    out, *parts = call(
        functools.partial(out_body, n, share, rows),
        shapes,
        [*pickers, out_weight, *near, *far],
        flops=2 * steps * total * chans * outs,
    )
    if direct:
        for k in order:
            out = out + swap(parts[k - 1], "wide", k).astype(F32)
        out = out.astype(BF16)
    else:
        out = lax.psum_scatter(out, "wide", scatter_dimension=0, tiled=True)
    return (out.reshape(steps, rows, outs), fresh.transpose(2, 1, 0, 3))


def solution(mesh):
    in_specs = (
        P(None, ("groups", "wide"), "narrow"),
        P(None, "groups"),
        P(("groups", "narrow"), None, None, "wide"),
        P("narrow"),
        P("narrow", None, "wide"),
        P(None, None, "wide"),
        P("wide", "narrow"),
    )
    out_specs = (P(None, ("groups", "wide"), "narrow"), P(("groups", "narrow"), None, None, "wide"))
    return jax.shard_map(shards, mesh=mesh, in_specs=in_specs, out_specs=out_specs, check_vma=False)
```

time: 236 us -> 57 us (0.24)
  waiting for transfers between devices: 83.8 us -> 21.8 us
  blocking collectives: 48.5 us -> 0 us
  local copies, waits for them, and re-layouts: 43 us -> 1.86 us
  matrix products: 38.4 us -> 0 us
  starting transfers between devices: 0.24 us -> 16.1 us
  Pallas kernels: 0 us -> 15.6 us
  between operations: 14.3 us -> 0.79 us
  other arithmetic: 6.65 us -> 0.72 us
    reduce_scatter x4 -> x0, waiting for transfers between devices: 47.2 us -> none  [the longest x2 26.7 us: shards(): lax.psum_scatter(partial_out.astype(jnp.bfloat16), 'wide', scatter_dimens...]
    all_gather x4 -> x0, blocking collectives: 40.2 us -> none  [the longest x2 28.3 us: shards(): gathered = lax.all_gather(normed, 'wide', axis=0, tiled=True)]
    dot_general x4 -> x0, matrix products: 38.4 us -> none  [the longest x2 27 us: shards(): jnp.dot(gathered, flat_in, preferred_element_type=jnp.float32)]
    all_gather x2 -> x0, waiting for transfers between devices: 35.8 us -> none  [shards(): piece = lax.all_gather(memory, 'narrow', axis=0, tiled=True)]
    unnamed x8 -> x17, local copies, waits for them, and re-layouts: 34.5 us -> 1.86 us
    ppermute x0 -> x18, waiting for transfers between devices: none -> 21.8 us  [swap(): return lax.ppermute(value, axis, [(i, i ^ hop) for i in range(count)])]
    ppermute x0 -> x18, starting transfers between devices: none -> 16.1 us  [swap(): return lax.ppermute(value, axis, [(i, i ^ hop) for i in range(count)])]
    pallas_call x0 -> x10, Pallas kernels: none -> 15.6 us  [the longest x1 8.23 us: load(): pl.pallas_call(functools.partial(load_body, n, share, rows, direct), out_...]
  transfers between devices with their start and end apart: 6 -> 18, of which waited for: 5 -> 6; matrix products, arithmetic and copies ran while one was open for 12% -> 2% of each run, Pallas kernels for 0% -> 24%
where the time goes in v3:
time: 57 us; the launch traced here: 56.9 us
  waiting for transfers between devices  21.8 us (38%)
  starting transfers between devices  16.1 us (28%)
  Pallas kernels  15.6 us (27%)
  local copies, waits for them, and re-layouts  1.86 us (3%)
  between operations  0.79 us (1%)
  other arithmetic  0.72 us (1%)
    ppermute x18, waiting for transfers between devices, swap(): return lax.ppermute(value, axis, [(i, i ^ hop) for i in range(count)])  21.8 us
    ppermute x18, starting transfers between devices, swap(): return lax.ppermute(value, axis, [(i, i ^ hop) for i in range(count)])  16.1 us
    pallas_call x1, Pallas kernels, load(): pl.pallas_call(functools.partial(load_body, n, share, rows, direct), out_...  8.23 us
    pallas_call x9, Pallas kernels, call(): pl.pallas_call(body, out_shape=outs, in_specs=[small] * scalars + [whole]...  7.41 us
    unnamed x17, local copies, waits for them, and re-layouts  1.86 us
  transfers between devices with their start and end apart: 18, of which 6 were waited for; matrix products, arithmetic and copies ran while one was open for 2% of the time, Pallas kernels for 24%

profile of v3, /device:TPU:0, one launch (start us, length us, event | category | flops | bytes accessed | tf_op | source)
XLA Modules:
  0.0 56.9 jit_solution(3219768408649480925)
XLA Ops:
  0.6 4.1 %collective-permute-start.3 = (bf16[32,2048]{1,0:T(8,128)(2,1)}, bf16[32,2048]{1,0:T(8,128)(2,1)S(1)}, u32[]{:S(2)}, u32[]{:S(2)}) collective-permute-start(bf16[32,2048]{1,0:T(8,128)(2,1)} %bitcast.12), channel_id=1, source_target_pairs={{0,8},{4,12},{8,0},{12,4},{1,9},{5,13},{9,1},{13,5},{2,10},{6,14},... | collective-permute-start | bytes 393224 | tf_op jit(solution)/shard_map/ppermute | solution.py:19
  4.7 1.3 %collective-permute-start.4 = (bf16[32,2048]{1,0:T(8,128)(2,1)}, bf16[32,2048]{1,0:T(8,128)(2,1)S(1)}, u32[]{:S(2)}, u32[]{:S(2)}) collective-permute-start(bf16[32,2048]{1,0:T(8,128)(2,1)} %bitcast.13), channel_id=1, source_target_pairs={{0,12},{4,8},{8,4},{12,0},{1,13},{5,9},{9,5},{13,1},{2,14},{6,10},... | collective-permute-start | bytes 393224 | tf_op jit(solution)/shard_map/ppermute | solution.py:19
  6.1 0.2 collective-permute-start.5
  6.3 1.5 %collective-permute-start.1 = (bf16[16,3,2,2048]{3,2,1,0:T(2,128)(2,1)}, bf16[16,3,2,2048]{3,2,1,0:T(2,128)(2,1)S(1)}, u32[]{:S(2)}, u32[]{:S(2)}) collective-permute-start(bf16[16,3,2,2048]{3,2,1,0:T(2,128)(2,1)} %bitcast.9), channel_id=1, source_target_pairs={{0,2},{1,3},{2,0},{3,1},{4,6},{5,7},{6,4},{7,5},{8,10},{9,11},{10,... | collective-permute-start | bytes 1179656 | tf_op jit(solution)/shard_map/ppermute | solution.py:19
  7.8 0.0 collective-permute-start
  7.8 0.0 copy-start.4
  7.8 0.7 %copy-done.4 = s32[2,64]{1,0:T(2,128)S(1)} copy-done((s32[2,64]{1,0:T(2,128)S(1)}, s32[2,64]{1,0:T(2,128)}, u32[]{:S(2)}) %copy-start.4) | copy-done | bytes 536
  8.5 0.0 copy-start.2
  8.5 0.0 copy-start.3
  8.5 8.2 %shard_map.86 = (bf16[64,64]{1,0:T(8,128)(2,1)S(1)}, bf16[64,64]{1,0:T(8,128)(2,1)S(1)}, bf16[2048,2048]{1,0:T(8,128)(2,1)S(1)}, bf16[2048,2048]{1,0:T(8,128)(2,1)S(1)}, bf16[2048,2048]{1,0:T(8,128)(2,1)S(1)}) custom-call(s32[2,64]{1,0:T(2,128)S(1)} %copy-done.4, bf16[3,2048,2048]{2,1,0:T(8,128)(2,1)} %bitcast.17), custom_call_target="tpu_custom_call" | custom-call | bytes 50331648 | tf_op jit(solution)/shard_map/pallas_call | solution.py:88
  16.7 0.0 collective-permute-done.3.refs_1_
  16.7 0.0 collective-permute-done.4.refs_2_
  16.7 0.0 collective-permute-done.5.refs_3_
  16.8 0.0 copy-done.2
  16.8 0.0 copy-done.3
  16.8 1.5 %shard_map.88 = (bf16[128,2048]{1,0:T(8,128)(2,1)S(1)}, f32[64,2048]{1,0:T(8,128)S(1)}, bf16[64,2176]{1,0:T(8,128)(2,1)S(1)}, f32[64,128]{1,0:T(8,128)S(1)}) custom-call(bf16[64,64]{1,0:T(8,128)(2,1)S(1)} %get-tuple-element.30.first, bf16[64,64]{1,0:T(8,128)(2,1)S(1)} %get-tuple-element.31.second, f32[1,2048]{1,0:T(1,128)S(1)} %bitcast.16, ...), custom_call_target="tpu_custom_call" | custom-call | flops 1073741824 | bytes 10297344 | tf_op jit(solution)/shard_map/pallas_call | solution.py:26
  18.3 0.6 %collective-permute-start.6 = (bf16[64,2176]{1,0:T(8,128)(2,1)S(1)}, bf16[64,2176]{1,0:T(8,128)(2,1)S(1)}, u32[]{:S(2)}, u32[]{:S(2)}) collective-permute-start(bf16[64,2176]{1,0:T(8,128)(2,1)S(1)} %get-tuple-element.36), channel_id=1, source_target_pairs={{0,1},{1,0},{2,3},{3,2},{4,5},{5,4},{6,7},{7,6},{8,9},{9,8},{10,11... | collective-permute-start | bytes 835592 | tf_op jit(solution)/shard_map/ppermute | solution.py:19
  18.9 0.0 copy-start
  18.9 0.0 copy-start.1
  18.9 0.0 copy-start.5
  18.9 1.3 %shard_map.92 = (f32[64,2048]{1,0:T(8,128)S(1)}, bf16[64,2048]{1,0:T(8,128)(2,1)S(1)}) custom-call(bf16[128,2048]{1,0:T(8,128)(2,1)S(1)} %get-tuple-element.40.scaled, bf16[2048,2048]{1,0:T(8,128)(2,1)S(1)} %get-tuple-element.45.refs_0_), custom_call_target="tpu_custom_call" | custom-call | flops 1073741824 | bytes 9699328 | tf_op jit(solution)/shard_map/pallas_call | solution.py:26
  20.2 0.0 slice-start
  20.2 0.1 collective-permute-start.8
  20.3 0.0 slice-start.1
  20.3 1.3 %shard_map.90 = (f32[64,2048]{1,0:T(8,128)S(1)}, bf16[64,2048]{1,0:T(8,128)(2,1)S(1)}) custom-call(bf16[128,2048]{1,0:T(8,128)(2,1)S(1)} %get-tuple-element.40.scaled, bf16[2048,2048]{1,0:T(8,128)(2,1)S(1)} %get-tuple-element.41.refs_0_), custom_call_target="tpu_custom_call" | custom-call | flops 1073741824 | bytes 9699328 | tf_op jit(solution)/shard_map/pallas_call | solution.py:26
  21.6 0.5 collective-permute-start.7
  22.1 0.0 collective-permute-done.1.refs_2_
  22.1 0.1 collective-permute-start.2
  22.2 0.0 collective-permute-done.6.got
  22.2 0.2 shard_map.89
  22.4 0.6 %collective-permute-start.9 = (bf16[32,2176]{1,0:T(8,128)(2,1)S(1)}, bf16[32,2176]{1,0:T(8,128)(2,1)S(1)}, u32[]{:S(2)}, u32[]{:S(2)}) collective-permute-start(bf16[32,2176]{1,0:T(8,128)(2,1)S(1)} %get-tuple-element.49), channel_id=1, source_target_pairs={{0,2},{1,3},{2,0},{3,1},{4,6},{5,7},{6,4},{7,5},{8,10},{9,11},{10,... | collective-permute-start | bytes 417800 | tf_op jit(solution)/shard_map/ppermute | solution.py:19
  23.0 0.0 collective-permute-done.8.got
  23.1 1.6 %collective-permute-start.11 = (bf16[32,2048]{1,0:T(8,128)(2,1)S(1)}, bf16[32,2048]{1,0:T(8,128)(2,1)S(1)}, u32[]{:S(2)}, u32[]{:S(2)}) collective-permute-start(bf16[32,2048]{1,0:T(8,128)(2,1)S(1)} %get-tuple-element.51), channel_id=1, source_target_pairs={{0,2},{1,3},{2,0},{3,1},{4,6},{5,7},{6,4},{7,5},{8,10},{9,11},{10,... | collective-permute-start | bytes 393224 | tf_op jit(solution)/shard_map/ppermute | solution.py:19
  24.6 0.0 collective-permute-done.7.got
  24.6 0.1 shard_map.91
  24.7 0.6 %collective-permute-start.10 = (bf16[32,2048]{1,0:T(8,128)(2,1)S(1)}, bf16[32,2048]{1,0:T(8,128)(2,1)S(1)}, u32[]{:S(2)}, u32[]{:S(2)}) collective-permute-start(bf16[32,2048]{1,0:T(8,128)(2,1)S(1)} %get-tuple-element.50), channel_id=1, source_target_pairs={{0,2},{1,3},{2,0},{3,1},{4,6},{5,7},{6,4},{7,5},{8,10},{9,11},{10,... | collective-permute-start | bytes 393224 | tf_op jit(solution)/shard_map/ppermute | solution.py:19
  25.3 0.0 collective-permute-done.refs_1_
  25.3 0.0 collective-permute-done.2.refs_3_
  25.3 0.0 copy-done
  25.3 0.0 copy-done.1
  25.3 0.0 copy-done.5
  25.3 1.2 %shard_map.87 = (f32[3,16,2048]{2,1,0:T(8,128)S(1)}, f32[3,16,2048]{2,1,0:T(8,128)S(1)}) custom-call(s32[2,64]{1,0:T(2,128)S(1)} %copy-done.5, f32[3,3,2048]{2,1,0:T(4,128)S(1)} %copy-done, bf16[16,3,2,2048]{3,2,1,0:T(2,128)(2,1)S(1)} %bitcast.11, bf16[16,3,2,2048]{3,2,1,0:T(2,128)(2,1)S(1)} %collective-permute-done.refs_1_, ...), custom_call_target="tpu_custom_call" | custom-call | bytes 2433536 | tf_op jit(solution)/shard_map/pallas_call | solution.py:26
  26.5 5.3 %collective-permute-done.11.refs_5_ = bf16[32,2048]{1,0:T(8,128)(2,1)S(1)} collective-permute-done((bf16[32,2048]{1,0:T(8,128)(2,1)S(1)}, bf16[32,2048]{1,0:T(8,128)(2,1)S(1)}, u32[]{:S(2)}, u32[]{:S(2)}) %collective-permute-start.11) | collective-permute-done | bytes 131104 | tf_op jit(solution)/shard_map/ppermute | solution.py:19
  31.8 2.3 %collective-permute-done.10.refs_4_ = bf16[32,2048]{1,0:T(8,128)(2,1)S(1)} collective-permute-done((bf16[32,2048]{1,0:T(8,128)(2,1)S(1)}, bf16[32,2048]{1,0:T(8,128)(2,1)S(1)}, u32[]{:S(2)}, u32[]{:S(2)}) %collective-permute-start.10) | collective-permute-done | bytes 131104 | tf_op jit(solution)/shard_map/ppermute | solution.py:19
  34.1 0.0 collective-permute-done.9.refs_3_
  34.1 0.4 shard_map.94
  34.5 0.6 %collective-permute-start.12 = (bf16[32,2048]{1,0:T(8,128)(2,1)S(1)}, bf16[32,2048]{1,0:T(8,128)(2,1)S(1)}, u32[]{:S(2)}, u32[]{:S(2)}) collective-permute-start(bf16[32,2048]{1,0:T(8,128)(2,1)S(1)} %get-tuple-element.52.refs_0_), channel_id=1, source_target_pairs={{0,2},{1,3},{2,0},{3,1},{4,6},{5,7},{6,4},{7,5},{8,10},{9,11},{10,... | collective-permute-start | bytes 393224 | tf_op jit(solution)/shard_map/ppermute | solution.py:19
  35.1 0.0 collective-permute-start.13
  35.1 4.5 %collective-permute-done.12.refs_1_ = bf16[32,2048]{1,0:T(8,128)(2,1)S(1)} collective-permute-done((bf16[32,2048]{1,0:T(8,128)(2,1)S(1)}, bf16[32,2048]{1,0:T(8,128)(2,1)S(1)}, u32[]{:S(2)}, u32[]{:S(2)}) %collective-permute-start.12) | collective-permute-done | bytes 131104 | tf_op jit(solution)/shard_map/ppermute | solution.py:19
  39.6 0.0 collective-permute-start.14
  39.6 0.0 collective-permute-done.13.refs_2_
  39.6 1.3 %collective-permute-done.14.refs_3_ = bf16[32,2048]{1,0:T(8,128)(2,1)S(1)} collective-permute-done((bf16[32,2048]{1,0:T(8,128)(2,1)S(1)}, bf16[32,2048]{1,0:T(8,128)(2,1)S(1)}, u32[]{:S(2)}, u32[]{:S(2)}) %collective-permute-start.14) | collective-permute-done | bytes 131104 | tf_op jit(solution)/shard_map/ppermute | solution.py:19
  41.0 0.0 slice-done
  41.0 0.0 slice-done.1
  41.0 1.5 %shard_map.95 = (f32[32,2048]{1,0:T(8,128)S(1)}, bf16[32,2048]{1,0:T(8,128)(2,1)S(1)}, bf16[32,2048]{1,0:T(8,128)(2,1)S(1)}, bf16[32,2048]{1,0:T(8,128)(2,1)S(1)}) custom-call(bf16[64,64]{1,0:T(8,128)(2,1)S(1)} %get-tuple-element.30.first, bf16[64,64]{1,0:T(8,128)(2,1)S(1)} %get-tuple-element.31.second, bf16[2048,2048]{1,0:T(8,128)(2,1)S(1)} %bitcast.7, ...), custom_call_target="tpu_custom_call" | custom-call | flops 1073741824 | bytes 9584640 | tf_op jit(solution)/shard_map/pallas_call | solution.py:26
  42.5 2.9 %collective-permute-start.15 = (bf16[32,2048]{1,0:T(8,128)(2,1)S(1)}, bf16[32,2048]{1,0:T(8,128)(2,1)S(1)}, u32[]{:S(2)}, u32[]{:S(2)}) collective-permute-start(bf16[32,2048]{1,0:T(8,128)(2,1)S(1)} %get-tuple-element.54), channel_id=1, source_target_pairs={{0,8},{4,12},{8,0},{12,4},{1,9},{5,13},{9,1},{13,5},{2,10},{6,14},... | collective-permute-start | bytes 393224 | tf_op jit(solution)/shard_map/ppermute | solution.py:19
  45.4 1.3 %collective-permute-start.16 = (bf16[32,2048]{1,0:T(8,128)(2,1)S(1)}, bf16[32,2048]{1,0:T(8,128)(2,1)S(1)}, u32[]{:S(2)}, u32[]{:S(2)}) collective-permute-start(bf16[32,2048]{1,0:T(8,128)(2,1)S(1)} %get-tuple-element.55), channel_id=1, source_target_pairs={{0,12},{4,8},{8,4},{12,0},{1,13},{5,9},{9,5},{13,1},{2,14},{6,10},... | collective-permute-start | bytes 393224 | tf_op jit(solution)/shard_map/ppermute | solution.py:19
  46.7 0.0 collective-permute-start.17
  46.7 1.2 %copy.9 = bf16[16,2,3,2048]{3,1,2,0:T(2,128)(2,1)} copy(bf16[16,2,3,2048]{3,0,1,2:T(8,128)(2,1)S(1)} %bitcast.8) | data formatting | bytes 786432
  47.9 7.6 %collective-permute-done.15 = bf16[32,2048]{1,0:T(8,128)(2,1)S(1)} collective-permute-done((bf16[32,2048]{1,0:T(8,128)(2,1)S(1)}, bf16[32,2048]{1,0:T(8,128)(2,1)S(1)}, u32[]{:S(2)}, u32[]{:S(2)}) %collective-permute-start.15) | collective-permute-done | bytes 131104 | tf_op jit(solution)/shard_map/ppermute | solution.py:19
  55.4 0.0 collective-permute-done.16
  55.4 0.7 %collective-permute-done.17 = bf16[32,2048]{1,0:T(8,128)(2,1)S(1)} collective-permute-done((bf16[32,2048]{1,0:T(8,128)(2,1)S(1)}, bf16[32,2048]{1,0:T(8,128)(2,1)S(1)}, u32[]{:S(2)}, u32[]{:S(2)}) %collective-permute-start.17) | collective-permute-done | bytes 131104 | tf_op jit(solution)/shard_map/ppermute | solution.py:19
  56.2 0.7 %add_convert_fusion = bf16[32,2048]{1,0:T(8,128)(2,1)} fusion(bf16[32,2048]{1,0:T(8,128)(2,1)S(1)} %collective-permute-done.17, bf16[32,2048]{1,0:T(8,128)(2,1)S(1)} %collective-permute-done.16, f32[32,2048]{1,0:T(8,128)S(1)} %get-tuple-element.53, bf16[32,2048]{1,0:T(8,128)(2,1)S(1)} %collective-permute-done.15), kind=kLoop, calls=%fused_computation | loop fusion | flops 458752 | bytes 786432 | tf_op jit(solution)/shard_map/convert_element_type | solution.py:340
  (2 shorter events, 0.0 us)
Async XLA Ops:
  0.6 16.1 %collective-permute-start.3 = (bf16[32,2048]{1,0:T(8,128)(2,1)}, bf16[32,2048]{1,0:T(8,128)(2,1)S(1)}, u32[]{:S(2)}, u32[]{:S(2)}) collective-permute-start(bf16[32,2048]{1,0:T(8,128)(2,1)} %bitcast.12), channel_id=1, source_target_pairs={{0,8},{4,12},{8,0},{12,4},{1,9},{5,13},{9,1},{13,5},{2,10},{6,14},... | collective-permute-start | bytes 393224 | tf_op jit(solution)/shard_map/ppermute | solution.py:19
  4.7 12.0 %collective-permute-start.4 = (bf16[32,2048]{1,0:T(8,128)(2,1)}, bf16[32,2048]{1,0:T(8,128)(2,1)S(1)}, u32[]{:S(2)}, u32[]{:S(2)}) collective-permute-start(bf16[32,2048]{1,0:T(8,128)(2,1)} %bitcast.13), channel_id=1, source_target_pairs={{0,12},{4,8},{8,4},{12,0},{1,13},{5,9},{9,5},{13,1},{2,14},{6,10},... | collective-permute-start | bytes 393224 | tf_op jit(solution)/shard_map/ppermute | solution.py:19
  6.1 10.7 %collective-permute-start.5 = (bf16[32,2048]{1,0:T(8,128)(2,1)}, bf16[32,2048]{1,0:T(8,128)(2,1)S(1)}, u32[]{:S(2)}, u32[]{:S(2)}) collective-permute-start(bf16[32,2048]{1,0:T(8,128)(2,1)} %bitcast.14), channel_id=1, source_target_pairs={{0,4},{4,0},{8,12},{12,8},{1,5},{5,1},{9,13},{13,9},{2,6},{6,2},{1... | collective-permute-start | bytes 393224 | tf_op jit(solution)/shard_map/ppermute | solution.py:19
  6.3 15.8 %collective-permute-start.1 = (bf16[16,3,2,2048]{3,2,1,0:T(2,128)(2,1)}, bf16[16,3,2,2048]{3,2,1,0:T(2,128)(2,1)S(1)}, u32[]{:S(2)}, u32[]{:S(2)}) collective-permute-start(bf16[16,3,2,2048]{3,2,1,0:T(2,128)(2,1)} %bitcast.9), channel_id=1, source_target_pairs={{0,2},{1,3},{2,0},{3,1},{4,6},{5,7},{6,4},{7,5},{8,10},{9,11},{10,... | collective-permute-start | bytes 1179656 | tf_op jit(solution)/shard_map/ppermute | solution.py:19
  7.8 17.5 %collective-permute-start = (bf16[16,3,2,2048]{3,2,1,0:T(2,128)(2,1)}, bf16[16,3,2,2048]{3,2,1,0:T(2,128)(2,1)S(1)}, u32[]{:S(2)}, u32[]{:S(2)}) collective-permute-start(bf16[16,3,2,2048]{3,2,1,0:T(2,128)(2,1)} %bitcast.10), channel_id=1, source_target_pairs={{0,1},{1,0},{2,3},{3,2},{4,5},{5,4},{6,7},{7,6},{8,9},{9,8},{10,11... | collective-permute-start | bytes 1179656 | tf_op jit(solution)/shard_map/ppermute | solution.py:19
  7.8 0.7 %copy-start.4 = (s32[2,64]{1,0:T(2,128)S(1)}, s32[2,64]{1,0:T(2,128)}, u32[]{:S(2)}) copy-start(s32[2,64]{1,0:T(2,128)} %assign.3) | copy-start | bytes 1540
  8.5 8.3 %copy-start.2 = (bf16[2,16,2048]{2,1,0:T(8,128)(2,1)S(1)}, bf16[2,16,2048]{2,1,0:T(8,128)(2,1)}, u32[]{:S(2)}) copy-start(bf16[2,16,2048]{2,1,0:T(8,128)(2,1)} %param.7) | copy-start | bytes 393220
  8.5 8.3 %copy-start.3 = (f32[2048]{0:T(1024)S(1)}, f32[2048]{0:T(1024)}, u32[]{:S(2)}) copy-start(f32[2048]{0:T(1024)} %param.10) | copy-start | bytes 24580
  18.3 3.9 %collective-permute-start.6 = (bf16[64,2176]{1,0:T(8,128)(2,1)S(1)}, bf16[64,2176]{1,0:T(8,128)(2,1)S(1)}, u32[]{:S(2)}, u32[]{:S(2)}) collective-permute-start(bf16[64,2176]{1,0:T(8,128)(2,1)S(1)} %get-tuple-element.36), channel_id=1, source_target_pairs={{0,1},{1,0},{2,3},{3,2},{4,5},{5,4},{6,7},{7,6},{8,9},{9,8},{10,11... | collective-permute-start | bytes 835592 | tf_op jit(solution)/shard_map/ppermute | solution.py:19
  18.9 6.4 %copy-start = (f32[3,3,2048]{2,1,0:T(4,128)S(1)}, f32[3,3,2048]{2,1,0:T(4,128)}, u32[]{:S(2)}) copy-start(f32[3,3,2048]{2,1,0:T(4,128)} %conv.3) | copy-start | bytes 221188
  18.9 6.4 %copy-start.1 = (bf16[16,2,3,2048]{3,1,2,0:T(2,128)(2,1)S(1)}, bf16[16,2,3,2048]{3,1,2,0:T(2,128)(2,1)}, u32[]{:S(2)}) copy-start(bf16[16,2,3,2048]{3,1,2,0:T(2,128)(2,1)} %param.9) | copy-start | bytes 1179652
  18.9 6.4 %copy-start.5 = (s32[2,64]{1,0:T(2,128)S(1)}, s32[2,64]{1,0:T(2,128)}, u32[]{:S(2)}) copy-start(s32[2,64]{1,0:T(2,128)} %assign.3) | copy-start | bytes 1540
  20.2 20.8 %slice-start = ((s8[8388608]{0:T(1024)(128)(4,1)}), s8[4194304]{0:T(1024)(128)(4,1)S(1)}, s32[]{:S(2)}) async-start(s8[8388608]{0:T(1024)(128)(4,1)} %bitcast.6), calls=%async_computation | async-start | bytes 8388608
  20.2 2.8 %collective-permute-start.8 = (bf16[64,2048]{1,0:T(8,128)(2,1)S(1)}, bf16[64,2048]{1,0:T(8,128)(2,1)S(1)}, u32[]{:S(2)}, u32[]{:S(2)}) collective-permute-start(bf16[64,2048]{1,0:T(8,128)(2,1)S(1)} %get-tuple-element.47), channel_id=1, source_target_pairs={{0,1},{1,0},{2,3},{3,2},{4,5},{5,4},{6,7},{7,6},{8,9},{9,8},{10,11... | collective-permute-start | bytes 786440 | tf_op jit(solution)/shard_map/ppermute | solution.py:19
  20.3 20.7 %slice-start.1 = ((s8[8388608]{0:T(1024)(128)(4,1)}), s8[4194304]{0:T(1024)(128)(4,1)S(1)}, s32[]{:S(2)}) async-start(s8[8388608]{0:T(1024)(128)(4,1)} %bitcast.6), calls=%async_computation.1 | async-start | bytes 8388608
  21.6 3.0 %collective-permute-start.7 = (bf16[64,2048]{1,0:T(8,128)(2,1)S(1)}, bf16[64,2048]{1,0:T(8,128)(2,1)S(1)}, u32[]{:S(2)}, u32[]{:S(2)}) collective-permute-start(bf16[64,2048]{1,0:T(8,128)(2,1)S(1)} %get-tuple-element.43), channel_id=1, source_target_pairs={{0,1},{1,0},{2,3},{3,2},{4,5},{5,4},{6,7},{7,6},{8,9},{9,8},{10,11... | collective-permute-start | bytes 786440 | tf_op jit(solution)/shard_map/ppermute | solution.py:19
  22.1 3.1 %collective-permute-start.2 = (bf16[16,3,2,2048]{3,2,1,0:T(2,128)(2,1)S(1)}, bf16[16,3,2,2048]{3,2,1,0:T(2,128)(2,1)S(1)}, u32[]{:S(2)}, u32[]{:S(2)}) collective-permute-start(bf16[16,3,2,2048]{3,2,1,0:T(2,128)(2,1)S(1)} %collective-permute-done.1.refs_2_), channel_id=1, source_target_pairs={{0,1},{1,0},{2,3},{3,2},{4,5},{5,4},{6,7},{7,6},{8,9},{9,8},{10,11... | collective-permute-start | bytes 1179656 | tf_op jit(solution)/shard_map/ppermute | solution.py:19
  22.4 11.7 %collective-permute-start.9 = (bf16[32,2176]{1,0:T(8,128)(2,1)S(1)}, bf16[32,2176]{1,0:T(8,128)(2,1)S(1)}, u32[]{:S(2)}, u32[]{:S(2)}) collective-permute-start(bf16[32,2176]{1,0:T(8,128)(2,1)S(1)} %get-tuple-element.49), channel_id=1, source_target_pairs={{0,2},{1,3},{2,0},{3,1},{4,6},{5,7},{6,4},{7,5},{8,10},{9,11},{10,... | collective-permute-start | bytes 417800 | tf_op jit(solution)/shard_map/ppermute | solution.py:19
  23.1 8.7 %collective-permute-start.11 = (bf16[32,2048]{1,0:T(8,128)(2,1)S(1)}, bf16[32,2048]{1,0:T(8,128)(2,1)S(1)}, u32[]{:S(2)}, u32[]{:S(2)}) collective-permute-start(bf16[32,2048]{1,0:T(8,128)(2,1)S(1)} %get-tuple-element.51), channel_id=1, source_target_pairs={{0,2},{1,3},{2,0},{3,1},{4,6},{5,7},{6,4},{7,5},{8,10},{9,11},{10,... | collective-permute-start | bytes 393224 | tf_op jit(solution)/shard_map/ppermute | solution.py:19
  24.7 9.4 %collective-permute-start.10 = (bf16[32,2048]{1,0:T(8,128)(2,1)S(1)}, bf16[32,2048]{1,0:T(8,128)(2,1)S(1)}, u32[]{:S(2)}, u32[]{:S(2)}) collective-permute-start(bf16[32,2048]{1,0:T(8,128)(2,1)S(1)} %get-tuple-element.50), channel_id=1, source_target_pairs={{0,2},{1,3},{2,0},{3,1},{4,6},{5,7},{6,4},{7,5},{8,10},{9,11},{10,... | collective-permute-start | bytes 393224 | tf_op jit(solution)/shard_map/ppermute | solution.py:19
  34.5 5.1 %collective-permute-start.12 = (bf16[32,2048]{1,0:T(8,128)(2,1)S(1)}, bf16[32,2048]{1,0:T(8,128)(2,1)S(1)}, u32[]{:S(2)}, u32[]{:S(2)}) collective-permute-start(bf16[32,2048]{1,0:T(8,128)(2,1)S(1)} %get-tuple-element.52.refs_0_), channel_id=1, source_target_pairs={{0,2},{1,3},{2,0},{3,1},{4,6},{5,7},{6,4},{7,5},{8,10},{9,11},{10,... | collective-permute-start | bytes 393224 | tf_op jit(solution)/shard_map/ppermute | solution.py:19
  35.1 4.5 %collective-permute-start.13 = (bf16[32,2048]{1,0:T(8,128)(2,1)S(1)}, bf16[32,2048]{1,0:T(8,128)(2,1)S(1)}, u32[]{:S(2)}, u32[]{:S(2)}) collective-permute-start(bf16[32,2048]{1,0:T(8,128)(2,1)S(1)} %get-tuple-element.52.refs_0_), channel_id=1, source_target_pairs={{0,1},{1,0},{2,3},{3,2},{4,5},{5,4},{6,7},{7,6},{8,9},{9,8},{10,11... | collective-permute-start | bytes 393224 | tf_op jit(solution)/shard_map/ppermute | solution.py:19
  39.6 1.3 %collective-permute-start.14 = (bf16[32,2048]{1,0:T(8,128)(2,1)S(1)}, bf16[32,2048]{1,0:T(8,128)(2,1)S(1)}, u32[]{:S(2)}, u32[]{:S(2)}) collective-permute-start(bf16[32,2048]{1,0:T(8,128)(2,1)S(1)} %collective-permute-done.12.refs_1_), channel_id=1, source_target_pairs={{0,1},{1,0},{2,3},{3,2},{4,5},{5,4},{6,7},{7,6},{8,9},{9,8},{10,11... | collective-permute-start | bytes 393224 | tf_op jit(solution)/shard_map/ppermute | solution.py:19
  42.5 12.9 %collective-permute-start.15 = (bf16[32,2048]{1,0:T(8,128)(2,1)S(1)}, bf16[32,2048]{1,0:T(8,128)(2,1)S(1)}, u32[]{:S(2)}, u32[]{:S(2)}) collective-permute-start(bf16[32,2048]{1,0:T(8,128)(2,1)S(1)} %get-tuple-element.54), channel_id=1, source_target_pairs={{0,8},{4,12},{8,0},{12,4},{1,9},{5,13},{9,1},{13,5},{2,10},{6,14},... | collective-permute-start | bytes 393224 | tf_op jit(solution)/shard_map/ppermute | solution.py:19
  45.4 10.1 %collective-permute-start.16 = (bf16[32,2048]{1,0:T(8,128)(2,1)S(1)}, bf16[32,2048]{1,0:T(8,128)(2,1)S(1)}, u32[]{:S(2)}, u32[]{:S(2)}) collective-permute-start(bf16[32,2048]{1,0:T(8,128)(2,1)S(1)} %get-tuple-element.55), channel_id=1, source_target_pairs={{0,12},{4,8},{8,4},{12,0},{1,13},{5,9},{9,5},{13,1},{2,14},{6,10},... | collective-permute-start | bytes 393224 | tf_op jit(solution)/shard_map/ppermute | solution.py:19
  46.7 9.5 %collective-permute-start.17 = (bf16[32,2048]{1,0:T(8,128)(2,1)S(1)}, bf16[32,2048]{1,0:T(8,128)(2,1)S(1)}, u32[]{:S(2)}, u32[]{:S(2)}) collective-permute-start(bf16[32,2048]{1,0:T(8,128)(2,1)S(1)} %get-tuple-element.56), channel_id=1, source_target_pairs={{0,4},{4,0},{8,12},{12,8},{1,5},{5,1},{9,13},{13,9},{2,6},{6,2},{1... | collective-permute-start | bytes 393224 | tf_op jit(solution)/shard_map/ppermute | solution.py:19

commit v4 on v3

--- a/solution.py
+++ b/solution.py
@@ -161,7 +161,7 @@
     project_tiles(scaled, weights, keep, send)
 
 
-def add_body(unit, with_squares, keep, got, *refs):
+def add_body(unit, with_squares, cuts, keep, got, *refs):
     width = keep.shape[1]
     if with_squares:
         squares, own, own_squares, *sends = refs
@@ -169,11 +169,14 @@
         own_squares[...] = jnp.broadcast_to(total[:unit], own_squares.shape)
     else:
         own, *sends = refs
-    for cols in tiles(width):
-        own[:, cols] = keep[:unit, cols] + got[:unit, cols].astype(F32)
-        for p, send in enumerate(sends, 1):
-            part = slice(p * unit, (p + 1) * unit)
-            send[:, cols] = (keep[part, cols] + got[part, cols].astype(F32)).astype(BF16)
+    piece = width // cuts
+    for cols in tiles(piece):
+        for cut in range(cuts):
+            at = slice(cut * piece + cols.start, cut * piece + cols.stop)
+            own[:, at] = keep[:unit, at] + got[:unit, at].astype(F32)
+            for p, send in enumerate(sends[cut::cuts], 1):
+                part = slice(p * unit, (p + 1) * unit)
+                send[:, cols] = (keep[part, at] + got[part, at].astype(F32)).astype(BF16)
     if with_squares:
         for p, send in enumerate(sends, 1):
             send[:, width:] = split3(total[p * unit : (p + 1) * unit])
@@ -199,48 +202,48 @@
     lax.fori_loop(0, share, one, 0)
 
 
-def mix_body(share, peers, groups, conv, older, newer, squares, *refs):
-    gated, fresh = refs[-2:]
-    owns = refs[: len(groups)]
-    gots = [refs[at : at + peers] for at in range(len(groups), len(refs) - 2, peers)]
+def mix_body(share, peers, cut, conv, older, newer, squares, *refs):
+    owns, gots, (gated, fresh) = refs[:3], refs[3:-2], refs[-2:]
     width = gated.shape[1]
     total = squares[:, :1]
-    for got in gots[0]:
+    for got in gots[:peers]:
         total = total + join3(got[:, owns[0].shape[1] :])
     scale = lax.rsqrt(total / D + 1e-05)
     for cols in tiles(width):
+        at = slice(cut * width + cols.start, cut * width + cols.stop)
         gate = None
-        for g, group in enumerate(groups):
-            for at, j in enumerate(group):
-                spot = slice(at * width + cols.start, at * width + cols.stop)
-                new = owns[g][:, spot]
-                for got in gots[g]:
-                    new = new + got[:, spot].astype(F32)
-                new = (new * scale).astype(BF16)
-                new0, new1 = new[:share], new[share:]
-                fresh[j, 0, :, cols] = new0
-                fresh[j, 1, :, cols] = new1
-                new0, new1 = new0.astype(F32), new1.astype(F32)
-                last = conv[2, j : j + 1, cols]
-                mixed0 = older[j, :, cols] + last * new0
-                mixed1 = newer[j, :, cols] + conv[1, j : j + 1, cols] * new0 + last * new1
-                mixed = jnp.concatenate([mixed0, mixed1])
-                gate = mixed if gate is None else gate * mixed
+        for j in range(3):
+            new = owns[j][:, at]
+            for got in gots[j * peers : (j + 1) * peers]:
+                new = new + got[:, cols if j == 2 else at].astype(F32)
+            new = (new * scale).astype(BF16)
+            new0, new1 = new[:share], new[share:]
+            fresh[j, 0, :, cols] = new0
+            fresh[j, 1, :, cols] = new1
+            new0, new1 = new0.astype(F32), new1.astype(F32)
+            last = conv[2, j : j + 1, at]
+            mixed0 = older[j, :, at] + last * new0
+            mixed1 = newer[j, :, at] + conv[1, j : j + 1, at] * new0 + last * new1
+            mixed = jnp.concatenate([mixed0, mixed1])
+            gate = mixed if gate is None else gate * mixed
         gated[:, cols] = gate.astype(BF16)
 
 
-def out_body(n, share, rows, first, second, weight, *refs):
-    pieces, own, rest = refs[:n], refs[n], refs[n + 1 :]
+def out_body(n, cuts, share, rows, first, second, weight, *refs):
+    pieces, own, rest = refs[: n * cuts], refs[n * cuts], refs[n * cuts + 1 :]
+    blocks = range(0, first.shape[0], rows)
     lined = []
     for stage, picker in enumerate((first, second)):
         part = slice(stage * share, (stage + 1) * share)
-        every = jnp.concatenate([piece[part, :] for piece in pieces])
-        lined.append(
-            lax.dot_general(
-                picker[...], every, (((0,), (0,)), ((), ())), preferred_element_type=F32
-            ).astype(BF16)
-        )
-    blocks = range(0, first.shape[0], rows)
+        sides = []
+        for cut in range(cuts):
+            every = jnp.concatenate([piece[part, :] for piece in pieces[cut * n : (cut + 1) * n]])
+            sides.append(
+                lax.dot_general(
+                    picker[...], every, (((0,), (0,)), ((), ())), preferred_element_type=F32
+                ).astype(BF16)
+            )
+        lined.append(jnp.concatenate(sides, axis=1))
     lined = jnp.concatenate([part[at : at + rows] for at in blocks for part in lined])
     block = own.shape[0]
     for cols in tiles(weight.shape[1]):
@@ -306,36 +309,46 @@
                 [scaled, *(weights[j] for j in group)],
                 flops=cost * len(group),
             )
+        cuts = 2 if len(owns) == 2 and chans % (2 * LANES) == 0 else 1
         extra = [squares] if first else []
         kept = [struct(unit, width, dtype=F32)] + [struct(unit, LANES, dtype=F32)] * len(extra)
         result = call(
-            functools.partial(add_body, unit, first),
-            kept + [struct(unit, wider)] * (n // 2 - 1),
+            functools.partial(add_body, unit, first, cuts),
+            kept + [struct(unit, wider // cuts)] * ((n // 2 - 1) * cuts),
             [keep, swap(send, "narrow", 1), *extra],
         )
         owns.append(result[0])
         if first:
             squares = result[1]
-        gots += [swap(p, "narrow", k) for p, k in zip(result[len(kept) :], evens[1:])]
-    gated, fresh = call(
-        functools.partial(mix_body, share, n // 2 - 1, GROUPS),
-        [struct(unit, chans), struct(3, 2, share, chans)],
-        [conv_weight, older, newer, squares, *owns, *gots],
-    )
-    near = [swap(gated, "narrow", k) if k else gated for k in evens]
-    far = [swap(piece, "narrow", 1) for piece in near]
+        leaving = result[len(kept) :]
+        gots += [
+            [swap(p, "narrow", k) for p, k in zip(leaving[cut::cuts], evens[1:])]
+            for cut in range(cuts)
+        ]
+    fresh, near, far = [], [], []
+    for cut in range(cuts):
+        gated, part = call(
+            functools.partial(mix_body, share, n // 2 - 1, cut),
+            [struct(unit, chans // cuts), struct(3, 2, share, chans // cuts)],
+            [conv_weight, older, newer, squares, *owns, *gots[0], *gots[1], *gots[2 + cut]],
+        )
+        fresh.append(part)
+        near.append([swap(gated, "narrow", k) if k else gated for k in evens])
+        far.append([swap(piece, "narrow", 1) for piece in near[-1]])
+    fresh = jnp.concatenate(fresh, axis=3)
+    pieces = [piece for cut in range(cuts) for piece in near[cut] + far[cut]]
     block = steps * rows
     shapes = [struct(steps * total, outs)]
     if direct:
         shapes = [struct(block, outs, dtype=F32)] + [struct(block, outs)] * (wide - 1)
     out, *parts = call(
-        functools.partial(out_body, n, share, rows),
+        functools.partial(out_body, n, cuts, share, rows),
         shapes,
-        [*pickers, out_weight, *near, *far],
+        [*pickers, out_weight, *pieces],
         flops=2 * steps * total * chans * outs,
     )
     if direct:
-        for k in order:
+        for k in [k for k in (2, 1, 3) if k < wide]:
             out = out + swap(parts[k - 1], "wide", k).astype(F32)
         out = out.astype(BF16)
     else:

time: 57 us -> 56.6 us (level)
  waiting for transfers between devices: 21.8 us -> 16.7 us
  starting transfers between devices: 16.1 us -> 20.5 us
    ppermute x18 -> x22, waiting for transfers between devices: 21.8 us -> 16.7 us  [swap(): return lax.ppermute(value, axis, [(i, i ^ hop) for i in range(count)])]
    ppermute x18 -> x22, starting transfers between devices: 16.1 us -> 20.5 us  [swap(): return lax.ppermute(value, axis, [(i, i ^ hop) for i in range(count)])]
    pallas_call x9 -> x10, Pallas kernels: 7.41 us -> 7.6 us  [call(): pl.pallas_call(body, out_shape=outs, in_specs=[small] * scalars + [whole]...]
    unnamed x17 -> x15, local copies, waits for them, and re-layouts: 1.86 us -> 1.85 us
  transfers between devices with their start and end apart: 18 -> 22, of which waited for: 6 -> 8; matrix products, arithmetic and copies ran while one was open for 2% -> 2% of each run, Pallas kernels for 24% -> 25%
where the time goes in v4:
time: 56.6 us; the launch traced here: 56.4 us
  starting transfers between devices  20.5 us (36%)
  waiting for transfers between devices  16.7 us (30%)
  Pallas kernels  15.8 us (28%)
  local copies, waits for them, and re-layouts  1.85 us (3%)
  between operations  0.78 us (1%)
  other arithmetic  0.75 us (1%)
    ppermute x22, starting transfers between devices, swap(): return lax.ppermute(value, axis, [(i, i ^ hop) for i in range(count)])  20.5 us
    ppermute x22, waiting for transfers between devices, swap(): return lax.ppermute(value, axis, [(i, i ^ hop) for i in range(count)])  16.7 us
    pallas_call x1, Pallas kernels, load(): pl.pallas_call(functools.partial(load_body, n, share, rows, direct), out_...  8.23 us
    pallas_call x10, Pallas kernels, call(): pl.pallas_call(body, out_shape=outs, in_specs=[small] * scalars + [whole]...  7.6 us
    unnamed x15, local copies, waits for them, and re-layouts  1.85 us
  transfers between devices with their start and end apart: 22, of which 8 were waited for; matrix products, arithmetic and copies ran while one was open for 2% of the time, Pallas kernels for 25%

profile of v4, /device:TPU:0, one launch (start us, length us, event | category | flops | bytes accessed | tf_op | source)
XLA Modules:
  0.0 56.4 jit_solution(16026228538583180660)
XLA Ops:
  0.6 3.0 %collective-permute-start.1 = (bf16[16,3,2,2048]{3,2,1,0:T(2,128)(2,1)}, bf16[16,3,2,2048]{3,2,1,0:T(2,128)(2,1)S(1)}, u32[]{:S(2)}, u32[]{:S(2)}) collective-permute-start(bf16[16,3,2,2048]{3,2,1,0:T(2,128)(2,1)} %bitcast.9), channel_id=1, source_target_pairs={{0,2},{1,3},{2,0},{3,1},{4,6},{5,7},{6,4},{7,5},{8,10},{9,11},{10,... | collective-permute-start | bytes 1179656 | tf_op jit(solution)/shard_map/ppermute | solution.py:19
  3.6 2.6 %collective-permute-start.3 = (bf16[32,2048]{1,0:T(8,128)(2,1)}, bf16[32,2048]{1,0:T(8,128)(2,1)S(1)}, u32[]{:S(2)}, u32[]{:S(2)}) collective-permute-start(bf16[32,2048]{1,0:T(8,128)(2,1)} %bitcast.12), channel_id=1, source_target_pairs={{0,8},{4,12},{8,0},{12,4},{1,9},{5,13},{9,1},{13,5},{2,10},{6,14},... | collective-permute-start | bytes 393224 | tf_op jit(solution)/shard_map/ppermute | solution.py:19
  6.2 1.3 %collective-permute-start.4 = (bf16[32,2048]{1,0:T(8,128)(2,1)}, bf16[32,2048]{1,0:T(8,128)(2,1)S(1)}, u32[]{:S(2)}, u32[]{:S(2)}) collective-permute-start(bf16[32,2048]{1,0:T(8,128)(2,1)} %bitcast.13), channel_id=1, source_target_pairs={{0,12},{4,8},{8,4},{12,0},{1,13},{5,9},{9,5},{13,1},{2,14},{6,10},... | collective-permute-start | bytes 393224 | tf_op jit(solution)/shard_map/ppermute | solution.py:19
  7.6 0.2 collective-permute-start.5
  7.8 0.0 collective-permute-start
  7.8 0.7 %copy-done.4 = s32[2,64]{1,0:T(2,128)S(1)} copy-done((s32[2,64]{1,0:T(2,128)S(1)}, s32[2,64]{1,0:T(2,128)}, u32[]{:S(2)}) %copy-start.4) | copy-done | bytes 536
  8.5 8.2 %shard_map.86 = (bf16[64,64]{1,0:T(8,128)(2,1)S(1)}, bf16[64,64]{1,0:T(8,128)(2,1)S(1)}, bf16[2048,2048]{1,0:T(8,128)(2,1)S(1)}, bf16[2048,2048]{1,0:T(8,128)(2,1)S(1)}, bf16[2048,2048]{1,0:T(8,128)(2,1)S(1)}) custom-call(s32[2,64]{1,0:T(2,128)S(1)} %copy-done.4, bf16[3,2048,2048]{2,1,0:T(8,128)(2,1)} %bitcast.17), custom_call_target="tpu_custom_call" | custom-call | bytes 50331648 | tf_op jit(solution)/shard_map/pallas_call | solution.py:88
  16.7 0.0 collective-permute-done.3.refs_1_
  16.7 0.0 collective-permute-done.4.refs_2_
  16.7 0.0 collective-permute-done.5.refs_3_
  16.8 0.0 copy-done.2
  16.8 0.0 copy-done.3
  16.8 1.5 %shard_map.88 = (bf16[128,2048]{1,0:T(8,128)(2,1)S(1)}, f32[64,2048]{1,0:T(8,128)S(1)}, bf16[64,2176]{1,0:T(8,128)(2,1)S(1)}, f32[64,128]{1,0:T(8,128)S(1)}) custom-call(bf16[64,64]{1,0:T(8,128)(2,1)S(1)} %get-tuple-element.33.first, bf16[64,64]{1,0:T(8,128)(2,1)S(1)} %get-tuple-element.34.second, f32[1,2048]{1,0:T(1,128)S(1)} %bitcast.16, ...), custom_call_target="tpu_custom_call" | custom-call | flops 1073741824 | bytes 10297344 | tf_op jit(solution)/shard_map/pallas_call | solution.py:26
  18.3 0.6 collective-permute-start.6
  18.9 1.3 %shard_map.90 = (f32[64,2048]{1,0:T(8,128)S(1)}, bf16[64,2048]{1,0:T(8,128)(2,1)S(1)}) custom-call(bf16[128,2048]{1,0:T(8,128)(2,1)S(1)} %get-tuple-element.43.scaled, bf16[2048,2048]{1,0:T(8,128)(2,1)S(1)} %get-tuple-element.44.refs_0_), custom_call_target="tpu_custom_call" | custom-call | flops 1073741824 | bytes 9699328 | tf_op jit(solution)/shard_map/pallas_call | solution.py:26
  20.2 0.1 collective-permute-start.7
  20.3 0.0 collective-permute-done.1.refs_2_
  20.3 0.5 collective-permute-start.2
  20.7 1.3 %shard_map.92 = (f32[64,2048]{1,0:T(8,128)S(1)}, bf16[64,2048]{1,0:T(8,128)(2,1)S(1)}) custom-call(bf16[128,2048]{1,0:T(8,128)(2,1)S(1)} %get-tuple-element.43.scaled, bf16[2048,2048]{1,0:T(8,128)(2,1)S(1)} %get-tuple-element.48.refs_0_), custom_call_target="tpu_custom_call" | custom-call | flops 1073741824 | bytes 9699328 | tf_op jit(solution)/shard_map/pallas_call | solution.py:26
  22.1 0.1 collective-permute-start.8
  22.2 0.0 collective-permute-done.6.got
  22.2 0.2 shard_map.89
  22.4 0.6 %collective-permute-start.9 = (bf16[32,2176]{1,0:T(8,128)(2,1)S(1)}, bf16[32,2176]{1,0:T(8,128)(2,1)S(1)}, u32[]{:S(2)}, u32[]{:S(2)}) collective-permute-start(bf16[32,2176]{1,0:T(8,128)(2,1)S(1)} %get-tuple-element.52), channel_id=1, source_target_pairs={{0,2},{1,3},{2,0},{3,1},{4,6},{5,7},{6,4},{7,5},{8,10},{9,11},{10,... | collective-permute-start | bytes 417800 | tf_op jit(solution)/shard_map/ppermute | solution.py:19
  23.0 0.0 collective-permute-done.7.got
  23.0 0.1 shard_map.91
  23.1 1.6 %collective-permute-start.10 = (bf16[32,2048]{1,0:T(8,128)(2,1)S(1)}, bf16[32,2048]{1,0:T(8,128)(2,1)S(1)}, u32[]{:S(2)}, u32[]{:S(2)}) collective-permute-start(bf16[32,2048]{1,0:T(8,128)(2,1)S(1)} %get-tuple-element.53), channel_id=1, source_target_pairs={{0,2},{1,3},{2,0},{3,1},{4,6},{5,7},{6,4},{7,5},{8,10},{9,11},{10,... | collective-permute-start | bytes 393224 | tf_op jit(solution)/shard_map/ppermute | solution.py:19
  24.6 0.0 collective-permute-done.8.got
  24.6 0.1 shard_map.93
  24.7 0.6 %collective-permute-start.15 = (bf16[32,1024]{1,0:T(8,128)(2,1)S(1)}, bf16[32,1024]{1,0:T(8,128)(2,1)S(1)}, u32[]{:S(2)}, u32[]{:S(2)}) collective-permute-start(bf16[32,1024]{1,0:T(8,128)(2,1)S(1)} %get-tuple-element.56), channel_id=1, source_target_pairs={{0,2},{1,3},{2,0},{3,1},{4,6},{5,7},{6,4},{7,5},{8,10},{9,11},{10,... | collective-permute-start | bytes 196616 | tf_op jit(solution)/shard_map/ppermute | solution.py:19
  25.3 0.0 collective-permute-done.refs_1_
  25.3 1.5 %collective-permute-start.11 = (bf16[32,1024]{1,0:T(8,128)(2,1)S(1)}, bf16[32,1024]{1,0:T(8,128)(2,1)S(1)}, u32[]{:S(2)}, u32[]{:S(2)}) collective-permute-start(bf16[32,1024]{1,0:T(8,128)(2,1)S(1)} %get-tuple-element.54), channel_id=1, source_target_pairs={{0,2},{1,3},{2,0},{3,1},{4,6},{5,7},{6,4},{7,5},{8,10},{9,11},{10,... | collective-permute-start | bytes 196616 | tf_op jit(solution)/shard_map/ppermute | solution.py:19
  26.8 0.0 collective-permute-done.2.refs_3_
  26.8 0.0 copy-done
  26.8 0.0 copy-done.1
  26.8 1.2 %shard_map.87 = (f32[3,16,2048]{2,1,0:T(8,128)S(1)}, f32[3,16,2048]{2,1,0:T(8,128)S(1)}) custom-call(s32[2,64]{1,0:T(2,128)S(1)} %copy-done.4, f32[3,3,2048]{2,1,0:T(4,128)S(1)} %copy-done, bf16[16,3,2,2048]{3,2,1,0:T(2,128)(2,1)S(1)} %bitcast.11, bf16[16,3,2,2048]{3,2,1,0:T(2,128)(2,1)S(1)} %collective-permute-done.refs_1_, ...), custom_call_target="tpu_custom_call" | custom-call | bytes 2433536 | tf_op jit(solution)/shard_map/pallas_call | solution.py:26
  28.0 5.2 %collective-permute-done.15.refs_5_ = bf16[32,1024]{1,0:T(8,128)(2,1)S(1)} collective-permute-done((bf16[32,1024]{1,0:T(8,128)(2,1)S(1)}, bf16[32,1024]{1,0:T(8,128)(2,1)S(1)}, u32[]{:S(2)}, u32[]{:S(2)}) %collective-permute-start.15) | collective-permute-done | bytes 65568 | tf_op jit(solution)/shard_map/ppermute | solution.py:19
  33.2 0.0 collective-permute-done.10.refs_4_
  33.2 0.0 collective-permute-done.9.refs_3_
  33.2 0.3 shard_map.95
  33.4 0.6 %collective-permute-start.16 = (bf16[32,1024]{1,0:T(8,128)(2,1)S(1)}, bf16[32,1024]{1,0:T(8,128)(2,1)S(1)}, u32[]{:S(2)}, u32[]{:S(2)}) collective-permute-start(bf16[32,1024]{1,0:T(8,128)(2,1)S(1)} %get-tuple-element.57.refs_4_), channel_id=1, source_target_pairs={{0,2},{1,3},{2,0},{3,1},{4,6},{5,7},{6,4},{7,5},{8,10},{9,11},{10,... | collective-permute-start | bytes 196616 | tf_op jit(solution)/shard_map/ppermute | solution.py:19
  34.1 0.1 collective-permute-done.11.refs_5_
  34.1 0.3 shard_map.94
  34.4 1.5 %collective-permute-start.12 = (bf16[32,1024]{1,0:T(8,128)(2,1)S(1)}, bf16[32,1024]{1,0:T(8,128)(2,1)S(1)}, u32[]{:S(2)}, u32[]{:S(2)}) collective-permute-start(bf16[32,1024]{1,0:T(8,128)(2,1)S(1)} %get-tuple-element.55.refs_0_), channel_id=1, source_target_pairs={{0,2},{1,3},{2,0},{3,1},{4,6},{5,7},{6,4},{7,5},{8,10},{9,11},{10,... | collective-permute-start | bytes 196616 | tf_op jit(solution)/shard_map/ppermute | solution.py:19
  35.9 0.0 collective-permute-start.17
  35.9 0.5 collective-permute-start.13
  36.4 1.7 %collective-permute-done.16.refs_5_ = bf16[32,1024]{1,0:T(8,128)(2,1)S(1)} collective-permute-done((bf16[32,1024]{1,0:T(8,128)(2,1)S(1)}, bf16[32,1024]{1,0:T(8,128)(2,1)S(1)}, u32[]{:S(2)}, u32[]{:S(2)}) %collective-permute-start.16) | collective-permute-done | bytes 65568 | tf_op jit(solution)/shard_map/ppermute | solution.py:19
  38.1 0.0 collective-permute-start.18
  38.1 0.7 %collective-permute-done.12.refs_1_ = bf16[32,1024]{1,0:T(8,128)(2,1)S(1)} collective-permute-done((bf16[32,1024]{1,0:T(8,128)(2,1)S(1)}, bf16[32,1024]{1,0:T(8,128)(2,1)S(1)}, u32[]{:S(2)}, u32[]{:S(2)}) %collective-permute-start.12) | collective-permute-done | bytes 65568 | tf_op jit(solution)/shard_map/ppermute | solution.py:19
  38.8 0.0 collective-permute-start.14
  38.8 0.0 collective-permute-done.17.refs_6_
  38.8 0.0 collective-permute-done.13.refs_2_
  38.8 0.5 collective-permute-done.18.refs_7_
  39.4 0.7 %collective-permute-done.14.refs_3_ = bf16[32,1024]{1,0:T(8,128)(2,1)S(1)} collective-permute-done((bf16[32,1024]{1,0:T(8,128)(2,1)S(1)}, bf16[32,1024]{1,0:T(8,128)(2,1)S(1)}, u32[]{:S(2)}, u32[]{:S(2)}) %collective-permute-start.14) | collective-permute-done | bytes 65568 | tf_op jit(solution)/shard_map/ppermute | solution.py:19
  40.1 0.0 slice-done
  40.1 0.0 slice-done.1
  40.1 1.5 %shard_map.96 = (f32[32,2048]{1,0:T(8,128)S(1)}, bf16[32,2048]{1,0:T(8,128)(2,1)S(1)}, bf16[32,2048]{1,0:T(8,128)(2,1)S(1)}, bf16[32,2048]{1,0:T(8,128)(2,1)S(1)}) custom-call(bf16[64,64]{1,0:T(8,128)(2,1)S(1)} %get-tuple-element.33.first, bf16[64,64]{1,0:T(8,128)(2,1)S(1)} %get-tuple-element.34.second, bf16[2048,2048]{1,0:T(8,128)(2,1)S(1)} %bitcast.8, ...), custom_call_target="tpu_custom_call" | custom-call | flops 1073741824 | bytes 9584640 | tf_op jit(solution)/shard_map/pallas_call | solution.py:26
  41.6 3.7 %collective-permute-start.19 = (bf16[32,2048]{1,0:T(8,128)(2,1)S(1)}, bf16[32,2048]{1,0:T(8,128)(2,1)S(1)}, u32[]{:S(2)}, u32[]{:S(2)}) collective-permute-start(bf16[32,2048]{1,0:T(8,128)(2,1)S(1)} %get-tuple-element.59), channel_id=1, source_target_pairs={{0,8},{4,12},{8,0},{12,4},{1,9},{5,13},{9,1},{13,5},{2,10},{6,14},... | collective-permute-start | bytes 393224 | tf_op jit(solution)/shard_map/ppermute | solution.py:19
  45.2 0.0 collective-permute-start.20
  45.3 1.5 %collective-permute-start.21 = (bf16[32,2048]{1,0:T(8,128)(2,1)S(1)}, bf16[32,2048]{1,0:T(8,128)(2,1)S(1)}, u32[]{:S(2)}, u32[]{:S(2)}) collective-permute-start(bf16[32,2048]{1,0:T(8,128)(2,1)S(1)} %get-tuple-element.61), channel_id=1, source_target_pairs={{0,12},{4,8},{8,4},{12,0},{1,13},{5,9},{9,5},{13,1},{2,14},{6,10},... | collective-permute-start | bytes 393224 | tf_op jit(solution)/shard_map/ppermute | solution.py:19
  46.8 1.2 %copy.9 = bf16[16,2,3,2048]{3,1,2,0:T(2,128)(2,1)} copy(bf16[16,2,3,2048]{3,0,1,2:T(8,128)(2,1)S(1)} %maximum_bitcast_fusion) | data formatting | bytes 786432
  48.0 5.1 %collective-permute-done.19 = bf16[32,2048]{1,0:T(8,128)(2,1)S(1)} collective-permute-done((bf16[32,2048]{1,0:T(8,128)(2,1)S(1)}, bf16[32,2048]{1,0:T(8,128)(2,1)S(1)}, u32[]{:S(2)}, u32[]{:S(2)}) %collective-permute-start.19) | collective-permute-done | bytes 131104 | tf_op jit(solution)/shard_map/ppermute | solution.py:19
  53.1 2.7 %collective-permute-done.20 = bf16[32,2048]{1,0:T(8,128)(2,1)S(1)} collective-permute-done((bf16[32,2048]{1,0:T(8,128)(2,1)S(1)}, bf16[32,2048]{1,0:T(8,128)(2,1)S(1)}, u32[]{:S(2)}, u32[]{:S(2)}) %collective-permute-start.20) | collective-permute-done | bytes 131104 | tf_op jit(solution)/shard_map/ppermute | solution.py:19
  55.7 0.0 collective-permute-done.21
  55.7 0.7 %add_convert_fusion = bf16[32,2048]{1,0:T(8,128)(2,1)} fusion(bf16[32,2048]{1,0:T(8,128)(2,1)S(1)} %collective-permute-done.21, bf16[32,2048]{1,0:T(8,128)(2,1)S(1)} %collective-permute-done.20, f32[32,2048]{1,0:T(8,128)S(1)} %get-tuple-element.58, bf16[32,2048]{1,0:T(8,128)(2,1)S(1)} %collective-permute-done.19), kind=kLoop, calls=%fused_computation.1 | loop fusion | flops 458752 | bytes 786432 | tf_op jit(solution)/shard_map/convert_element_type | solution.py:353
  (9 shorter events, 0.0 us)
Async XLA Ops:
  0.6 19.6 %collective-permute-start.1 = (bf16[16,3,2,2048]{3,2,1,0:T(2,128)(2,1)}, bf16[16,3,2,2048]{3,2,1,0:T(2,128)(2,1)S(1)}, u32[]{:S(2)}, u32[]{:S(2)}) collective-permute-start(bf16[16,3,2,2048]{3,2,1,0:T(2,128)(2,1)} %bitcast.9), channel_id=1, source_target_pairs={{0,2},{1,3},{2,0},{3,1},{4,6},{5,7},{6,4},{7,5},{8,10},{9,11},{10,... | collective-permute-start | bytes 1179656 | tf_op jit(solution)/shard_map/ppermute | solution.py:19
  3.6 13.1 %collective-permute-start.3 = (bf16[32,2048]{1,0:T(8,128)(2,1)}, bf16[32,2048]{1,0:T(8,128)(2,1)S(1)}, u32[]{:S(2)}, u32[]{:S(2)}) collective-permute-start(bf16[32,2048]{1,0:T(8,128)(2,1)} %bitcast.12), channel_id=1, source_target_pairs={{0,8},{4,12},{8,0},{12,4},{1,9},{5,13},{9,1},{13,5},{2,10},{6,14},... | collective-permute-start | bytes 393224 | tf_op jit(solution)/shard_map/ppermute | solution.py:19
  6.2 10.5 %collective-permute-start.4 = (bf16[32,2048]{1,0:T(8,128)(2,1)}, bf16[32,2048]{1,0:T(8,128)(2,1)S(1)}, u32[]{:S(2)}, u32[]{:S(2)}) collective-permute-start(bf16[32,2048]{1,0:T(8,128)(2,1)} %bitcast.13), channel_id=1, source_target_pairs={{0,12},{4,8},{8,4},{12,0},{1,13},{5,9},{9,5},{13,1},{2,14},{6,10},... | collective-permute-start | bytes 393224 | tf_op jit(solution)/shard_map/ppermute | solution.py:19
  7.6 9.2 %collective-permute-start.5 = (bf16[32,2048]{1,0:T(8,128)(2,1)}, bf16[32,2048]{1,0:T(8,128)(2,1)S(1)}, u32[]{:S(2)}, u32[]{:S(2)}) collective-permute-start(bf16[32,2048]{1,0:T(8,128)(2,1)} %bitcast.14), channel_id=1, source_target_pairs={{0,4},{4,0},{8,12},{12,8},{1,5},{5,1},{9,13},{13,9},{2,6},{6,2},{1... | collective-permute-start | bytes 393224 | tf_op jit(solution)/shard_map/ppermute | solution.py:19
  7.8 17.5 %collective-permute-start = (bf16[16,3,2,2048]{3,2,1,0:T(2,128)(2,1)}, bf16[16,3,2,2048]{3,2,1,0:T(2,128)(2,1)S(1)}, u32[]{:S(2)}, u32[]{:S(2)}) collective-permute-start(bf16[16,3,2,2048]{3,2,1,0:T(2,128)(2,1)} %bitcast.10), channel_id=1, source_target_pairs={{0,1},{1,0},{2,3},{3,2},{4,5},{5,4},{6,7},{7,6},{8,9},{9,8},{10,11... | collective-permute-start | bytes 1179656 | tf_op jit(solution)/shard_map/ppermute | solution.py:19
  7.8 0.7 %copy-start.4 = (s32[2,64]{1,0:T(2,128)S(1)}, s32[2,64]{1,0:T(2,128)}, u32[]{:S(2)}) copy-start(s32[2,64]{1,0:T(2,128)} %assign.3) | copy-start | bytes 1540
  8.5 8.3 %copy-start.2 = (bf16[2,16,2048]{2,1,0:T(8,128)(2,1)S(1)}, bf16[2,16,2048]{2,1,0:T(8,128)(2,1)}, u32[]{:S(2)}) copy-start(bf16[2,16,2048]{2,1,0:T(8,128)(2,1)} %param.7) | copy-start | bytes 393220
  8.5 8.3 %copy-start.3 = (f32[2048]{0:T(1024)S(1)}, f32[2048]{0:T(1024)}, u32[]{:S(2)}) copy-start(f32[2048]{0:T(1024)} %param.10) | copy-start | bytes 24580
  18.3 3.9 %collective-permute-start.6 = (bf16[64,2176]{1,0:T(8,128)(2,1)S(1)}, bf16[64,2176]{1,0:T(8,128)(2,1)S(1)}, u32[]{:S(2)}, u32[]{:S(2)}) collective-permute-start(bf16[64,2176]{1,0:T(8,128)(2,1)S(1)} %get-tuple-element.39), channel_id=1, source_target_pairs={{0,1},{1,0},{2,3},{3,2},{4,5},{5,4},{6,7},{7,6},{8,9},{9,8},{10,11... | collective-permute-start | bytes 835592 | tf_op jit(solution)/shard_map/ppermute | solution.py:19
  18.9 7.9 %copy-start = (f32[3,3,2048]{2,1,0:T(4,128)S(1)}, f32[3,3,2048]{2,1,0:T(4,128)}, u32[]{:S(2)}) copy-start(f32[3,3,2048]{2,1,0:T(4,128)} %conv.5) | copy-start | bytes 221188
  18.9 7.9 %copy-start.1 = (bf16[16,2,3,2048]{3,1,2,0:T(2,128)(2,1)S(1)}, bf16[16,2,3,2048]{3,1,2,0:T(2,128)(2,1)}, u32[]{:S(2)}) copy-start(bf16[16,2,3,2048]{3,1,2,0:T(2,128)(2,1)} %param.9) | copy-start | bytes 1179652
  20.2 2.8 %collective-permute-start.7 = (bf16[64,2048]{1,0:T(8,128)(2,1)S(1)}, bf16[64,2048]{1,0:T(8,128)(2,1)S(1)}, u32[]{:S(2)}, u32[]{:S(2)}) collective-permute-start(bf16[64,2048]{1,0:T(8,128)(2,1)S(1)} %get-tuple-element.46), channel_id=1, source_target_pairs={{0,1},{1,0},{2,3},{3,2},{4,5},{5,4},{6,7},{7,6},{8,9},{9,8},{10,11... | collective-permute-start | bytes 786440 | tf_op jit(solution)/shard_map/ppermute | solution.py:19
  20.3 6.5 %collective-permute-start.2 = (bf16[16,3,2,2048]{3,2,1,0:T(2,128)(2,1)S(1)}, bf16[16,3,2,2048]{3,2,1,0:T(2,128)(2,1)S(1)}, u32[]{:S(2)}, u32[]{:S(2)}) collective-permute-start(bf16[16,3,2,2048]{3,2,1,0:T(2,128)(2,1)S(1)} %collective-permute-done.1.refs_2_), channel_id=1, source_target_pairs={{0,1},{1,0},{2,3},{3,2},{4,5},{5,4},{6,7},{7,6},{8,9},{9,8},{10,11... | collective-permute-start | bytes 1179656 | tf_op jit(solution)/shard_map/ppermute | solution.py:19
  20.7 19.3 %slice-start = ((s8[8388608]{0:T(1024)(128)(4,1)}), s8[4194304]{0:T(1024)(128)(4,1)S(1)}, s32[]{:S(2)}) async-start(s8[8388608]{0:T(1024)(128)(4,1)} %bitcast.7), calls=%async_computation | async-start | bytes 8388608
  20.7 19.3 %slice-start.1 = ((s8[8388608]{0:T(1024)(128)(4,1)}), s8[4194304]{0:T(1024)(128)(4,1)S(1)}, s32[]{:S(2)}) async-start(s8[8388608]{0:T(1024)(128)(4,1)} %bitcast.7), calls=%async_computation.1 | async-start | bytes 8388608
  22.1 2.6 %collective-permute-start.8 = (bf16[64,2048]{1,0:T(8,128)(2,1)S(1)}, bf16[64,2048]{1,0:T(8,128)(2,1)S(1)}, u32[]{:S(2)}, u32[]{:S(2)}) collective-permute-start(bf16[64,2048]{1,0:T(8,128)(2,1)S(1)} %get-tuple-element.50), channel_id=1, source_target_pairs={{0,1},{1,0},{2,3},{3,2},{4,5},{5,4},{6,7},{7,6},{8,9},{9,8},{10,11... | collective-permute-start | bytes 786440 | tf_op jit(solution)/shard_map/ppermute | solution.py:19
  22.4 10.8 %collective-permute-start.9 = (bf16[32,2176]{1,0:T(8,128)(2,1)S(1)}, bf16[32,2176]{1,0:T(8,128)(2,1)S(1)}, u32[]{:S(2)}, u32[]{:S(2)}) collective-permute-start(bf16[32,2176]{1,0:T(8,128)(2,1)S(1)} %get-tuple-element.52), channel_id=1, source_target_pairs={{0,2},{1,3},{2,0},{3,1},{4,6},{5,7},{6,4},{7,5},{8,10},{9,11},{10,... | collective-permute-start | bytes 417800 | tf_op jit(solution)/shard_map/ppermute | solution.py:19
  23.1 10.1 %collective-permute-start.10 = (bf16[32,2048]{1,0:T(8,128)(2,1)S(1)}, bf16[32,2048]{1,0:T(8,128)(2,1)S(1)}, u32[]{:S(2)}, u32[]{:S(2)}) collective-permute-start(bf16[32,2048]{1,0:T(8,128)(2,1)S(1)} %get-tuple-element.53), channel_id=1, source_target_pairs={{0,2},{1,3},{2,0},{3,1},{4,6},{5,7},{6,4},{7,5},{8,10},{9,11},{10,... | collective-permute-start | bytes 393224 | tf_op jit(solution)/shard_map/ppermute | solution.py:19
  24.7 8.5 %collective-permute-start.15 = (bf16[32,1024]{1,0:T(8,128)(2,1)S(1)}, bf16[32,1024]{1,0:T(8,128)(2,1)S(1)}, u32[]{:S(2)}, u32[]{:S(2)}) collective-permute-start(bf16[32,1024]{1,0:T(8,128)(2,1)S(1)} %get-tuple-element.56), channel_id=1, source_target_pairs={{0,2},{1,3},{2,0},{3,1},{4,6},{5,7},{6,4},{7,5},{8,10},{9,11},{10,... | collective-permute-start | bytes 196616 | tf_op jit(solution)/shard_map/ppermute | solution.py:19
  25.3 8.8 %collective-permute-start.11 = (bf16[32,1024]{1,0:T(8,128)(2,1)S(1)}, bf16[32,1024]{1,0:T(8,128)(2,1)S(1)}, u32[]{:S(2)}, u32[]{:S(2)}) collective-permute-start(bf16[32,1024]{1,0:T(8,128)(2,1)S(1)} %get-tuple-element.54), channel_id=1, source_target_pairs={{0,2},{1,3},{2,0},{3,1},{4,6},{5,7},{6,4},{7,5},{8,10},{9,11},{10,... | collective-permute-start | bytes 196616 | tf_op jit(solution)/shard_map/ppermute | solution.py:19
  33.4 4.6 %collective-permute-start.16 = (bf16[32,1024]{1,0:T(8,128)(2,1)S(1)}, bf16[32,1024]{1,0:T(8,128)(2,1)S(1)}, u32[]{:S(2)}, u32[]{:S(2)}) collective-permute-start(bf16[32,1024]{1,0:T(8,128)(2,1)S(1)} %get-tuple-element.57.refs_4_), channel_id=1, source_target_pairs={{0,2},{1,3},{2,0},{3,1},{4,6},{5,7},{6,4},{7,5},{8,10},{9,11},{10,... | collective-permute-start | bytes 196616 | tf_op jit(solution)/shard_map/ppermute | solution.py:19
  34.4 4.4 %collective-permute-start.12 = (bf16[32,1024]{1,0:T(8,128)(2,1)S(1)}, bf16[32,1024]{1,0:T(8,128)(2,1)S(1)}, u32[]{:S(2)}, u32[]{:S(2)}) collective-permute-start(bf16[32,1024]{1,0:T(8,128)(2,1)S(1)} %get-tuple-element.55.refs_0_), channel_id=1, source_target_pairs={{0,2},{1,3},{2,0},{3,1},{4,6},{5,7},{6,4},{7,5},{8,10},{9,11},{10,... | collective-permute-start | bytes 196616 | tf_op jit(solution)/shard_map/ppermute | solution.py:19
  35.9 2.9 %collective-permute-start.17 = (bf16[32,1024]{1,0:T(8,128)(2,1)S(1)}, bf16[32,1024]{1,0:T(8,128)(2,1)S(1)}, u32[]{:S(2)}, u32[]{:S(2)}) collective-permute-start(bf16[32,1024]{1,0:T(8,128)(2,1)S(1)} %get-tuple-element.57.refs_4_), channel_id=1, source_target_pairs={{0,1},{1,0},{2,3},{3,2},{4,5},{5,4},{6,7},{7,6},{8,9},{9,8},{10,11... | collective-permute-start | bytes 196616 | tf_op jit(solution)/shard_map/ppermute | solution.py:19
  35.9 2.9 %collective-permute-start.13 = (bf16[32,1024]{1,0:T(8,128)(2,1)S(1)}, bf16[32,1024]{1,0:T(8,128)(2,1)S(1)}, u32[]{:S(2)}, u32[]{:S(2)}) collective-permute-start(bf16[32,1024]{1,0:T(8,128)(2,1)S(1)} %get-tuple-element.55.refs_0_), channel_id=1, source_target_pairs={{0,1},{1,0},{2,3},{3,2},{4,5},{5,4},{6,7},{7,6},{8,9},{9,8},{10,11... | collective-permute-start | bytes 196616 | tf_op jit(solution)/shard_map/ppermute | solution.py:19
  38.1 1.3 %collective-permute-start.18 = (bf16[32,1024]{1,0:T(8,128)(2,1)S(1)}, bf16[32,1024]{1,0:T(8,128)(2,1)S(1)}, u32[]{:S(2)}, u32[]{:S(2)}) collective-permute-start(bf16[32,1024]{1,0:T(8,128)(2,1)S(1)} %collective-permute-done.16.refs_5_), channel_id=1, source_target_pairs={{0,1},{1,0},{2,3},{3,2},{4,5},{5,4},{6,7},{7,6},{8,9},{9,8},{10,11... | collective-permute-start | bytes 196616 | tf_op jit(solution)/shard_map/ppermute | solution.py:19
  38.8 1.3 %collective-permute-start.14 = (bf16[32,1024]{1,0:T(8,128)(2,1)S(1)}, bf16[32,1024]{1,0:T(8,128)(2,1)S(1)}, u32[]{:S(2)}, u32[]{:S(2)}) collective-permute-start(bf16[32,1024]{1,0:T(8,128)(2,1)S(1)} %collective-permute-done.12.refs_1_), channel_id=1, source_target_pairs={{0,1},{1,0},{2,3},{3,2},{4,5},{5,4},{6,7},{7,6},{8,9},{9,8},{10,11... | collective-permute-start | bytes 196616 | tf_op jit(solution)/shard_map/ppermute | solution.py:19
  41.6 11.5 %collective-permute-start.19 = (bf16[32,2048]{1,0:T(8,128)(2,1)S(1)}, bf16[32,2048]{1,0:T(8,128)(2,1)S(1)}, u32[]{:S(2)}, u32[]{:S(2)}) collective-permute-start(bf16[32,2048]{1,0:T(8,128)(2,1)S(1)} %get-tuple-element.59), channel_id=1, source_target_pairs={{0,8},{4,12},{8,0},{12,4},{1,9},{5,13},{9,1},{13,5},{2,10},{6,14},... | collective-permute-start | bytes 393224 | tf_op jit(solution)/shard_map/ppermute | solution.py:19
  45.2 10.5 %collective-permute-start.20 = (bf16[32,2048]{1,0:T(8,128)(2,1)S(1)}, bf16[32,2048]{1,0:T(8,128)(2,1)S(1)}, u32[]{:S(2)}, u32[]{:S(2)}) collective-permute-start(bf16[32,2048]{1,0:T(8,128)(2,1)S(1)} %get-tuple-element.60), channel_id=1, source_target_pairs={{0,4},{4,0},{8,12},{12,8},{1,5},{5,1},{9,13},{13,9},{2,6},{6,2},{1... | collective-permute-start | bytes 393224 | tf_op jit(solution)/shard_map/ppermute | solution.py:19
  45.3 10.5 %collective-permute-start.21 = (bf16[32,2048]{1,0:T(8,128)(2,1)S(1)}, bf16[32,2048]{1,0:T(8,128)(2,1)S(1)}, u32[]{:S(2)}, u32[]{:S(2)}) collective-permute-start(bf16[32,2048]{1,0:T(8,128)(2,1)S(1)} %get-tuple-element.61), channel_id=1, source_target_pairs={{0,12},{4,8},{8,4},{12,0},{1,13},{5,9},{9,5},{13,1},{2,14},{6,10},... | collective-permute-start | bytes 393224 | tf_op jit(solution)/shard_map/ppermute | solution.py:19

commit v5 on v4

--- a/solution.py
+++ b/solution.py
@@ -229,25 +229,40 @@
         gated[:, cols] = gate.astype(BF16)
 
 
-def out_body(n, cuts, share, rows, first, second, weight, *refs):
-    pieces, own, rest = refs[: n * cuts], refs[n * cuts], refs[n * cuts + 1 :]
-    blocks = range(0, first.shape[0], rows)
+def sorted_rows(share, rows, first, second, pieces):
     lined = []
     for stage, picker in enumerate((first, second)):
         part = slice(stage * share, (stage + 1) * share)
-        sides = []
-        for cut in range(cuts):
-            every = jnp.concatenate([piece[part, :] for piece in pieces[cut * n : (cut + 1) * n]])
-            sides.append(
-                lax.dot_general(
-                    picker[...], every, (((0,), (0,)), ((), ())), preferred_element_type=F32
-                ).astype(BF16)
-            )
-        lined.append(jnp.concatenate(sides, axis=1))
-    lined = jnp.concatenate([part[at : at + rows] for at in blocks for part in lined])
+        every = jnp.concatenate([piece[part, :] for piece in pieces])
+        lined.append(
+            lax.dot_general(
+                picker[...], every, (((0,), (0,)), ((), ())), preferred_element_type=F32
+            ).astype(BF16)
+        )
+    blocks = range(0, first.shape[0], rows)
+    return jnp.concatenate([part[at : at + rows] for at in blocks for part in lined])
+
+
+def begin_body(share, rows, first, second, weight, *refs):
+    *pieces, total = refs
+    lined = sorted_rows(share, rows, first, second, pieces)
+    for cols in tiles(weight.shape[1]):
+        total[:, cols] = jnp.dot(
+            lined, weight[: lined.shape[1], cols], preferred_element_type=F32
+        )
+
+
+def finish_body(n, share, rows, first, second, weight, *refs):
+    pieces, refs = refs[:n], refs[n:]
+    begun = weight.shape[0] > pieces[0].shape[1]
+    before = refs[0] if begun else None
+    own, *rest = refs[1:] if begun else refs
+    lined = sorted_rows(share, rows, first, second, pieces)
     block = own.shape[0]
     for cols in tiles(weight.shape[1]):
-        product = jnp.dot(lined, weight[:, cols], preferred_element_type=F32)
+        product = jnp.dot(lined, weight[weight.shape[0] - lined.shape[1] :, cols], preferred_element_type=F32)
+        if before is not None:
+            product = product + before[:, cols]
         own[:, cols] = product[:block].astype(own.dtype)
         for k, ref in enumerate(rest, 1):
             ref[:, cols] = product[k * block : (k + 1) * block].astype(BF16)
@@ -336,16 +351,24 @@
         near.append([swap(gated, "narrow", k) if k else gated for k in evens])
         far.append([swap(piece, "narrow", 1) for piece in near[-1]])
     fresh = jnp.concatenate(fresh, axis=3)
-    pieces = [piece for cut in range(cuts) for piece in near[cut] + far[cut]]
     block = steps * rows
     shapes = [struct(steps * total, outs)]
     if direct:
         shapes = [struct(block, outs, dtype=F32)] + [struct(block, outs)] * (wide - 1)
+    cost = 2 * steps * total * (chans // cuts) * outs
+    begun = []
+    if cuts == 2:
+        begun = call(
+            functools.partial(begin_body, share, rows),
+            [struct(steps * total, outs, dtype=F32)],
+            [*pickers, out_weight, *near[0], *far[0]],
+            flops=cost,
+        )
     out, *parts = call(
-        functools.partial(out_body, n, cuts, share, rows),
+        functools.partial(finish_body, n, share, rows),
         shapes,
-        [*pickers, out_weight, *pieces],
-        flops=2 * steps * total * chans * outs,
+        [*pickers, out_weight, *near[-1], *far[-1], *begun],
+        flops=cost,
     )
     if direct:
         for k in [k for k in (2, 1, 3) if k < wide]:

time: 56.6 us -> 56.1 us (level)
  waiting for transfers between devices: 16.7 us -> 16 us
    ppermute x22, waiting for transfers between devices: 16.7 us -> 16 us  [swap(): return lax.ppermute(value, axis, [(i, i ^ hop) for i in range(count)])]
    pallas_call x10 -> x11, Pallas kernels: 7.6 us -> 7.92 us  [call(): pl.pallas_call(body, out_shape=outs, in_specs=[small] * scalars + [whole]...]
  transfers between devices with their start and end apart: 22 -> 22, of which waited for: 8 -> 6; matrix products, arithmetic and copies ran while one was open for 2% -> 2% of each run, Pallas kernels for 25% -> 27%
where the time goes in v5:
time: 56.1 us; the launch traced here: 56 us
  starting transfers between devices  20.4 us (36%)
  Pallas kernels  16.1 us (29%)
  waiting for transfers between devices  16 us (29%)
  local copies, waits for them, and re-layouts  1.85 us (3%)
  between operations  0.8 us (1%)
  other arithmetic  0.75 us (1%)
    ppermute x22, starting transfers between devices, swap(): return lax.ppermute(value, axis, [(i, i ^ hop) for i in range(count)])  20.4 us
    ppermute x22, waiting for transfers between devices, swap(): return lax.ppermute(value, axis, [(i, i ^ hop) for i in range(count)])  16 us
    pallas_call x1, Pallas kernels, load(): pl.pallas_call(functools.partial(load_body, n, share, rows, direct), out_...  8.23 us
    pallas_call x11, Pallas kernels, call(): pl.pallas_call(body, out_shape=outs, in_specs=[small] * scalars + [whole]...  7.92 us
    unnamed x15, local copies, waits for them, and re-layouts  1.85 us
  transfers between devices with their start and end apart: 22, of which 6 were waited for; matrix products, arithmetic and copies ran while one was open for 2% of the time, Pallas kernels for 27%

profile of v5, /device:TPU:0, one launch (start us, length us, event | category | flops | bytes accessed | tf_op | source)
XLA Modules:
  0.0 56.0 jit_solution(8409977863190847378)
XLA Ops:
  0.6 3.0 %collective-permute-start.1 = (bf16[16,3,2,2048]{3,2,1,0:T(2,128)(2,1)}, bf16[16,3,2,2048]{3,2,1,0:T(2,128)(2,1)S(1)}, u32[]{:S(2)}, u32[]{:S(2)}) collective-permute-start(bf16[16,3,2,2048]{3,2,1,0:T(2,128)(2,1)} %bitcast.9), channel_id=1, source_target_pairs={{0,2},{1,3},{2,0},{3,1},{4,6},{5,7},{6,4},{7,5},{8,10},{9,11},{10,... | collective-permute-start | bytes 1179656 | tf_op jit(solution)/shard_map/ppermute | solution.py:19
  3.6 2.6 %collective-permute-start.3 = (bf16[32,2048]{1,0:T(8,128)(2,1)}, bf16[32,2048]{1,0:T(8,128)(2,1)S(1)}, u32[]{:S(2)}, u32[]{:S(2)}) collective-permute-start(bf16[32,2048]{1,0:T(8,128)(2,1)} %bitcast.12), channel_id=1, source_target_pairs={{0,8},{4,12},{8,0},{12,4},{1,9},{5,13},{9,1},{13,5},{2,10},{6,14},... | collective-permute-start | bytes 393224 | tf_op jit(solution)/shard_map/ppermute | solution.py:19
  6.2 1.3 %collective-permute-start.4 = (bf16[32,2048]{1,0:T(8,128)(2,1)}, bf16[32,2048]{1,0:T(8,128)(2,1)S(1)}, u32[]{:S(2)}, u32[]{:S(2)}) collective-permute-start(bf16[32,2048]{1,0:T(8,128)(2,1)} %bitcast.13), channel_id=1, source_target_pairs={{0,12},{4,8},{8,4},{12,0},{1,13},{5,9},{9,5},{13,1},{2,14},{6,10},... | collective-permute-start | bytes 393224 | tf_op jit(solution)/shard_map/ppermute | solution.py:19
  7.6 0.2 collective-permute-start.5
  7.8 0.0 collective-permute-start
  7.8 0.0 copy-start.4
  7.8 0.7 %copy-done.4 = s32[2,64]{1,0:T(2,128)S(1)} copy-done((s32[2,64]{1,0:T(2,128)S(1)}, s32[2,64]{1,0:T(2,128)}, u32[]{:S(2)}) %copy-start.4) | copy-done | bytes 536
  8.5 8.2 %shard_map.86 = (bf16[64,64]{1,0:T(8,128)(2,1)S(1)}, bf16[64,64]{1,0:T(8,128)(2,1)S(1)}, bf16[2048,2048]{1,0:T(8,128)(2,1)S(1)}, bf16[2048,2048]{1,0:T(8,128)(2,1)S(1)}, bf16[2048,2048]{1,0:T(8,128)(2,1)S(1)}) custom-call(s32[2,64]{1,0:T(2,128)S(1)} %copy-done.4, bf16[3,2048,2048]{2,1,0:T(8,128)(2,1)} %bitcast.17), custom_call_target="tpu_custom_call" | custom-call | bytes 50331648 | tf_op jit(solution)/shard_map/pallas_call | solution.py:88
  16.7 0.0 collective-permute-done.3.refs_1_
  16.7 0.0 collective-permute-done.4.refs_2_
  16.7 0.0 collective-permute-done.5.refs_3_
  16.8 0.0 copy-done.2
  16.8 0.0 copy-done.3
  16.8 1.5 %shard_map.88 = (bf16[128,2048]{1,0:T(8,128)(2,1)S(1)}, f32[64,2048]{1,0:T(8,128)S(1)}, bf16[64,2176]{1,0:T(8,128)(2,1)S(1)}, f32[64,128]{1,0:T(8,128)S(1)}) custom-call(bf16[64,64]{1,0:T(8,128)(2,1)S(1)} %get-tuple-element.33.first, bf16[64,64]{1,0:T(8,128)(2,1)S(1)} %get-tuple-element.34.second, f32[1,2048]{1,0:T(1,128)S(1)} %bitcast.16, ...), custom_call_target="tpu_custom_call" | custom-call | flops 1073741824 | bytes 10297344 | tf_op jit(solution)/shard_map/pallas_call | solution.py:26
  18.3 0.6 %collective-permute-start.6 = (bf16[64,2176]{1,0:T(8,128)(2,1)S(1)}, bf16[64,2176]{1,0:T(8,128)(2,1)S(1)}, u32[]{:S(2)}, u32[]{:S(2)}) collective-permute-start(bf16[64,2176]{1,0:T(8,128)(2,1)S(1)} %get-tuple-element.39), channel_id=1, source_target_pairs={{0,1},{1,0},{2,3},{3,2},{4,5},{5,4},{6,7},{7,6},{8,9},{9,8},{10,11... | collective-permute-start | bytes 835592 | tf_op jit(solution)/shard_map/ppermute | solution.py:19
  18.9 1.3 %shard_map.90 = (f32[64,2048]{1,0:T(8,128)S(1)}, bf16[64,2048]{1,0:T(8,128)(2,1)S(1)}) custom-call(bf16[128,2048]{1,0:T(8,128)(2,1)S(1)} %get-tuple-element.43.scaled, bf16[2048,2048]{1,0:T(8,128)(2,1)S(1)} %get-tuple-element.44.refs_0_), custom_call_target="tpu_custom_call" | custom-call | flops 1073741824 | bytes 9699328 | tf_op jit(solution)/shard_map/pallas_call | solution.py:26
  20.2 0.1 collective-permute-start.7
  20.3 0.0 collective-permute-done.1.refs_2_
  20.3 0.5 collective-permute-start.2
  20.8 1.3 %shard_map.92 = (f32[64,2048]{1,0:T(8,128)S(1)}, bf16[64,2048]{1,0:T(8,128)(2,1)S(1)}) custom-call(bf16[128,2048]{1,0:T(8,128)(2,1)S(1)} %get-tuple-element.43.scaled, bf16[2048,2048]{1,0:T(8,128)(2,1)S(1)} %get-tuple-element.48.refs_0_), custom_call_target="tpu_custom_call" | custom-call | flops 1073741824 | bytes 9699328 | tf_op jit(solution)/shard_map/pallas_call | solution.py:26
  22.1 0.1 collective-permute-start.8
  22.2 0.0 collective-permute-done.6.got
  22.2 0.2 shard_map.89
  22.4 0.6 %collective-permute-start.9 = (bf16[32,2176]{1,0:T(8,128)(2,1)S(1)}, bf16[32,2176]{1,0:T(8,128)(2,1)S(1)}, u32[]{:S(2)}, u32[]{:S(2)}) collective-permute-start(bf16[32,2176]{1,0:T(8,128)(2,1)S(1)} %get-tuple-element.52), channel_id=1, source_target_pairs={{0,2},{1,3},{2,0},{3,1},{4,6},{5,7},{6,4},{7,5},{8,10},{9,11},{10,... | collective-permute-start | bytes 417800 | tf_op jit(solution)/shard_map/ppermute | solution.py:19
  23.0 0.0 collective-permute-done.7.got
  23.1 1.5 %collective-permute-start.10 = (bf16[32,2048]{1,0:T(8,128)(2,1)S(1)}, bf16[32,2048]{1,0:T(8,128)(2,1)S(1)}, u32[]{:S(2)}, u32[]{:S(2)}) collective-permute-start(bf16[32,2048]{1,0:T(8,128)(2,1)S(1)} %get-tuple-element.53), channel_id=1, source_target_pairs={{0,2},{1,3},{2,0},{3,1},{4,6},{5,7},{6,4},{7,5},{8,10},{9,11},{10,... | collective-permute-start | bytes 393224 | tf_op jit(solution)/shard_map/ppermute | solution.py:19
  24.6 0.0 collective-permute-done.8.got
  24.7 0.6 %collective-permute-start.15 = (bf16[32,1024]{1,0:T(8,128)(2,1)S(1)}, bf16[32,1024]{1,0:T(8,128)(2,1)S(1)}, u32[]{:S(2)}, u32[]{:S(2)}) collective-permute-start(bf16[32,1024]{1,0:T(8,128)(2,1)S(1)} %get-tuple-element.56), channel_id=1, source_target_pairs={{0,2},{1,3},{2,0},{3,1},{4,6},{5,7},{6,4},{7,5},{8,10},{9,11},{10,... | collective-permute-start | bytes 196616 | tf_op jit(solution)/shard_map/ppermute | solution.py:19
  25.3 0.0 collective-permute-done.refs_1_
  25.3 1.5 %collective-permute-start.11 = (bf16[32,1024]{1,0:T(8,128)(2,1)S(1)}, bf16[32,1024]{1,0:T(8,128)(2,1)S(1)}, u32[]{:S(2)}, u32[]{:S(2)}) collective-permute-start(bf16[32,1024]{1,0:T(8,128)(2,1)S(1)} %get-tuple-element.54), channel_id=1, source_target_pairs={{0,2},{1,3},{2,0},{3,1},{4,6},{5,7},{6,4},{7,5},{8,10},{9,11},{10,... | collective-permute-start | bytes 196616 | tf_op jit(solution)/shard_map/ppermute | solution.py:19
  26.8 0.0 collective-permute-done.2.refs_3_
  26.8 0.0 copy-done
  26.8 0.0 copy-done.1
  26.8 1.2 %shard_map.87 = (f32[3,16,2048]{2,1,0:T(8,128)S(1)}, f32[3,16,2048]{2,1,0:T(8,128)S(1)}) custom-call(s32[2,64]{1,0:T(2,128)S(1)} %copy-done.4, f32[3,3,2048]{2,1,0:T(4,128)S(1)} %copy-done, bf16[16,3,2,2048]{3,2,1,0:T(2,128)(2,1)S(1)} %bitcast.11, bf16[16,3,2,2048]{3,2,1,0:T(2,128)(2,1)S(1)} %collective-permute-done.refs_1_, ...), custom_call_target="tpu_custom_call" | custom-call | bytes 2433536 | tf_op jit(solution)/shard_map/pallas_call | solution.py:26
  28.0 5.2 %collective-permute-done.15.refs_5_ = bf16[32,1024]{1,0:T(8,128)(2,1)S(1)} collective-permute-done((bf16[32,1024]{1,0:T(8,128)(2,1)S(1)}, bf16[32,1024]{1,0:T(8,128)(2,1)S(1)}, u32[]{:S(2)}, u32[]{:S(2)}) %collective-permute-start.15) | collective-permute-done | bytes 65568 | tf_op jit(solution)/shard_map/ppermute | solution.py:19
  33.2 0.0 collective-permute-done.10.refs_4_
  33.2 0.0 collective-permute-done.9.refs_3_
  33.2 0.3 shard_map.95
  33.5 0.6 %collective-permute-start.16 = (bf16[32,1024]{1,0:T(8,128)(2,1)S(1)}, bf16[32,1024]{1,0:T(8,128)(2,1)S(1)}, u32[]{:S(2)}, u32[]{:S(2)}) collective-permute-start(bf16[32,1024]{1,0:T(8,128)(2,1)S(1)} %get-tuple-element.57.refs_0_), channel_id=1, source_target_pairs={{0,2},{1,3},{2,0},{3,1},{4,6},{5,7},{6,4},{7,5},{8,10},{9,11},{10,... | collective-permute-start | bytes 196616 | tf_op jit(solution)/shard_map/ppermute | solution.py:19
  34.1 0.0 collective-permute-done.11.refs_5_
  34.1 0.3 shard_map.94
  34.4 1.5 %collective-permute-start.12 = (bf16[32,1024]{1,0:T(8,128)(2,1)S(1)}, bf16[32,1024]{1,0:T(8,128)(2,1)S(1)}, u32[]{:S(2)}, u32[]{:S(2)}) collective-permute-start(bf16[32,1024]{1,0:T(8,128)(2,1)S(1)} %get-tuple-element.55.refs_0_), channel_id=1, source_target_pairs={{0,2},{1,3},{2,0},{3,1},{4,6},{5,7},{6,4},{7,5},{8,10},{9,11},{10,... | collective-permute-start | bytes 196616 | tf_op jit(solution)/shard_map/ppermute | solution.py:19
  35.9 0.0 collective-permute-start.17
  35.9 2.2 %collective-permute-done.16.refs_1_ = bf16[32,1024]{1,0:T(8,128)(2,1)S(1)} collective-permute-done((bf16[32,1024]{1,0:T(8,128)(2,1)S(1)}, bf16[32,1024]{1,0:T(8,128)(2,1)S(1)}, u32[]{:S(2)}, u32[]{:S(2)}) %collective-permute-start.16) | collective-permute-done | bytes 65568 | tf_op jit(solution)/shard_map/ppermute | solution.py:19
  38.1 0.0 collective-permute-start.18
  38.1 0.5 collective-permute-start.13
  38.6 0.2 collective-permute-done.12.refs_1_
  38.8 0.0 collective-permute-start.14
  38.8 0.0 collective-permute-done.17.refs_2_
  38.8 0.5 collective-permute-done.18.refs_3_
  39.4 0.0 slice-done
  39.4 0.0 slice-done.1
  39.4 0.9 %shard_map.96.refs_4_ = f32[128,2048]{1,0:T(8,128)S(1)} custom-call(bf16[64,64]{1,0:T(8,128)(2,1)S(1)} %get-tuple-element.33.first, bf16[64,64]{1,0:T(8,128)(2,1)S(1)} %get-tuple-element.34.second, bf16[2048,2048]{1,0:T(8,128)(2,1)S(1)} %bitcast.8, bf16[32,1024]{1,0:T(8,128)(2,1)S(1)} %get-tuple-element.57.refs_0_, ...), custom_call_target="tpu_custom_call" | custom-call | flops 536870912 | bytes 9715712 | tf_op jit(solution)/shard_map/pallas_call | solution.py:26
  40.3 0.0 collective-permute-done.13.refs_2_
  40.3 0.0 collective-permute-done.14.refs_3_
  40.3 0.9 %shard_map.97 = (f32[32,2048]{1,0:T(8,128)S(1)}, bf16[32,2048]{1,0:T(8,128)(2,1)S(1)}, bf16[32,2048]{1,0:T(8,128)(2,1)S(1)}, bf16[32,2048]{1,0:T(8,128)(2,1)S(1)}) custom-call(bf16[64,64]{1,0:T(8,128)(2,1)S(1)} %get-tuple-element.33.first, bf16[64,64]{1,0:T(8,128)(2,1)S(1)} %get-tuple-element.34.second, bf16[2048,2048]{1,0:T(8,128)(2,1)S(1)} %bitcast.8, ...), custom_call_target="tpu_custom_call" | custom-call | flops 536870912 | bytes 10371072 | tf_op jit(solution)/shard_map/pallas_call | solution.py:26
  41.2 3.5 %collective-permute-start.19 = (bf16[32,2048]{1,0:T(8,128)(2,1)S(1)}, bf16[32,2048]{1,0:T(8,128)(2,1)S(1)}, u32[]{:S(2)}, u32[]{:S(2)}) collective-permute-start(bf16[32,2048]{1,0:T(8,128)(2,1)S(1)} %get-tuple-element.59), channel_id=1, source_target_pairs={{0,8},{4,12},{8,0},{12,4},{1,9},{5,13},{9,1},{13,5},{2,10},{6,14},... | collective-permute-start | bytes 393224 | tf_op jit(solution)/shard_map/ppermute | solution.py:19
  44.7 0.0 collective-permute-start.20
  44.8 1.5 %collective-permute-start.21 = (bf16[32,2048]{1,0:T(8,128)(2,1)S(1)}, bf16[32,2048]{1,0:T(8,128)(2,1)S(1)}, u32[]{:S(2)}, u32[]{:S(2)}) collective-permute-start(bf16[32,2048]{1,0:T(8,128)(2,1)S(1)} %get-tuple-element.61), channel_id=1, source_target_pairs={{0,12},{4,8},{8,4},{12,0},{1,13},{5,9},{9,5},{13,1},{2,14},{6,10},... | collective-permute-start | bytes 393224 | tf_op jit(solution)/shard_map/ppermute | solution.py:19
  46.3 1.2 %copy.9 = bf16[16,2,3,2048]{3,1,2,0:T(2,128)(2,1)} copy(bf16[16,2,3,2048]{3,0,1,2:T(8,128)(2,1)S(1)} %maximum_bitcast_fusion) | data formatting | bytes 786432
  47.5 5.1 %collective-permute-done.19 = bf16[32,2048]{1,0:T(8,128)(2,1)S(1)} collective-permute-done((bf16[32,2048]{1,0:T(8,128)(2,1)S(1)}, bf16[32,2048]{1,0:T(8,128)(2,1)S(1)}, u32[]{:S(2)}, u32[]{:S(2)}) %collective-permute-start.19) | collective-permute-done | bytes 131104 | tf_op jit(solution)/shard_map/ppermute | solution.py:19
  52.6 2.7 %collective-permute-done.20 = bf16[32,2048]{1,0:T(8,128)(2,1)S(1)} collective-permute-done((bf16[32,2048]{1,0:T(8,128)(2,1)S(1)}, bf16[32,2048]{1,0:T(8,128)(2,1)S(1)}, u32[]{:S(2)}, u32[]{:S(2)}) %collective-permute-start.20) | collective-permute-done | bytes 131104 | tf_op jit(solution)/shard_map/ppermute | solution.py:19
  55.2 0.0 collective-permute-done.21
  55.2 0.7 %add_convert_fusion = bf16[32,2048]{1,0:T(8,128)(2,1)} fusion(bf16[32,2048]{1,0:T(8,128)(2,1)S(1)} %collective-permute-done.21, bf16[32,2048]{1,0:T(8,128)(2,1)S(1)} %collective-permute-done.20, f32[32,2048]{1,0:T(8,128)S(1)} %get-tuple-element.58, bf16[32,2048]{1,0:T(8,128)(2,1)S(1)} %collective-permute-done.19), kind=kLoop, calls=%fused_computation.1 | loop fusion | flops 458752 | bytes 786432 | tf_op jit(solution)/shard_map/convert_element_type | solution.py:376
  (10 shorter events, 0.1 us)
Async XLA Ops:
  0.6 19.7 %collective-permute-start.1 = (bf16[16,3,2,2048]{3,2,1,0:T(2,128)(2,1)}, bf16[16,3,2,2048]{3,2,1,0:T(2,128)(2,1)S(1)}, u32[]{:S(2)}, u32[]{:S(2)}) collective-permute-start(bf16[16,3,2,2048]{3,2,1,0:T(2,128)(2,1)} %bitcast.9), channel_id=1, source_target_pairs={{0,2},{1,3},{2,0},{3,1},{4,6},{5,7},{6,4},{7,5},{8,10},{9,11},{10,... | collective-permute-start | bytes 1179656 | tf_op jit(solution)/shard_map/ppermute | solution.py:19
  3.6 13.1 %collective-permute-start.3 = (bf16[32,2048]{1,0:T(8,128)(2,1)}, bf16[32,2048]{1,0:T(8,128)(2,1)S(1)}, u32[]{:S(2)}, u32[]{:S(2)}) collective-permute-start(bf16[32,2048]{1,0:T(8,128)(2,1)} %bitcast.12), channel_id=1, source_target_pairs={{0,8},{4,12},{8,0},{12,4},{1,9},{5,13},{9,1},{13,5},{2,10},{6,14},... | collective-permute-start | bytes 393224 | tf_op jit(solution)/shard_map/ppermute | solution.py:19
  6.2 10.5 %collective-permute-start.4 = (bf16[32,2048]{1,0:T(8,128)(2,1)}, bf16[32,2048]{1,0:T(8,128)(2,1)S(1)}, u32[]{:S(2)}, u32[]{:S(2)}) collective-permute-start(bf16[32,2048]{1,0:T(8,128)(2,1)} %bitcast.13), channel_id=1, source_target_pairs={{0,12},{4,8},{8,4},{12,0},{1,13},{5,9},{9,5},{13,1},{2,14},{6,10},... | collective-permute-start | bytes 393224 | tf_op jit(solution)/shard_map/ppermute | solution.py:19
  7.6 9.2 %collective-permute-start.5 = (bf16[32,2048]{1,0:T(8,128)(2,1)}, bf16[32,2048]{1,0:T(8,128)(2,1)S(1)}, u32[]{:S(2)}, u32[]{:S(2)}) collective-permute-start(bf16[32,2048]{1,0:T(8,128)(2,1)} %bitcast.14), channel_id=1, source_target_pairs={{0,4},{4,0},{8,12},{12,8},{1,5},{5,1},{9,13},{13,9},{2,6},{6,2},{1... | collective-permute-start | bytes 393224 | tf_op jit(solution)/shard_map/ppermute | solution.py:19
  7.8 17.5 %collective-permute-start = (bf16[16,3,2,2048]{3,2,1,0:T(2,128)(2,1)}, bf16[16,3,2,2048]{3,2,1,0:T(2,128)(2,1)S(1)}, u32[]{:S(2)}, u32[]{:S(2)}) collective-permute-start(bf16[16,3,2,2048]{3,2,1,0:T(2,128)(2,1)} %bitcast.10), channel_id=1, source_target_pairs={{0,1},{1,0},{2,3},{3,2},{4,5},{5,4},{6,7},{7,6},{8,9},{9,8},{10,11... | collective-permute-start | bytes 1179656 | tf_op jit(solution)/shard_map/ppermute | solution.py:19
  7.8 0.7 %copy-start.4 = (s32[2,64]{1,0:T(2,128)S(1)}, s32[2,64]{1,0:T(2,128)}, u32[]{:S(2)}) copy-start(s32[2,64]{1,0:T(2,128)} %assign.3) | copy-start | bytes 1540
  8.5 8.3 %copy-start.2 = (bf16[2,16,2048]{2,1,0:T(8,128)(2,1)S(1)}, bf16[2,16,2048]{2,1,0:T(8,128)(2,1)}, u32[]{:S(2)}) copy-start(bf16[2,16,2048]{2,1,0:T(8,128)(2,1)} %param.7) | copy-start | bytes 393220
  8.5 8.3 %copy-start.3 = (f32[2048]{0:T(1024)S(1)}, f32[2048]{0:T(1024)}, u32[]{:S(2)}) copy-start(f32[2048]{0:T(1024)} %param.10) | copy-start | bytes 24580
  18.3 3.9 %collective-permute-start.6 = (bf16[64,2176]{1,0:T(8,128)(2,1)S(1)}, bf16[64,2176]{1,0:T(8,128)(2,1)S(1)}, u32[]{:S(2)}, u32[]{:S(2)}) collective-permute-start(bf16[64,2176]{1,0:T(8,128)(2,1)S(1)} %get-tuple-element.39), channel_id=1, source_target_pairs={{0,1},{1,0},{2,3},{3,2},{4,5},{5,4},{6,7},{7,6},{8,9},{9,8},{10,11... | collective-permute-start | bytes 835592 | tf_op jit(solution)/shard_map/ppermute | solution.py:19
  18.9 7.9 %copy-start = (f32[3,3,2048]{2,1,0:T(4,128)S(1)}, f32[3,3,2048]{2,1,0:T(4,128)}, u32[]{:S(2)}) copy-start(f32[3,3,2048]{2,1,0:T(4,128)} %conv.5) | copy-start | bytes 221188
  18.9 7.9 %copy-start.1 = (bf16[16,2,3,2048]{3,1,2,0:T(2,128)(2,1)S(1)}, bf16[16,2,3,2048]{3,1,2,0:T(2,128)(2,1)}, u32[]{:S(2)}) copy-start(bf16[16,2,3,2048]{3,1,2,0:T(2,128)(2,1)} %param.9) | copy-start | bytes 1179652
  20.2 2.9 %collective-permute-start.7 = (bf16[64,2048]{1,0:T(8,128)(2,1)S(1)}, bf16[64,2048]{1,0:T(8,128)(2,1)S(1)}, u32[]{:S(2)}, u32[]{:S(2)}) collective-permute-start(bf16[64,2048]{1,0:T(8,128)(2,1)S(1)} %get-tuple-element.46), channel_id=1, source_target_pairs={{0,1},{1,0},{2,3},{3,2},{4,5},{5,4},{6,7},{7,6},{8,9},{9,8},{10,11... | collective-permute-start | bytes 786440 | tf_op jit(solution)/shard_map/ppermute | solution.py:19
  20.3 6.5 %collective-permute-start.2 = (bf16[16,3,2,2048]{3,2,1,0:T(2,128)(2,1)S(1)}, bf16[16,3,2,2048]{3,2,1,0:T(2,128)(2,1)S(1)}, u32[]{:S(2)}, u32[]{:S(2)}) collective-permute-start(bf16[16,3,2,2048]{3,2,1,0:T(2,128)(2,1)S(1)} %collective-permute-done.1.refs_2_), channel_id=1, source_target_pairs={{0,1},{1,0},{2,3},{3,2},{4,5},{5,4},{6,7},{7,6},{8,9},{9,8},{10,11... | collective-permute-start | bytes 1179656 | tf_op jit(solution)/shard_map/ppermute | solution.py:19
  20.8 18.6 %slice-start = ((s8[8388608]{0:T(1024)(128)(4,1)}), s8[4194304]{0:T(1024)(128)(4,1)S(1)}, s32[]{:S(2)}) async-start(s8[8388608]{0:T(1024)(128)(4,1)} %bitcast.7), calls=%async_computation | async-start | bytes 8388608
  20.8 18.6 %slice-start.1 = ((s8[8388608]{0:T(1024)(128)(4,1)}), s8[4194304]{0:T(1024)(128)(4,1)S(1)}, s32[]{:S(2)}) async-start(s8[8388608]{0:T(1024)(128)(4,1)} %bitcast.7), calls=%async_computation.1 | async-start | bytes 8388608
  22.1 2.5 %collective-permute-start.8 = (bf16[64,2048]{1,0:T(8,128)(2,1)S(1)}, bf16[64,2048]{1,0:T(8,128)(2,1)S(1)}, u32[]{:S(2)}, u32[]{:S(2)}) collective-permute-start(bf16[64,2048]{1,0:T(8,128)(2,1)S(1)} %get-tuple-element.50), channel_id=1, source_target_pairs={{0,1},{1,0},{2,3},{3,2},{4,5},{5,4},{6,7},{7,6},{8,9},{9,8},{10,11... | collective-permute-start | bytes 786440 | tf_op jit(solution)/shard_map/ppermute | solution.py:19
  22.4 10.8 %collective-permute-start.9 = (bf16[32,2176]{1,0:T(8,128)(2,1)S(1)}, bf16[32,2176]{1,0:T(8,128)(2,1)S(1)}, u32[]{:S(2)}, u32[]{:S(2)}) collective-permute-start(bf16[32,2176]{1,0:T(8,128)(2,1)S(1)} %get-tuple-element.52), channel_id=1, source_target_pairs={{0,2},{1,3},{2,0},{3,1},{4,6},{5,7},{6,4},{7,5},{8,10},{9,11},{10,... | collective-permute-start | bytes 417800 | tf_op jit(solution)/shard_map/ppermute | solution.py:19
  23.1 10.1 %collective-permute-start.10 = (bf16[32,2048]{1,0:T(8,128)(2,1)S(1)}, bf16[32,2048]{1,0:T(8,128)(2,1)S(1)}, u32[]{:S(2)}, u32[]{:S(2)}) collective-permute-start(bf16[32,2048]{1,0:T(8,128)(2,1)S(1)} %get-tuple-element.53), channel_id=1, source_target_pairs={{0,2},{1,3},{2,0},{3,1},{4,6},{5,7},{6,4},{7,5},{8,10},{9,11},{10,... | collective-permute-start | bytes 393224 | tf_op jit(solution)/shard_map/ppermute | solution.py:19
  24.7 8.5 %collective-permute-start.15 = (bf16[32,1024]{1,0:T(8,128)(2,1)S(1)}, bf16[32,1024]{1,0:T(8,128)(2,1)S(1)}, u32[]{:S(2)}, u32[]{:S(2)}) collective-permute-start(bf16[32,1024]{1,0:T(8,128)(2,1)S(1)} %get-tuple-element.56), channel_id=1, source_target_pairs={{0,2},{1,3},{2,0},{3,1},{4,6},{5,7},{6,4},{7,5},{8,10},{9,11},{10,... | collective-permute-start | bytes 196616 | tf_op jit(solution)/shard_map/ppermute | solution.py:19
  25.3 8.8 %collective-permute-start.11 = (bf16[32,1024]{1,0:T(8,128)(2,1)S(1)}, bf16[32,1024]{1,0:T(8,128)(2,1)S(1)}, u32[]{:S(2)}, u32[]{:S(2)}) collective-permute-start(bf16[32,1024]{1,0:T(8,128)(2,1)S(1)} %get-tuple-element.54), channel_id=1, source_target_pairs={{0,2},{1,3},{2,0},{3,1},{4,6},{5,7},{6,4},{7,5},{8,10},{9,11},{10,... | collective-permute-start | bytes 196616 | tf_op jit(solution)/shard_map/ppermute | solution.py:19
  33.5 4.7 %collective-permute-start.16 = (bf16[32,1024]{1,0:T(8,128)(2,1)S(1)}, bf16[32,1024]{1,0:T(8,128)(2,1)S(1)}, u32[]{:S(2)}, u32[]{:S(2)}) collective-permute-start(bf16[32,1024]{1,0:T(8,128)(2,1)S(1)} %get-tuple-element.57.refs_0_), channel_id=1, source_target_pairs={{0,2},{1,3},{2,0},{3,1},{4,6},{5,7},{6,4},{7,5},{8,10},{9,11},{10,... | collective-permute-start | bytes 196616 | tf_op jit(solution)/shard_map/ppermute | solution.py:19
  34.4 4.4 %collective-permute-start.12 = (bf16[32,1024]{1,0:T(8,128)(2,1)S(1)}, bf16[32,1024]{1,0:T(8,128)(2,1)S(1)}, u32[]{:S(2)}, u32[]{:S(2)}) collective-permute-start(bf16[32,1024]{1,0:T(8,128)(2,1)S(1)} %get-tuple-element.55.refs_0_), channel_id=1, source_target_pairs={{0,2},{1,3},{2,0},{3,1},{4,6},{5,7},{6,4},{7,5},{8,10},{9,11},{10,... | collective-permute-start | bytes 196616 | tf_op jit(solution)/shard_map/ppermute | solution.py:19
  35.9 2.9 %collective-permute-start.17 = (bf16[32,1024]{1,0:T(8,128)(2,1)S(1)}, bf16[32,1024]{1,0:T(8,128)(2,1)S(1)}, u32[]{:S(2)}, u32[]{:S(2)}) collective-permute-start(bf16[32,1024]{1,0:T(8,128)(2,1)S(1)} %get-tuple-element.57.refs_0_), channel_id=1, source_target_pairs={{0,1},{1,0},{2,3},{3,2},{4,5},{5,4},{6,7},{7,6},{8,9},{9,8},{10,11... | collective-permute-start | bytes 196616 | tf_op jit(solution)/shard_map/ppermute | solution.py:19
  38.1 1.3 %collective-permute-start.18 = (bf16[32,1024]{1,0:T(8,128)(2,1)S(1)}, bf16[32,1024]{1,0:T(8,128)(2,1)S(1)}, u32[]{:S(2)}, u32[]{:S(2)}) collective-permute-start(bf16[32,1024]{1,0:T(8,128)(2,1)S(1)} %collective-permute-done.16.refs_1_), channel_id=1, source_target_pairs={{0,1},{1,0},{2,3},{3,2},{4,5},{5,4},{6,7},{7,6},{8,9},{9,8},{10,11... | collective-permute-start | bytes 196616 | tf_op jit(solution)/shard_map/ppermute | solution.py:19
  38.1 2.2 %collective-permute-start.13 = (bf16[32,1024]{1,0:T(8,128)(2,1)S(1)}, bf16[32,1024]{1,0:T(8,128)(2,1)S(1)}, u32[]{:S(2)}, u32[]{:S(2)}) collective-permute-start(bf16[32,1024]{1,0:T(8,128)(2,1)S(1)} %get-tuple-element.55.refs_0_), channel_id=1, source_target_pairs={{0,1},{1,0},{2,3},{3,2},{4,5},{5,4},{6,7},{7,6},{8,9},{9,8},{10,11... | collective-permute-start | bytes 196616 | tf_op jit(solution)/shard_map/ppermute | solution.py:19
  38.8 1.5 %collective-permute-start.14 = (bf16[32,1024]{1,0:T(8,128)(2,1)S(1)}, bf16[32,1024]{1,0:T(8,128)(2,1)S(1)}, u32[]{:S(2)}, u32[]{:S(2)}) collective-permute-start(bf16[32,1024]{1,0:T(8,128)(2,1)S(1)} %collective-permute-done.12.refs_1_), channel_id=1, source_target_pairs={{0,1},{1,0},{2,3},{3,2},{4,5},{5,4},{6,7},{7,6},{8,9},{9,8},{10,11... | collective-permute-start | bytes 196616 | tf_op jit(solution)/shard_map/ppermute | solution.py:19
  41.2 11.3 %collective-permute-start.19 = (bf16[32,2048]{1,0:T(8,128)(2,1)S(1)}, bf16[32,2048]{1,0:T(8,128)(2,1)S(1)}, u32[]{:S(2)}, u32[]{:S(2)}) collective-permute-start(bf16[32,2048]{1,0:T(8,128)(2,1)S(1)} %get-tuple-element.59), channel_id=1, source_target_pairs={{0,8},{4,12},{8,0},{12,4},{1,9},{5,13},{9,1},{13,5},{2,10},{6,14},... | collective-permute-start | bytes 393224 | tf_op jit(solution)/shard_map/ppermute | solution.py:19
  44.7 10.5 %collective-permute-start.20 = (bf16[32,2048]{1,0:T(8,128)(2,1)S(1)}, bf16[32,2048]{1,0:T(8,128)(2,1)S(1)}, u32[]{:S(2)}, u32[]{:S(2)}) collective-permute-start(bf16[32,2048]{1,0:T(8,128)(2,1)S(1)} %get-tuple-element.60), channel_id=1, source_target_pairs={{0,4},{4,0},{8,12},{12,8},{1,5},{5,1},{9,13},{13,9},{2,6},{6,2},{1... | collective-permute-start | bytes 393224 | tf_op jit(solution)/shard_map/ppermute | solution.py:19
  44.8 10.5 %collective-permute-start.21 = (bf16[32,2048]{1,0:T(8,128)(2,1)S(1)}, bf16[32,2048]{1,0:T(8,128)(2,1)S(1)}, u32[]{:S(2)}, u32[]{:S(2)}) collective-permute-start(bf16[32,2048]{1,0:T(8,128)(2,1)S(1)} %get-tuple-element.61), channel_id=1, source_target_pairs={{0,12},{4,8},{8,4},{12,0},{1,13},{5,9},{9,5},{13,1},{2,14},{6,10},... | collective-permute-start | bytes 393224 | tf_op jit(solution)/shard_map/ppermute | solution.py:19
